TPU v7x, 32 devices: a whole 2x2x4 slice. The times are simulated.
32 devices in a mesh: dp: 4 (over x, core), blk: 2 (over y), head: 4 (over z).
Axes of the slice: x: 2, y: 2, z: 4, core: 2. Of those that a mesh axis runs over, the one named last changes fastest.
Arguments:
- dec_in: bfloat16 [1024, 768], P(('dp', 'blk')), may hold values from -6 to 6
- enc_out: bfloat16 [61440, 768], P(('dp', 'blk', 'head')), may hold values from -6 to 6
- passage_len: int32 [160], P(('dp', 'blk')), may hold values from 288 to 384
- dec_len: int32 [8], P(('dp', 'blk')), may hold values from 64 to 128
- passage_owner: int32 [160], P(('dp', 'blk')), may hold values from 0 to 1, as said below
- gain_self: bfloat16 [768], replicated, may hold values from 0.099609375 to 1.8984375
- gain_cross: bfloat16 [768], replicated, may hold values from 0.099609375 to 1.8984375
- gain_ffn: bfloat16 [768], replicated, may hold values from 0.099609375 to 1.8984375
- w_query: bfloat16 [768, 768], P('head'), may hold values from -0.109375 to 0.109375
- w_key: bfloat16 [768, 768], P('head'), may hold values from -0.109375 to 0.109375
- w_value: bfloat16 [768, 768], P('head'), may hold values from -0.21875 to 0.21875
- w_out: bfloat16 [768, 768], P('head'), may hold values from -0.3125 to 0.3125
- c_query: bfloat16 [768, 768], P('head'), may hold values from -0.109375 to 0.109375
- c_key: bfloat16 [768, 768], P('head'), may hold values from -0.109375 to 0.109375
- c_value: bfloat16 [768, 768], P('head'), may hold values from -0.21875 to 0.21875
- c_out: bfloat16 [768, 768], P('head'), may hold values from -2.5 to 2.5
- w_in: bfloat16 [768, 3072], P(None, 'head'), may hold values from -0.21875 to 0.21875
- w_back: bfloat16 [3072, 768], P('head'), may hold values from -0.15625 to 0.15625
- cotangent: bfloat16 [1024, 768], P(('dp', 'blk')), may hold values from -6 to 6
Outputs:
- layer_out: bfloat16 [1024, 768], P(('dp', 'blk'))
- grad_in: float32 [1024, 768], P(('dp', 'blk'))
- grad_enc: float32 [61440, 768], P(('dp', 'blk', 'head'))
- grad_gain_self: float32 [768], replicated
- grad_gain_cross: float32 [768], replicated
- grad_gain_ffn: float32 [768], replicated
- grad_w_query: float32 [768, 768], P('head')
- grad_w_key: float32 [768, 768], P('head')
- grad_w_value: float32 [768, 768], P('head')
- grad_w_out: float32 [768, 768], P('head')
- grad_c_query: float32 [768, 768], P('head')
- grad_c_key: float32 [768, 768], P('head')
- grad_c_value: float32 [768, 768], P('head')
- grad_c_out: float32 [768, 768], P('head')
- grad_w_in: float32 [768, 3072], P(None, 'head')
- grad_w_back: float32 [3072, 768], P('head')
Inputs may be any that keep to these rules, and one draw needn't show every extreme that they name: `passage_owner`: A question number of its dp group (question g of a group has its decoder tokens on the device of index g // 1 along blk). Each question owns exactly 20 passages of its group, at least one and at most 10 among the 20 passages of any one device of blk; on every device some question owns exactly 10.
All inputs are finite; a program needn't handle non-finite values.
Results may differ from a plain program's by a relative error of at most 0.035.
The roundings to bfloat16 on the way count: a program that leaves them out, or rounds other values in their place, can miss the bound.
Values may be sent and summed in bfloat16 or wider, within the bound.
No kernel may reach another device: no remote copies, remote signals or barrier semaphores. Data moves between devices by JAX's collectives and lax.ppermute only.
A program may use at most 192 MiB of HBM per device.

v0:
```python
import jax
import jax.numpy as jnp
from jax import lax
from jax.sharding import PartitionSpec as P

DHEAD = 64
LQ = 128
LP = 384
NPASS = 20
QDEV = 1
PDEV = 20


norm_epsilon = 1e-06
masked_score = -1e30


def passed_along(array, axis, by):
    size = lax.axis_size(axis)
    return lax.ppermute(array, axis, [(i, (i + by) % size) for i in range(size)])


def normalize(values, gain):
    return (
        values * lax.rsqrt(jnp.mean(values * values, axis=-1, keepdims=True) + norm_epsilon) * gain
    )


def matmul(left, right):
    return jnp.dot(left, right, preferred_element_type=jnp.float32)


def times_transposed(left, right):
    return lax.dot_general(
        left, right, (((1,), (1,)), ((), ())), preferred_element_type=jnp.float32
    )


def transposed_times(left, right):
    return lax.dot_general(
        left, right, (((0,), (0,)), ((), ())), preferred_element_type=jnp.float32
    )


def across_heads(partial_value):
    return lax.psum(partial_value, "head")


def score_block(queries, key_rows):
    return jnp.einsum("qhd,khd->hqk", queries, key_rows, preferred_element_type=jnp.float32)


def online_update(running, totals, accumulated, queries, key_rows, value_rows, allowed):
    scores = jnp.where(allowed[None], score_block(queries, key_rows), masked_score)
    newest = jnp.maximum(running, jnp.max(scores, axis=-1))
    factor = jnp.exp(running - newest)
    soft_weights = jnp.where(allowed[None], jnp.exp(scores - newest[:, :, None]), 0.0)
    totals = totals * factor + jnp.sum(soft_weights, axis=-1)
    update = jnp.einsum(
        "hqk,khd->qhd",
        soft_weights.astype(jnp.bfloat16),
        value_rows,
        preferred_element_type=jnp.float32,
    )
    return (newest, totals, accumulated * factor.T[:, :, None] + update)


def self_forward(queries, key_rows, value_rows, allowed):
    scores = jnp.where(allowed[None], score_block(queries, key_rows), masked_score)
    highest = jnp.max(scores, axis=-1, keepdims=True)
    raised = jnp.exp(scores - highest)
    totals = jnp.sum(raised, axis=-1, keepdims=True)
    output = jnp.einsum(
        "hqk,khd->qhd",
        (raised / totals).astype(jnp.bfloat16),
        value_rows,
        preferred_element_type=jnp.float32,
    )
    return (output, (highest + jnp.log(totals))[:, :, 0])


def block_grads(queries, key_rows, value_rows, allowed, grad_out, logsum, deltas):
    scores = score_block(queries, key_rows)
    soft_weights = jnp.where(allowed[None], jnp.exp(scores - logsum[:, :, None]), 0.0)
    grad_values = jnp.einsum(
        "hqk,qhd->khd",
        soft_weights.astype(jnp.bfloat16),
        grad_out,
        preferred_element_type=jnp.float32,
    )
    grad_soft = jnp.einsum("qhd,khd->hqk", grad_out, value_rows, preferred_element_type=jnp.float32)
    grad_scores = (soft_weights * (grad_soft - deltas[:, :, None])).astype(jnp.bfloat16)
    grad_queries = jnp.einsum(
        "hqk,khd->qhd", grad_scores, key_rows, preferred_element_type=jnp.float32
    )
    grad_keys = jnp.einsum("hqk,qhd->khd", grad_scores, queries, preferred_element_type=jnp.float32)
    return (grad_queries, grad_keys, grad_values)


def body(
    dec_in,
    enc_out,
    passage_len,
    dec_len,
    passage_owner,
    gain_self,
    gain_cross,
    gain_ffn,
    w_query,
    w_key,
    w_value,
    w_out,
    c_query,
    c_key,
    c_value,
    c_out,
    w_in,
    w_back,
    cotangent,
):
    blk_count = lax.axis_size("blk")
    head_count = lax.axis_size("head")
    most = -(-NPASS // blk_count)
    width = w_query.shape[0]
    heads = width // DHEAD
    row_count = dec_in.shape[0]
    enc_slots = enc_out.shape[0] * head_count

    def split_heads(values):
        return values.reshape(QDEV, LQ, heads, DHEAD)

    inputs = dec_in.astype(jnp.float32)
    gain_one = gain_self.astype(jnp.float32)
    gain_two = gain_cross.astype(jnp.float32)
    gain_three = gain_ffn.astype(jnp.float32)
    normed_one = normalize(inputs, gain_one).astype(jnp.bfloat16)
    self_q = times_transposed(normed_one, w_query).astype(jnp.bfloat16)
    self_k = times_transposed(normed_one, w_key).astype(jnp.bfloat16)
    self_v = times_transposed(normed_one, w_value).astype(jnp.bfloat16)
    positions = jnp.arange(LQ, dtype=jnp.int32)
    self_allowed = (positions[None, None, :] <= positions[None, :, None]) & (
        positions[None, None, :] < dec_len[:, None, None]
    )
    self_out, self_logsum = jax.vmap(self_forward)(
        split_heads(self_q), split_heads(self_k), split_heads(self_v), self_allowed
    )
    self_flat = self_out.reshape(row_count, width).astype(jnp.bfloat16)
    first = inputs + across_heads(matmul(self_flat, w_out))
    normed_two = normalize(first, gain_two).astype(jnp.bfloat16)
    cross_q = split_heads(times_transposed(normed_two, c_query).astype(jnp.bfloat16))
    piece = lax.all_gather(enc_out, "head", axis=0, tiled=True)
    projected = jnp.concatenate(
        [times_transposed(piece, c_key), times_transposed(piece, c_value)], axis=1
    )
    enc_keys = projected[:, :width].astype(jnp.bfloat16)
    enc_values = projected[:, width:].astype(jnp.bfloat16)
    order = jnp.argsort(passage_owner, stable=True)
    inverse = jnp.argsort(order)
    spare = jnp.zeros((most, LP, width), jnp.bfloat16)
    sorted_keys = jnp.concatenate(
        [jnp.take(enc_keys.reshape(PDEV, LP, width), order, axis=0), spare], axis=0
    )
    sorted_values = jnp.concatenate(
        [jnp.take(enc_values.reshape(PDEV, LP, width), order, axis=0), spare], axis=0
    )
    sorted_lengths = jnp.concatenate(
        [jnp.take(passage_len, order, axis=0), jnp.zeros((most,), jnp.int32)], axis=0
    )
    slot_ids = jnp.arange(most, dtype=jnp.int32)
    token_ids = jnp.arange(LP, dtype=jnp.int32)
    blk_place = lax.axis_index("blk")

    def local_block(question):
        offset = jnp.sum(passage_owner < question)
        amount = jnp.sum(passage_owner == question)
        key_rows = lax.dynamic_slice_in_dim(sorted_keys, offset, most, 0).reshape(
            most * LP, heads, DHEAD
        )
        value_rows = lax.dynamic_slice_in_dim(sorted_values, offset, most, 0).reshape(
            most * LP, heads, DHEAD
        )
        lengths = lax.dynamic_slice_in_dim(sorted_lengths, offset, most, 0)
        allowed = ((slot_ids[:, None] < amount) & (token_ids[None, :] < lengths[:, None])).reshape(
            1, most * LP
        )
        return (offset, key_rows, value_rows, allowed)

    def forward_turn(rotation, carried):
        visiting, running, totals, accumulated = carried
        source = (blk_place - rotation) % blk_count
        next_running, next_totals, next_accum = ([], [], [])
        unused, key_rows, value_rows, allowed = local_block(source * QDEV + 0)
        outcome = online_update(
            running[0],
            totals[0],
            accumulated[0],
            visiting[0].astype(jnp.bfloat16),
            key_rows,
            value_rows,
            allowed,
        )
        next_running.append(outcome[0])
        next_totals.append(outcome[1])
        next_accum.append(outcome[2])
        return passed_along(
            (visiting, jnp.stack(next_running), jnp.stack(next_totals), jnp.stack(next_accum)),
            "blk",
            1,
        )

    start_state = (
        cross_q.astype(jnp.float32),
        jnp.full((QDEV, heads, LQ), masked_score, jnp.float32),
        jnp.zeros((QDEV, heads, LQ), jnp.float32),
        jnp.zeros((QDEV, LQ, heads, DHEAD), jnp.float32),
    )
    final_state = lax.fori_loop(0, blk_count, forward_turn, start_state)
    cross_out = final_state[3] / jnp.transpose(final_state[2], (0, 2, 1))[:, :, :, None]
    cross_logsum = final_state[1] + jnp.log(final_state[2])
    cross_flat = cross_out.reshape(row_count, width).astype(jnp.bfloat16)
    second = first + across_heads(matmul(cross_flat, c_out))
    normed_three = normalize(second, gain_three).astype(jnp.bfloat16)
    hidden_pre = matmul(normed_three, w_in)
    hidden = jax.nn.gelu(hidden_pre).astype(jnp.bfloat16)
    layer_out = (second + across_heads(matmul(hidden, w_back))).astype(jnp.bfloat16)
    grad_w_back = transposed_times(hidden, cotangent)
    grad_hidden = times_transposed(cotangent, w_back)
    unused, gelu_pull = jax.vjp(jax.nn.gelu, hidden_pre)
    grad_pre = gelu_pull(grad_hidden)[0].astype(jnp.bfloat16)
    grad_w_in = transposed_times(normed_three, grad_pre)
    grad_normed = across_heads(times_transposed(grad_pre, w_in))
    unused, norm_pull = jax.vjp(normalize, second, gain_three)
    grad_resid, grad_gain_ffn = norm_pull(grad_normed)
    grad_second = cotangent.astype(jnp.float32) + grad_resid
    branch_two = grad_second.astype(jnp.bfloat16)
    grad_c_out = transposed_times(cross_flat, branch_two)
    grad_cross = split_heads(times_transposed(branch_two, c_out).astype(jnp.bfloat16))
    cross_deltas = jnp.transpose(
        jnp.sum(grad_cross.astype(jnp.float32) * cross_out, axis=-1), (0, 2, 1)
    )
    empty_slots = jnp.zeros((PDEV + most, LP, width), jnp.float32)

    def add_block(key_grads, value_grads, offset, grad_key, grad_value):
        key_grads = lax.dynamic_update_slice_in_dim(
            key_grads,
            lax.dynamic_slice_in_dim(key_grads, offset, most, 0)
            + grad_key.reshape(most, LP, width),
            offset,
            0,
        )
        value_grads = lax.dynamic_update_slice_in_dim(
            value_grads,
            lax.dynamic_slice_in_dim(value_grads, offset, most, 0)
            + grad_value.reshape(most, LP, width),
            offset,
            0,
        )
        return (key_grads, value_grads)

    def backward_turn(rotation, carried):
        travel, key_grads, value_grads = carried
        visiting, grad_visiting, logsums, deltas, grad_sums = travel
        source = (blk_place - rotation) % blk_count
        offset, key_rows, value_rows, allowed = local_block(source * QDEV + 0)
        grad_query, grad_key, grad_value = block_grads(
            visiting[0].astype(jnp.bfloat16),
            key_rows,
            value_rows,
            allowed,
            grad_visiting[0].astype(jnp.bfloat16),
            logsums[0],
            deltas[0],
        )
        next_grads = [grad_sums[0] + grad_query]
        key_grads, value_grads = add_block(key_grads, value_grads, offset, grad_key, grad_value)
        travel = passed_along(
            (visiting, grad_visiting, logsums, deltas, jnp.stack(next_grads)), "blk", 1
        )
        return (travel, key_grads, value_grads)

    start_travel = (
        final_state[0],
        grad_cross.astype(jnp.float32),
        cross_logsum,
        cross_deltas,
        jnp.zeros((QDEV, LQ, heads, DHEAD), jnp.float32),
    )
    back_state = lax.fori_loop(
        0, blk_count, backward_turn, (start_travel, empty_slots, empty_slots)
    )
    query_total = back_state[0][4]
    key_accum = back_state[1]
    value_accum = back_state[2]
    grad_cross_q = query_total.reshape(row_count, width).astype(jnp.bfloat16)
    enc_key_grads = (
        jnp.take(key_accum[:PDEV], inverse, axis=0).reshape(enc_slots, width).astype(jnp.bfloat16)
    )
    enc_value_grads = (
        jnp.take(value_accum[:PDEV], inverse, axis=0).reshape(enc_slots, width).astype(jnp.bfloat16)
    )
    grad_c_query = transposed_times(grad_cross_q, normed_two)
    grad_normed = across_heads(matmul(grad_cross_q, c_query))
    grad_enc = lax.psum_scatter(
        matmul(enc_key_grads, c_key) + matmul(enc_value_grads, c_value),
        "head",
        scatter_dimension=0,
        tiled=True,
    )
    piece = lax.all_gather(enc_out, "head", axis=0, tiled=True)
    grad_c_key = transposed_times(enc_key_grads, piece)
    grad_c_value = transposed_times(enc_value_grads, piece)
    unused, norm_pull = jax.vjp(normalize, first, gain_two)
    grad_resid, grad_gain_cross = norm_pull(grad_normed)
    grad_first = grad_second + grad_resid
    branch_one = grad_first.astype(jnp.bfloat16)
    grad_w_out = transposed_times(self_flat, branch_one)
    grad_self = split_heads(times_transposed(branch_one, w_out).astype(jnp.bfloat16))
    self_deltas = jnp.transpose(
        jnp.sum(grad_self.astype(jnp.float32) * self_out, axis=-1), (0, 2, 1)
    )
    grad_q_heads, grad_k_heads, grad_v_heads = jax.vmap(block_grads)(
        split_heads(self_q),
        split_heads(self_k),
        split_heads(self_v),
        self_allowed,
        grad_self,
        self_logsum,
        self_deltas,
    )
    grad_self_q = grad_q_heads.reshape(row_count, width).astype(jnp.bfloat16)
    grad_self_k = grad_k_heads.reshape(row_count, width).astype(jnp.bfloat16)
    grad_self_v = grad_v_heads.reshape(row_count, width).astype(jnp.bfloat16)
    grad_w_query = transposed_times(grad_self_q, normed_one)
    grad_w_key = transposed_times(grad_self_k, normed_one)
    grad_w_value = transposed_times(grad_self_v, normed_one)
    grad_normed = across_heads(
        matmul(grad_self_q, w_query) + matmul(grad_self_k, w_key) + matmul(grad_self_v, w_value)
    )
    unused, norm_pull = jax.vjp(normalize, inputs, gain_one)
    grad_resid, grad_gain_self = norm_pull(grad_normed)
    grad_in = grad_first + grad_resid
    summed = lax.psum(
        (
            grad_gain_self,
            grad_gain_cross,
            grad_gain_ffn,
            grad_w_query,
            grad_w_key,
            grad_w_value,
            grad_w_out,
            grad_c_query,
            grad_c_key,
            grad_c_value,
            grad_c_out,
            grad_w_in,
            grad_w_back,
        ),
        ("dp", "blk"),
    )
    return (
        layer_out,
        grad_in,
        grad_enc,
        summed[0],
        summed[1],
        summed[2],
        summed[3],
        summed[4],
        summed[5],
        summed[6],
        summed[7],
        summed[8],
        summed[9],
        summed[10],
        summed[11],
        summed[12],
    )


def solution(mesh):
    return jax.shard_map(
        body,
        mesh=mesh,
        in_specs=(
            P(("dp", "blk"), None),
            P(("dp", "blk", "head"), None),
            P(("dp", "blk")),
            P(("dp", "blk")),
            P(("dp", "blk")),
            P(),
            P(),
            P(),
            P("head", None),
            P("head", None),
            P("head", None),
            P("head", None),
            P("head", None),
            P("head", None),
            P("head", None),
            P("head", None),
            P(None, "head"),
            P("head", None),
            P(("dp", "blk"), None),
        ),
        out_specs=(
            P(("dp", "blk"), None),
            P(("dp", "blk"), None),
            P(("dp", "blk", "head"), None),
            P(),
            P(),
            P(),
            P("head", None),
            P("head", None),
            P("head", None),
            P("head", None),
            P("head", None),
            P("head", None),
            P("head", None),
            P("head", None),
            P(None, "head"),
            P("head", None),
        ),
        check_vma=False,
    )
```

profile of v0, /device:TPU:0, one launch (start us, length us, event | category | flops | bytes accessed | tf_op | source)
XLA Modules:
  0.0 1238.6 jit_solution(3320042578186985371)
XLA Ops:
  26.1 31.4 %all-reduce.13.cloned.1.call-done = f32[128,768]{1,0:T(8,128)} async-done(((f32[128,768]{1,0:T(8,128)}), f32[128,768]{1,0:T(8,128)}) %all-reduce.13.cloned.1.call-update) | async-done | bytes 393232 | tf_op jit(solution)/shard_map/psum | solution.py:46
  60.3 203.8 %all-gather.2.cloned.1.call-done = bf16[7680,768]{1,0:T(8,128)(2,1)} async-done(((bf16[1920,768]{1,0:T(8,128)(2,1)}), bf16[7680,768]{1,0:T(8,128)(2,1)}) %all-gather.2.cloned.1.call-update) | async-done | bytes 11796496 | tf_op jit(solution)/shard_map/all_gather | solution.py:151
  264.2 8.3 convolution_convert_fusion
  274.6 4.7 gather_fusion.2
  279.3 8.3 convolution_convert_fusion.1
  307.6 65.4 %while.50 = (s32[]{:T(128)}, bf16[1,128,3,64]{1,3,2,0:T(8,128)(2,1)}, f32[1,3,128]{2,1,0:T(4,128)S(1)}, f32[1,3,128]{2,1,0:T(4,128)S(1)}, f32[1,128,3,64]{1,3,2,...) while((s32[]{:T(128)}, ...), condition=%wide.region_11.13_spmd.clone, body=%wide.region_6.12_spmd.clone.sunk | while | flops 389342336 | bytes 40118028 | solution.py:217
  377.7 34.1 %all-reduce.15.cloned.1.call-done = f32[128,768]{1,0:T(8,128)} async-done(((f32[128,768]{1,0:T(8,128)}), f32[128,768]{1,0:T(8,128)}) %all-reduce.15.cloned.1.call-update) | async-done | bytes 393232 | tf_op jit(solution)/shard_map/psum | solution.py:46
  421.6 31.7 %all-reduce.17.cloned.1.call-done = f32[128,768]{1,0:T(8,128)} async-done(((f32[128,768]{1,0:T(8,128)}), f32[128,768]{1,0:T(8,128)}) %all-reduce.17.cloned.1.call-update) | async-done | bytes 393232 | tf_op jit(solution)/shard_map/psum | solution.py:46
  465.8 120.6 %while.51 = (s32[]{:T(128)}, bf16[1,128,3,64]{1,3,2,0:T(8,128)(2,1)}, bf16[1,128,3,64]{1,3,2,0:T(8,128)(2,1)S(1)}, f32[1,3,128]{2,1,0:T(4,128)S(1)}, f32[1,3,128...) while((s32[]{:T(128)}, ...), condition=%wide.region_21.23_spmd.clone, body=%wide.region_18.22_spmd.clone.sunk | while | flops 954072704 | bytes 129110864 | solution.py:288
  484.7 4.7 constant_dynamic-slice_fusion.14
  493.8 4.7 constant_dynamic-slice_fusion.15
  515.6 4.6 reshape.593
  539.8 4.7 constant_dynamic-slice_fusion.14
  548.9 4.7 constant_dynamic-slice_fusion.15
  570.1 4.6 reshape.593
  589.0 4.7 slice.7
  593.7 4.8 slice.6
  601.7 4.8 gather_fusion.3
  642.5 13.1 %fusion.114 = f32[7680,768]{1,0:T(8,128)} fusion(bf16[7680,192]{0,1:T(8,128)(2,1)} %bitcast.251, bf16[192,768]{1,0:T(8,128)(2,1)} %param.40), kind=kOutput, calls=%fused_computation.197 | convolution fusion | flops 2264924160 | bytes 26836992 | tf_op jit(solution)/shard_map/dot_general | solution.py:30
  655.6 15.7 %convolution_add_fusion = f32[7680,768]{1,0:T(8,128)} fusion(f32[7680,768]{1,0:T(8,128)} %fusion.114, bf16[7680,192]{0,1:T(8,128)(2,1)S(1)} %bitcast.249, bf16[192,768]{1,0:T(8,128)(2,1)S(1)} %copy-done.46), kind=kOutput, calls=%fused_computation.75 | convolution fusion | flops 2270822400 | bytes 50429952 | tf_op jit(solution)/shard_map/dot_general | solution.py:30
  671.4 6.9 all-reduce.23.cloned.1.call-done
  679.4 24.9 %all-reduce.3 = (f32[768]{0:T(1024)}, f32[768]{0:T(1024)}, f32[768]{0:T(1024)}) all-reduce(f32[768]{0:T(1024)S(1)} %get-tuple-element.757, f32[768]{0:T(1024)S(1)} %copy-done.64, f32[768]{0:T(1024)S(1)} %copy-done.63), channel_id=1, replica_groups=mesh['dp'=4,'blk'=2,'head'=4] {'dp','blk'}, use_global_device_ids=true, to_apply=%region_30.33 | all-reduce | flops 2304 | bytes 18432 | tf_op jit(solution)/shard_map/psum | solution.py:342
  706.5 119.6 %all-reduce.21.cloned.1.call-done = (f32[192,768]{1,0:T(8,128)}, f32[192,768]{1,0:T(8,128)}, f32[192,768]{1,0:T(8,128)}, f32[192,768]{1,0:T(8,128)}, f32[192,768...) async-done(((f32[192,768]{1,0:T(8,128)}, f32[192,768]{1,0:T(8,128)}, ...) | async-done | bytes 9437200 | tf_op jit(solution)/shard_map/psum | solution.py:342
  826.2 392.3 %reduce-scatter.2.cloned.1.call-done = f32[1920,768]{1,0:T(8,128)} async-done(((f32[7680,768]{1,0:T(8,128)}), f32[1920,768]{1,0:T(8,128)}) %reduce-scatter.2.cloned.1.call-update) | async-done | bytes 5898256 | tf_op jit(solution)/shard_map/reduce_scatter | solution.py:303
  (407 shorter events, 265.9 us)
Async XLA Ops:
  7.2 50.3 %all-reduce.13.cloned.1.call-start = ((), (), s32[]{:S(2)}) async-start(), calls=%async_computation.1 | async-start | bytes 786432 | tf_op jit(solution)/shard_map/psum | solution.py:46
  17.6 246.5 %all-gather.2.cloned.1.call-start = ((), (), s32[]{:S(2)}) async-start(), calls=%async_computation.2 | async-start | bytes 14745600 | tf_op jit(solution)/shard_map/all_gather | solution.py:151
  18.4 393.5 %all-reduce.15.cloned.1.call-start = ((), (), s32[]{:S(2)}) async-start(), calls=%async_computation.3 | async-start | bytes 786432 | tf_op jit(solution)/shard_map/psum | solution.py:46
  309.0 31.1 %collective-permute-start = (bf16[1,128,3,64]{1,3,2,0:T(8,128)(2,1)}, bf16[1,128,3,64]{1,3,2,0:T(8,128)(2,1)}, u32[]{:S(2)}, u32[]{:S(2)}) collective-permute-start(bf16[1,128,3,64]{1,3,2,0:T(8,128)(2,1)} %copy.110), channel_id=1, source_target_pairs={{0,4},{4,0},{1,5},{5,1},{2,6},{6,2},{3,7},{7,3},{8,12},{12,8},{9,1... | collective-permute-start | bytes 147464 | tf_op jit(solution)/shard_map/while/body/eval_jaxpr/ppermute | solution.py:20
  332.2 7.8 collective-permute-start.3
  334.9 3.7 collective-permute-start.1
  342.1 30.2 %collective-permute-start = (bf16[1,128,3,64]{1,3,2,0:T(8,128)(2,1)}, bf16[1,128,3,64]{1,3,2,0:T(8,128)(2,1)}, u32[]{:S(2)}, u32[]{:S(2)}) collective-permute-start(bf16[1,128,3,64]{1,3,2,0:T(8,128)(2,1)} %copy.110), channel_id=1, source_target_pairs={{0,4},{4,0},{1,5},{5,1},{2,6},{6,2},{3,7},{7,3},{8,12},{12,8},{9,1... | collective-permute-start | bytes 147464 | tf_op jit(solution)/shard_map/while/body/eval_jaxpr/ppermute | solution.py:20
  364.5 7.8 collective-permute-start.3
  368.1 3.7 collective-permute-start.1
  376.4 76.8 %all-reduce.17.cloned.1.call-start = ((), (), s32[]{:S(2)}) async-start(), calls=%async_computation.4 | async-start | bytes 786432 | tf_op jit(solution)/shard_map/psum | solution.py:46
  416.4 209.5 %all-reduce.19.cloned.1.call-start = ((), (), s32[]{:S(2)}) async-start(), calls=%async_computation.5 | async-start | bytes 786432 | tf_op jit(solution)/shard_map/psum | solution.py:46
  477.4 54.3 %collective-permute-start.4 = (bf16[1,128,3,64]{1,3,2,0:T(8,128)(2,1)S(1)}, bf16[1,128,3,64]{1,3,2,0:T(8,128)(2,1)}, u32[]{:S(2)}, u32[]{:S(2)}) collective-permute-start(bf16[1,128,3,64]{1,3,2,0:T(8,128)(2,1)S(1)} %copy.130), channel_id=1, source_target_pairs={{0,4},{4,0},{1,5},{5,1},{2,6},{6,2},{3,7},{7,3},{8,12},{12,8},{9,1... | collective-permute-start | bytes 147464 | tf_op jit(solution)/shard_map/while/body/eval_jaxpr/ppermute | solution.py:20
  478.7 53.0 %collective-permute-start.5 = (bf16[1,128,3,64]{1,3,2,0:T(8,128)(2,1)S(1)}, bf16[1,128,3,64]{1,3,2,0:T(8,128)(2,1)S(1)}, u32[]{:S(2)}, u32[]{:S(2)}) collective-permute-start(bf16[1,128,3,64]{1,3,2,0:T(8,128)(2,1)S(1)} %copy.131), channel_id=1, source_target_pairs={{0,4},{4,0},{1,5},{5,1},{2,6},{6,2},{3,7},{7,3},{8,12},{12,8},{9,1... | collective-permute-start | bytes 147464 | tf_op jit(solution)/shard_map/while/body/eval_jaxpr/ppermute | solution.py:20
  479.4 52.2 %collective-permute-start.6 = (f32[1,3,128]{2,1,0:T(4,128)S(1)}, f32[1,3,128]{2,1,0:T(4,128)S(1)}, u32[]{:S(2)}, u32[]{:S(2)}) collective-permute-start(f32[1,3,128]{2,1,0:T(4,128)S(1)} %copy.132), channel_id=1, source_target_pairs={{0,4},{4,0},{1,5},{5,1},{2,6},{6,2},{3,7},{7,3},{8,12},{12,8},{9,1... | collective-permute-start | bytes 4616 | tf_op jit(solution)/shard_map/while/body/eval_jaxpr/ppermute | solution.py:20
  480.7 51.0 %collective-permute-start.7 = (f32[1,3,128]{2,1,0:T(4,128)S(1)}, f32[1,3,128]{2,1,0:T(4,128)S(1)}, u32[]{:S(2)}, u32[]{:S(2)}) collective-permute-start(f32[1,3,128]{2,1,0:T(4,128)S(1)} %copy.133), channel_id=1, source_target_pairs={{0,4},{4,0},{1,5},{5,1},{2,6},{6,2},{3,7},{7,3},{8,12},{12,8},{9,1... | collective-permute-start | bytes 4616 | tf_op jit(solution)/shard_map/while/body/eval_jaxpr/ppermute | solution.py:20
  505.5 26.1 %collective-permute-start.8 = (f32[1,128,3,64]{1,3,2,0:T(8,128)S(1)}, f32[1,128,3,64]{1,3,2,0:T(8,128)S(1)}, u32[]{:S(2)}, u32[]{:S(2)}) collective-permute-start(f32[1,128,3,64]{1,3,2,0:T(8,128)S(1)} %fusion.225), channel_id=1, source_target_pairs={{0,4},{4,0},{1,5},{5,1},{2,6},{6,2},{3,7},{7,3},{8,12},{12,8},{9,1... | collective-permute-start | bytes 294920 | tf_op jit(solution)/shard_map/while/body/eval_jaxpr/ppermute | solution.py:20
  532.5 53.6 %collective-permute-start.4 = (bf16[1,128,3,64]{1,3,2,0:T(8,128)(2,1)S(1)}, bf16[1,128,3,64]{1,3,2,0:T(8,128)(2,1)}, u32[]{:S(2)}, u32[]{:S(2)}) collective-permute-start(bf16[1,128,3,64]{1,3,2,0:T(8,128)(2,1)S(1)} %copy.130), channel_id=1, source_target_pairs={{0,4},{4,0},{1,5},{5,1},{2,6},{6,2},{3,7},{7,3},{8,12},{12,8},{9,1... | collective-permute-start | bytes 147464 | tf_op jit(solution)/shard_map/while/body/eval_jaxpr/ppermute | solution.py:20
  533.2 52.9 %collective-permute-start.5 = (bf16[1,128,3,64]{1,3,2,0:T(8,128)(2,1)S(1)}, bf16[1,128,3,64]{1,3,2,0:T(8,128)(2,1)S(1)}, u32[]{:S(2)}, u32[]{:S(2)}) collective-permute-start(bf16[1,128,3,64]{1,3,2,0:T(8,128)(2,1)S(1)} %copy.131), channel_id=1, source_target_pairs={{0,4},{4,0},{1,5},{5,1},{2,6},{6,2},{3,7},{7,3},{8,12},{12,8},{9,1... | collective-permute-start | bytes 147464 | tf_op jit(solution)/shard_map/while/body/eval_jaxpr/ppermute | solution.py:20
  534.5 51.6 %collective-permute-start.6 = (f32[1,3,128]{2,1,0:T(4,128)S(1)}, f32[1,3,128]{2,1,0:T(4,128)S(1)}, u32[]{:S(2)}, u32[]{:S(2)}) collective-permute-start(f32[1,3,128]{2,1,0:T(4,128)S(1)} %copy.132), channel_id=1, source_target_pairs={{0,4},{4,0},{1,5},{5,1},{2,6},{6,2},{3,7},{7,3},{8,12},{12,8},{9,1... | collective-permute-start | bytes 4616 | tf_op jit(solution)/shard_map/while/body/eval_jaxpr/ppermute | solution.py:20
  535.2 50.9 %collective-permute-start.7 = (f32[1,3,128]{2,1,0:T(4,128)S(1)}, f32[1,3,128]{2,1,0:T(4,128)S(1)}, u32[]{:S(2)}, u32[]{:S(2)}) collective-permute-start(f32[1,3,128]{2,1,0:T(4,128)S(1)} %copy.133), channel_id=1, source_target_pairs={{0,4},{4,0},{1,5},{5,1},{2,6},{6,2},{3,7},{7,3},{8,12},{12,8},{9,1... | collective-permute-start | bytes 4616 | tf_op jit(solution)/shard_map/while/body/eval_jaxpr/ppermute | solution.py:20
  560.7 25.5 %collective-permute-start.8 = (f32[1,128,3,64]{1,3,2,0:T(8,128)S(1)}, f32[1,128,3,64]{1,3,2,0:T(8,128)S(1)}, u32[]{:S(2)}, u32[]{:S(2)}) collective-permute-start(f32[1,128,3,64]{1,3,2,0:T(8,128)S(1)} %fusion.225), channel_id=1, source_target_pairs={{0,4},{4,0},{1,5},{5,1},{2,6},{6,2},{3,7},{7,3},{8,12},{12,8},{9,1... | collective-permute-start | bytes 294920 | tf_op jit(solution)/shard_map/while/body/eval_jaxpr/ppermute | solution.py:20
  589.0 89.3 %all-reduce.23.cloned.1.call-start = ((), (), s32[]{:S(2)}) async-start(), calls=%async_computation.8 | async-start | bytes 1572864 | tf_op jit(solution)/shard_map/psum | solution.py:46
  634.5 191.7 %all-reduce.21.cloned.1.call-start = ((), (), s32[]{:S(2)}) async-start(), calls=%async_computation.7 | async-start | bytes 18874368 | tf_op jit(solution)/shard_map/psum | solution.py:342
  642.1 576.3 %reduce-scatter.2.cloned.1.call-start = ((), (), s32[]{:S(2)}) async-start(), calls=%async_computation.6 | async-start | bytes 29491200 | tf_op jit(solution)/shard_map/reduce_scatter | solution.py:303
  (91 other events, 3026.3 us)
Sparse Core Ops, SparseCore 0:
  17.7 39.7 all-reduce.12
  59.2 204.9 all-gather.1
  376.6 35.2 all-reduce.14
  416.6 36.6 all-reduce.16
  589.1 36.8 all-reduce.18
  634.6 43.6 all-reduce.22
  684.8 141.2 all-reduce.20
  829.2 389.1 reduce-scatter.1
where the time goes:
time: 1250 us; the launch traced here: 1240 us
  waiting for transfers between devices  830 us (66%)
  local copies, waits for them, and re-layouts  167 us (13%)
  matrix products  114 us (9%)
  other arithmetic  48.9 us (4%)
  blocking collectives  24.9 us (2%)
  loops' own time  19.2 us (2%)
  starting transfers between devices  19.1 us (2%)
  between operations  16.1 us (1%)
    reduce_scatter x1, waiting for transfers between devices, body(): lax.psum_scatter(matmul(enc_key_grads, c_key) + matmul(enc_value_grads, c...  392 us
    all_gather x1, waiting for transfers between devices, body(): piece = lax.all_gather(enc_out, 'head', axis=0, tiled=True)  204 us
    psum x1, waiting for transfers between devices, body(): lax.psum((grad_gain_self, grad_gain_cross, grad_gain_ffn, grad_w_query, g...  120 us
    psum x5, waiting for transfers between devices, across_heads(): return lax.psum(partial_value, 'head')  108 us
    dot_general x10, matrix products, matmul(): return jnp.dot(left, right, preferred_element_type=jnp.float32)  37.8 us
    dot_general x10, matrix products, times_transposed(): lax.dot_general(left, right, (((1,), (1,)), ((), ())), preferred_element_...  25.8 us
  transfers between devices with their start and end apart: 26, of which 12 were waited for; matrix products, arithmetic and copies ran while one was open for 18% of the time, Pallas kernels for 0%

commit v1 on v0

v1 whole, which is shorter than its diff:
```python
import functools

import jax
import jax.numpy as jnp
from jax import lax
from jax.experimental import pallas as pl
from jax.experimental.pallas import tpu as pltpu
from jax.sharding import PartitionSpec as P

DHEAD = 64
LP = 384
norm_epsilon = 1e-06
masked_score = -1e30
bf16 = jnp.bfloat16
f32 = jnp.float32
PAIR = 2 * DHEAD
STATS = 128
DELTA_LANE = 16
SPLIT_LANE = 32


def nn(left, right):
    return lax.dot_general(left, right, (((1,), (0,)), ((), ())), preferred_element_type=f32)


def nt(left, right):
    return lax.dot_general(left, right, (((1,), (1,)), ((), ())), preferred_element_type=f32)


def tn(left, right):
    return lax.dot_general(left, right, (((0,), (0,)), ((), ())), preferred_element_type=f32)


def exact_nn(left, right):
    return lax.dot_general(
        left,
        right,
        (((1,), (0,)), ((), ())),
        precision=lax.Precision.HIGHEST,
        preferred_element_type=f32,
    )


def norm_scale(values):
    return lax.rsqrt(jnp.mean(values * values, axis=-1, keepdims=True) + norm_epsilon)


def normalize(values, gain):
    return values * norm_scale(values) * gain


def norm_back(upstream, values, gain):
    scale = norm_scale(values)
    unit = values * scale
    scaled = upstream * gain
    grad = scale * (scaled - unit * jnp.mean(scaled * unit, axis=-1, keepdims=True))
    return grad, jnp.sum(upstream * unit, axis=0, keepdims=True)


def vmem():
    return pl.BlockSpec(memory_space=pltpu.VMEM)


def smem():
    return pl.BlockSpec(memory_space=pltpu.SMEM)


def shaped(shape, dtype):
    return jax.ShapeDtypeStruct(shape, dtype)


def call(kernel, outs, scalars, arrays, scratch=(), megabytes=40):
    return pl.pallas_call(
        kernel,
        out_shape=tuple(outs),
        in_specs=[smem()] * len(scalars) + [vmem()] * len(arrays),
        out_specs=tuple(vmem() for _ in outs),
        scratch_shapes=list(scratch),
        compiler_params=pltpu.CompilerParams(vmem_limit_bytes=megabytes * 1024 * 1024),
    )(*scalars, *arrays)


def rows_of(place, count):
    return pl.ds(pl.multiple_of(place * count, count), count)


def head_blocks(width, head_count, shift):
    return [(j ^ shift) * width for j in range(head_count)]


def permuted(values, width, head_count, shift):
    if shift == 0:
        return values
    return jnp.concatenate(
        [values[:, o : o + width] for o in head_blocks(width, head_count, shift)], axis=1
    )


def self_kernel(
    len_ref, dec_ref, gain_ref, wq_ref, wk_ref, wv_ref, normed_ref, qkv_ref, out_ref
):
    rows = dec_ref.shape[0]
    width = wq_ref.shape[0]
    normed = normalize(dec_ref[...].astype(f32), gain_ref[...].astype(f32)).astype(bf16)
    normed_ref[...] = normed
    for i, weight in enumerate((wq_ref, wk_ref, wv_ref)):
        qkv_ref[:, i * width : (i + 1) * width] = nt(normed, weight[...]).astype(bf16)
    at_q = lax.broadcasted_iota(jnp.int32, (rows, rows), 0)
    at_k = lax.broadcasted_iota(jnp.int32, (rows, rows), 1)
    allowed = (at_k <= at_q) & (at_k < len_ref[0])
    outs = []
    for h in range(width // DHEAD):
        o = h * DHEAD
        q = qkv_ref[:, o : o + DHEAD]
        k = qkv_ref[:, width + o : width + o + DHEAD]
        v = qkv_ref[:, 2 * width + o : 2 * width + o + DHEAD]
        scores = jnp.where(allowed, nt(q, k), masked_score)
        raised = jnp.exp(scores - jnp.max(scores, axis=-1, keepdims=True))
        probs = raised / jnp.sum(raised, axis=-1, keepdims=True)
        outs.append(nn(probs.astype(bf16), v))
    out_ref[...] = jnp.concatenate(outs, axis=1).astype(bf16)


def query_kernel(blk_count, head_count, *refs):
    chunks = refs[: blk_count * head_count]
    refs = refs[blk_count * head_count :]
    decs = refs[:blk_count]
    w_out_ref, c_query_ref, gain_ref, first_ref, normed_ref, q_ref = refs[blk_count:]
    gain = gain_ref[...].astype(f32)
    for kb in range(blk_count):
        attended = jnp.concatenate(
            [chunks[kb * head_count + kh][...] for kh in range(head_count)], axis=1
        )
        first = decs[kb][...].astype(f32) + nn(attended, w_out_ref[...])
        normed = normalize(first, gain).astype(bf16)
        if kb == 0:
            first_ref[...] = first
            normed_ref[...] = normed
        q_ref[kb] = nt(normed, c_query_ref[...]).astype(bf16)


def spread_pairs(values, target, kb):
    rows = values.shape[0]
    for j in range(values.shape[1] // PAIR):
        pair = values[:, j * PAIR : (j + 1) * PAIR]
        lane = lax.broadcasted_iota(jnp.int32, pair.shape, 1)
        zero = jnp.zeros_like(pair)
        target[kb, j, 0:rows, :] = jnp.where(lane < DHEAD, pair, zero)
        target[kb, j, rows : 2 * rows, :] = jnp.where(lane < DHEAD, zero, pair)


def cross_forward_kernel(blk_count, head_count, width, *refs):
    slot_ref, len_ref, me_ref, q_ref, k_ref, vt_ref = refs[:6]
    chunk_count = blk_count * head_count
    out_refs = refs[6 : 6 + chunk_count]
    q2, acc, highest, totals, stat, flat, flat_stat = refs[6 + chunk_count :]
    rows, depth = q_ref.shape[1], q_ref.shape[2]
    pairs = depth // PAIR
    step = pl.program_id(0)

    @pl.when(step == 0)
    def _():
        for kb in range(blk_count):
            spread_pairs(q_ref[kb], q2, kb)
        highest[...] = jnp.full(highest.shape, masked_score, f32)
        totals[...] = jnp.zeros(totals.shape, f32)
        acc[...] = jnp.zeros(acc.shape, f32)

    slot = slot_ref[step]
    valid = lax.broadcasted_iota(jnp.int32, (LP, 2 * rows), 0) < len_ref[step]
    for j in range(pairs):
        span = slice(j * PAIR, (j + 1) * PAIR)
        scores = jnp.where(valid, nt(k_ref[:, span], q2[slot, j]), masked_score)
        before = highest[slot, j : j + 1, :]
        newest = jnp.maximum(before, jnp.max(scores, axis=0, keepdims=True))
        raised = jnp.exp(scores - newest)
        factor = jnp.exp(before - newest)
        highest[slot, j : j + 1, :] = newest
        totals[slot, j : j + 1, :] = totals[slot, j : j + 1, :] * factor + jnp.sum(
            raised, axis=0, keepdims=True
        )
        update = nn(vt_ref[span, :], raised.astype(bf16))
        low = slice(j * PAIR, j * PAIR + DHEAD)
        high = slice(j * PAIR + DHEAD, (j + 1) * PAIR)
        acc[slot, low, :] = acc[slot, low, :] * factor[:, :rows] + update[:DHEAD, :rows]
        acc[slot, high, :] = acc[slot, high, :] * factor[:, rows:] + update[DHEAD:, rows:]

    @pl.when(step == pl.num_programs(0) - 1)
    def _():
        stat[...] = jnp.zeros(stat.shape, f32)
        piece = rows // head_count
        per = width // DHEAD
        for kb in range(blk_count):
            flat[...] = acc[kb].T
            for kh in range(head_count):
                for head in range(depth // DHEAD):
                    at = ((head // per) ^ kh) * per + head % per
                    lanes = slice((head % 2) * rows, (head % 2 + 1) * rows)
                    stat[at : at + 1, :] = highest[kb, head // 2 : head // 2 + 1, lanes]
                    stat[DHEAD + at : DHEAD + at + 1, :] = totals[
                        kb, head // 2 : head // 2 + 1, lanes
                    ]
                flat_stat[...] = stat[...].T
                mine = rows_of(me_ref[0] ^ kh, piece)
                target = out_refs[kb * head_count + kh]
                target[:, :depth] = permuted(flat[mine, :], width, head_count, kh)
                target[:, depth:] = flat_stat[mine, :]


def cross_forward(slots, lengths, me, queries, keys, values_t, head_count, width):
    blk_count, rows, depth = queries.shape
    passages = slots.shape[0]
    piece = rows // head_count
    chunk_count = blk_count * head_count
    pairs = depth // PAIR
    grid = pltpu.PrefetchScalarGridSpec(
        num_scalar_prefetch=3,
        grid=(passages,),
        in_specs=[
            pl.BlockSpec((blk_count, rows, depth), lambda p, *_: (0, 0, 0)),
            pl.BlockSpec((LP, depth), lambda p, *_: (p, 0)),
            pl.BlockSpec((depth, LP), lambda p, *_: (0, p)),
        ],
        out_specs=tuple(
            pl.BlockSpec((piece, depth + STATS), lambda p, *_: (0, 0)) for _ in range(chunk_count)
        ),
        scratch_shapes=[
            pltpu.VMEM((blk_count, pairs, 2 * rows, PAIR), bf16),
            pltpu.VMEM((blk_count, depth, rows), f32),
            pltpu.VMEM((blk_count, 8, 2 * rows), f32),
            pltpu.VMEM((blk_count, 8, 2 * rows), f32),
            pltpu.VMEM((STATS, rows), f32),
            pltpu.VMEM((rows, depth), f32),
            pltpu.VMEM((rows, STATS), f32),
        ],
    )
    return pl.pallas_call(
        functools.partial(cross_forward_kernel, blk_count, head_count, width),
        out_shape=tuple(shaped((piece, depth + STATS), f32) for _ in range(chunk_count)),
        grid_spec=grid,
        compiler_params=pltpu.CompilerParams(
            vmem_limit_bytes=50 * 1024 * 1024, dimension_semantics=("arbitrary",)
        ),
    )(slots, lengths, me, queries, keys, values_t)


def head_matrix(depth):
    head = lax.broadcasted_iota(jnp.int32, (STATS, depth), 0)
    column = lax.broadcasted_iota(jnp.int32, (STATS, depth), 1)
    return (head == column // DHEAD).astype(f32)


def combine_kernel(chunk_count, me_ref, *refs):
    chunks = refs[:chunk_count]
    first_ref, c_out_ref, gain_ref, cross_ref, second_ref, logsum_ref, message_ref = refs[
        chunk_count:
    ]
    piece, depth = cross_ref.shape
    stats = [chunk[:, depth:] for chunk in chunks]
    highest = stats[0]
    for other in stats[1:]:
        highest = jnp.maximum(highest, other)
    lane = lax.broadcasted_iota(jnp.int32, (piece, STATS), 1)
    real = lane < depth // DHEAD
    weights = [jnp.where(real, jnp.exp(one - highest), 0.0) for one in stats]
    total = sum(w * pltpu.roll(one, STATS - DHEAD, 1) for w, one in zip(weights, stats))
    total = jnp.where(real, total, 1.0)
    logsum_ref[...] = jnp.where(real, highest + jnp.log(total), 0.0)
    spread = head_matrix(depth)
    weighted = exact_nn(jnp.concatenate(weights, axis=0), spread)
    cross = sum(
        chunk[:, :depth] * weighted[i * piece : (i + 1) * piece] for i, chunk in enumerate(chunks)
    )
    cross = cross / exact_nn(total, spread)
    cross_ref[...] = cross
    rounded = cross.astype(bf16)
    first = first_ref[rows_of(me_ref[0], piece), :]
    second = first + nn(rounded, c_out_ref[...])
    second_ref[...] = second
    message_ref[:, :depth] = normalize(second, gain_ref[...].astype(f32)).astype(bf16)
    message_ref[:, depth:] = rounded


def ffn_kernel(head_count, width, me_ref, *refs):
    chunks = refs[:head_count]
    cot_ref, w_in_ref, w_back_ref = refs[head_count : head_count + 3]
    grads = refs[head_count + 3 : 2 * head_count + 3]
    normed_ref, hidden_ref, pre_grad_ref, cols_ref, partial_ref, total = refs[2 * head_count + 3 :]
    piece, depth = grads[0].shape
    for k, chunk in enumerate(chunks):
        mine = rows_of(me_ref[0] ^ k, piece)
        normed_ref[mine, :] = chunk[:, :depth]
        cols_ref[mine, :] = chunk[:, depth + k * width : depth + (k + 1) * width]
    before = nn(normed_ref[...], w_in_ref[...])
    root = 0.7978845608028654
    cube = 0.044715
    square = before * before
    bend = jnp.tanh(root * (before + cube * before * square))
    hidden_ref[...] = (0.5 * before * (1.0 + bend)).astype(bf16)
    slope = 0.5 * (1.0 + bend) + 0.5 * before * (1.0 - bend * bend) * root * (
        1.0 + 3.0 * cube * square
    )
    pre_grad_ref[...] = (nt(cot_ref[...], w_back_ref[...]) * slope).astype(bf16)
    total[...] = nt(pre_grad_ref[...], w_in_ref[...])
    for k, grad in enumerate(grads):
        grad[...] = total[rows_of(me_ref[0] ^ k, piece), :]
    partial_ref[...] = nn(hidden_ref[...], w_back_ref[...])


def branch_kernel(head_count, width, me_ref, *refs):
    chunks = refs[:head_count]
    second_ref, gain_ref, cot_ref, c_out_ref, cross_ref, logsum_ref = refs[
        head_count : head_count + 6
    ]
    grad_ref, gain_grad_ref = refs[head_count + 6 : head_count + 8]
    messages = refs[head_count + 8 :]
    piece, depth = second_ref.shape
    upstream = sum(chunk[...] for chunk in chunks)
    grad, gain_grad_ref[...] = norm_back(upstream, second_ref[...], gain_ref[...].astype(f32))
    grad = cot_ref[rows_of(me_ref[0], piece), :].astype(f32) + grad
    grad_ref[...] = grad
    branch = grad.astype(bf16)
    grad_cross = nt(branch, c_out_ref[...]).astype(bf16).astype(f32)
    spread = head_matrix(depth)
    deltas = lax.dot_general(
        grad_cross * cross_ref[...],
        spread,
        (((1,), (1,)), ((), ())),
        precision=lax.Precision.HIGHEST,
        preferred_element_type=f32,
    )
    stats = logsum_ref[...] + pltpu.roll(deltas, DELTA_LANE, 1)
    per = width // DHEAD
    heads = depth // DHEAD
    source = lax.broadcasted_iota(jnp.int32, (STATS, STATS), 0)
    target = lax.broadcasted_iota(jnp.int32, (STATS, STATS), 1)
    place = source % DELTA_LANE
    for k, message in enumerate(messages):
        moved = (source - place) + ((place // per) ^ k) * per + place % per
        shuffle = ((target == moved) & (place < heads) & (source < 2 * DELTA_LANE)).astype(f32)
        aligned = exact_nn(stats, shuffle)
        high = aligned.astype(bf16).astype(f32)
        middle = (aligned - high).astype(bf16).astype(f32)
        lowest = aligned - high - middle
        message[:, :depth] = branch
        message[:, depth:] = (
            high + pltpu.roll(middle, SPLIT_LANE, 1) + pltpu.roll(lowest, 2 * SPLIT_LANE, 1)
        ).astype(bf16)


def cross_backward_kernel(blk_count, head_count, width, *refs):
    slot_ref, len_ref, me_ref, q_ref, c_out_ref, k_ref, v_ref = refs[:7]
    chunk_count = blk_count * head_count
    chunks = refs[7 : 7 + chunk_count]
    refs = refs[7 + chunk_count :]
    out_refs = refs[:chunk_count]
    branch_ref, grad_k_ref, grad_v_ref = refs[chunk_count : chunk_count + 3]
    q2, g2, stats, branch, flat_stat, grad_q = refs[chunk_count + 3 :]
    rows, depth = q_ref.shape[1], q_ref.shape[2]
    pairs = depth // PAIR
    piece = rows // head_count
    step = pl.program_id(0)

    @pl.when(step == 0)
    def _():
        for kb in range(blk_count):
            for kh in range(head_count):
                chunk = chunks[kb * head_count + kh]
                mine = rows_of(me_ref[0] ^ kh, piece)
                branch[mine, :] = chunk[:, :depth]
                packed = chunk[:, depth:].astype(f32)
                flat_stat[mine, :] = (
                    packed
                    + pltpu.roll(packed, STATS - SPLIT_LANE, 1)
                    + pltpu.roll(packed, STATS - 2 * SPLIT_LANE, 1)
                )
            if kb == 0:
                branch_ref[...] = branch[...]
            stats[kb] = flat_stat[...].T
            spread_pairs(q_ref[kb], q2, kb)
            spread_pairs(nt(branch[...], c_out_ref[...]).astype(bf16), g2, kb)
        grad_q[...] = jnp.zeros(grad_q.shape, f32)

    slot = slot_ref[step]
    valid = lax.broadcasted_iota(jnp.int32, (LP, 2 * rows), 0) < len_ref[step]
    lane = lax.broadcasted_iota(jnp.int32, (rows, PAIR), 1)
    for j in range(pairs):
        span = slice(j * PAIR, (j + 1) * PAIR)
        logsum = jnp.concatenate(
            [stats[slot, 2 * j : 2 * j + 1, :], stats[slot, 2 * j + 1 : 2 * j + 2, :]], axis=1
        )
        o = DELTA_LANE + 2 * j
        delta = jnp.concatenate([stats[slot, o : o + 1, :], stats[slot, o + 1 : o + 2, :]], axis=1)
        scores = nt(k_ref[:, span], q2[slot, j])
        probs = jnp.where(valid, jnp.exp(scores - logsum), 0.0)
        grad_probs = nt(v_ref[:, span], g2[slot, j])
        grad_scores = (probs * (grad_probs - delta)).astype(bf16)
        grad_v_ref[:, span] = nn(probs.astype(bf16), g2[slot, j]).astype(bf16)
        grad_k_ref[:, span] = nn(grad_scores, q2[slot, j]).astype(bf16)
        both = tn(grad_scores, k_ref[:, span])
        grad_q[slot, :, span] = grad_q[slot, :, span] + jnp.where(
            lane < DHEAD, both[:rows], both[rows:]
        )

    @pl.when(step == pl.num_programs(0) - 1)
    def _():
        for kb in range(blk_count):
            for kh in range(head_count):
                mine = rows_of(me_ref[0] ^ kh, piece)
                out_refs[kb * head_count + kh][...] = permuted(
                    grad_q[kb, mine, :], width, head_count, kh
                )


def cross_backward(slots, lengths, me, queries, c_out, keys, values, chunks, head_count, width):
    blk_count, rows, depth = queries.shape
    passages = slots.shape[0]
    piece = rows // head_count
    chunk_count = blk_count * head_count
    pairs = depth // PAIR
    whole = lambda shape: pl.BlockSpec(shape, lambda p, *_: (0,) * len(shape))
    passage = pl.BlockSpec((LP, depth), lambda p, *_: (p, 0))
    grid = pltpu.PrefetchScalarGridSpec(
        num_scalar_prefetch=3,
        grid=(passages,),
        in_specs=[
            whole((blk_count, rows, depth)),
            whole((depth, depth)),
            passage,
            passage,
            *[whole((piece, depth + STATS)) for _ in range(chunk_count)],
        ],
        out_specs=(
            *[whole((piece, depth)) for _ in range(chunk_count)],
            whole((rows, depth)),
            passage,
            passage,
        ),
        scratch_shapes=[
            pltpu.VMEM((blk_count, pairs, 2 * rows, PAIR), bf16),
            pltpu.VMEM((blk_count, pairs, 2 * rows, PAIR), bf16),
            pltpu.VMEM((blk_count, STATS, rows), f32),
            pltpu.VMEM((rows, depth), bf16),
            pltpu.VMEM((rows, STATS), f32),
            pltpu.VMEM((blk_count, rows, depth), f32),
        ],
    )
    return pl.pallas_call(
        functools.partial(cross_backward_kernel, blk_count, head_count, width),
        out_shape=(
            *[shaped((piece, depth), f32) for _ in range(chunk_count)],
            shaped((rows, depth), bf16),
            shaped(keys.shape, bf16),
            shaped(keys.shape, bf16),
        ),
        grid_spec=grid,
        compiler_params=pltpu.CompilerParams(
            vmem_limit_bytes=56 * 1024 * 1024, dimension_semantics=("arbitrary",)
        ),
    )(slots, lengths, me, queries, c_out, keys, values, *chunks)


def first_kernel(chunk_count, me_ref, *refs):
    chunks = refs[:chunk_count]
    first_ref, gain_ref, c_query_ref, second_grad_ref, grad_ref, gain_grad_ref, message_ref = refs[
        chunk_count:
    ]
    piece, depth = grad_ref.shape
    grad_q = sum(chunk[...] for chunk in chunks).astype(bf16)
    upstream = nn(grad_q, c_query_ref[...])
    first = first_ref[rows_of(me_ref[0], piece), :]
    grad, gain_grad_ref[...] = norm_back(upstream, first, gain_ref[...].astype(f32))
    grad = second_grad_ref[...] + grad
    grad_ref[...] = grad
    message_ref[:, :depth] = grad.astype(bf16)
    message_ref[:, depth:] = grad_q


def self_back_kernel(head_count, len_ref, me_ref, *refs):
    chunks = refs[:head_count]
    w_out_ref, qkv_ref, wq_ref, wk_ref, wv_ref = refs[head_count : head_count + 5]
    grads = refs[head_count + 5 : 2 * head_count + 5]
    branch_ref, cols_ref, grad_qkv_ref, total = refs[2 * head_count + 5 :]
    rows, depth = branch_ref.shape
    width = wq_ref.shape[0]
    piece = rows // head_count
    for k, chunk in enumerate(chunks):
        mine = rows_of(me_ref[0] ^ k, piece)
        branch_ref[mine, :] = chunk[:, :depth]
        cols_ref[mine, :] = chunk[:, depth + k * width : depth + (k + 1) * width]
    grad_self = nt(branch_ref[...], w_out_ref[...]).astype(bf16)
    at_q = lax.broadcasted_iota(jnp.int32, (rows, rows), 0)
    at_k = lax.broadcasted_iota(jnp.int32, (rows, rows), 1)
    allowed = (at_k <= at_q) & (at_k < len_ref[0])
    grad_q, grad_k, grad_v = [], [], []
    for h in range(width // DHEAD):
        o = h * DHEAD
        q = qkv_ref[:, o : o + DHEAD]
        k = qkv_ref[:, width + o : width + o + DHEAD]
        v = qkv_ref[:, 2 * width + o : 2 * width + o + DHEAD]
        g = grad_self[:, o : o + DHEAD]
        scores = jnp.where(allowed, nt(q, k), masked_score)
        raised = jnp.exp(scores - jnp.max(scores, axis=-1, keepdims=True))
        probs = raised / jnp.sum(raised, axis=-1, keepdims=True)
        grad_probs = nt(g, v)
        delta = jnp.sum(probs * grad_probs, axis=-1, keepdims=True)
        grad_scores = (probs * (grad_probs - delta)).astype(bf16)
        grad_q.append(nn(grad_scores, k))
        grad_k.append(tn(grad_scores, q))
        grad_v.append(tn(probs.astype(bf16), g))
    for i, parts in enumerate((grad_q, grad_k, grad_v)):
        grad_qkv_ref[:, i * width : (i + 1) * width] = jnp.concatenate(parts, axis=1).astype(bf16)
    total[...] = (
        nn(grad_qkv_ref[:, :width], wq_ref[...])
        + nn(grad_qkv_ref[:, width : 2 * width], wk_ref[...])
        + nn(grad_qkv_ref[:, 2 * width :], wv_ref[...])
    )
    for k, grad in enumerate(grads):
        grad[...] = total[rows_of(me_ref[0] ^ k, piece), :]


def input_kernel(head_count, me_ref, *refs):
    chunks = refs[:head_count]
    dec_ref, gain_ref, first_grad_ref, grad_ref, gain_grad_ref = refs[head_count:]
    piece, depth = grad_ref.shape
    upstream = sum(chunk[...] for chunk in chunks)
    values = dec_ref[rows_of(me_ref[0], piece), :].astype(f32)
    grad, gain_grad_ref[...] = norm_back(upstream, values, gain_ref[...].astype(f32))
    grad_ref[...] = first_grad_ref[...] + grad


def place_kernel(head_count, me_ref, *refs):
    out_ref = refs[head_count]
    for k in range(head_count):
        out_ref[rows_of(me_ref[0] ^ k, refs[k].shape[0]), :] = refs[k][...]


def partner(array, axis, by):
    size = lax.axis_size(axis)
    return lax.ppermute(array, axis, [(i, i ^ by) for i in range(size)])


def group_gather(array, count):
    return [array] + [partner(array, ("blk", "head"), k) for k in range(1, count)]


def group_exchange(arrays):
    return [arrays[0]] + [partner(arrays[k], ("blk", "head"), k) for k in range(1, len(arrays))]


def head_gather(array):
    return [array] + [partner(array, "head", k) for k in range(1, lax.axis_size("head"))]


def head_exchange(arrays):
    return [arrays[0]] + [partner(arrays[k], "head", k) for k in range(1, len(arrays))]


def gather_pair(one, two, core):
    mine = jnp.where(core == 0, one, two)
    half = mine.shape[0] // 2
    near = partner(mine, "head", 1)
    far = partner(mine, "head", 3)
    lower = partner(far[:half], "head", 1)
    upper = partner(near[half:], "head", 3)
    whole = jnp.concatenate([mine, near, lower, upper, far], axis=0)
    other = partner(whole, "dp", 1)
    return jnp.where(core == 0, whole, other), jnp.where(core == 0, other, whole)


def plane_gather(array):
    array = jnp.concatenate([array, partner(array, "blk", 1)], axis=0)
    array = jnp.concatenate([array, partner(array, "dp", 2)], axis=0)
    return array, partner(array, "dp", 1)


def weight_grad(left, right):
    return sum(tn(a, b) for a, b in zip(left, right))


def body(
    dec_in,
    enc_out,
    passage_len,
    dec_len,
    passage_owner,
    gain_self,
    gain_cross,
    gain_ffn,
    w_query,
    w_key,
    w_value,
    w_out,
    c_query,
    c_key,
    c_value,
    c_out,
    w_in,
    w_back,
    cotangent,
):
    blk_count = lax.axis_size("blk")
    dp_count = lax.axis_size("dp")
    head_count = lax.axis_size("head")
    small = blk_count * dp_count == 8
    chunk_count = blk_count * head_count
    width, depth = w_query.shape
    rows = dec_in.shape[0]
    piece = rows // head_count
    passages = enc_out.shape[0] // LP
    head_place = lax.axis_index("head")
    blk_place = lax.axis_index("blk")
    core = lax.axis_index("dp") % 2
    me = head_place.astype(jnp.int32).reshape(1)
    gain_one = gain_self.reshape(1, depth)
    gain_two = gain_cross.reshape(1, depth)
    gain_three = gain_ffn.reshape(1, depth)

    key_full, value_full = gather_pair(c_key, c_value, core)
    out_full, query_full = gather_pair(w_out, c_query, core)
    cross_out_full, _ = gather_pair(c_out, c_out, core)

    slots = lax.dynamic_slice_in_dim(passage_owner, head_place * passages, passages) ^ blk_place
    lengths = lax.dynamic_slice_in_dim(passage_len, head_place * passages, passages)

    normed_one, self_qkv, self_flat = call(
        self_kernel,
        [shaped((rows, depth), bf16), shaped((rows, 3 * width), bf16), shaped((rows, width), bf16)],
        [dec_len],
        [dec_in, gain_one, w_query, w_key, w_value],
    )
    decs = [dec_in] + [partner(dec_in, "blk", k) for k in range(1, blk_count)]
    self_chunks = group_gather(self_flat, chunk_count)
    first, normed_two, queries = call(
        functools.partial(query_kernel, blk_count, head_count),
        [
            shaped((rows, depth), f32),
            shaped((rows, depth), bf16),
            shaped((blk_count, rows, depth), bf16),
        ],
        [],
        [*self_chunks, *decs, out_full, query_full, gain_two],
    )
    enc_keys = nt(enc_out, key_full).astype(bf16)
    enc_values_t = nt(value_full, enc_out).astype(bf16)
    enc_values = nt(enc_out, value_full).astype(bf16)

    partials = cross_forward(
        slots, lengths, me, queries, enc_keys, enc_values_t, head_count, width
    )
    partials = group_exchange(partials)
    cross, second, logsum, message = call(
        functools.partial(combine_kernel, chunk_count),
        [
            shaped((piece, depth), f32),
            shaped((piece, depth), f32),
            shaped((piece, STATS), f32),
            shaped((piece, 2 * depth), bf16),
        ],
        [me],
        [*partials, first, cross_out_full, gain_three],
    )
    messages = head_gather(message)
    outs = call(
        functools.partial(ffn_kernel, head_count, width),
        [shaped((piece, depth), f32)] * head_count
        + [
            shaped((rows, depth), bf16),
            shaped((rows, w_in.shape[1]), bf16),
            shaped((rows, w_in.shape[1]), bf16),
            shaped((rows, width), bf16),
            shaped((rows, depth), f32),
        ],
        [me],
        [*messages, cotangent, w_in, w_back],
        [pltpu.VMEM((rows, depth), f32)],
    )
    normed_three, hidden, grad_pre, cross_cols, ffn_partial = outs[head_count:]
    upstream = head_exchange(outs[:head_count])
    outs = call(
        functools.partial(branch_kernel, head_count, width),
        [shaped((piece, depth), f32), shaped((1, depth), f32)]
        + [shaped((piece, depth + STATS), bf16)] * head_count,
        [me],
        [*upstream, second, gain_three, cotangent, cross_out_full, cross, logsum],
    )
    grad_second, gain_ffn_part = outs[:2]
    messages = [outs[2 + k % head_count] for k in range(chunk_count)]
    branches = group_exchange(messages)
    outs = cross_backward(
        slots,
        lengths,
        me,
        queries,
        cross_out_full,
        enc_keys,
        enc_values,
        branches,
        head_count,
        width,
    )
    branch_two, enc_key_grads, enc_value_grads = outs[chunk_count:]
    query_grads = group_exchange(outs[:chunk_count])
    grad_first, gain_cross_part, message = call(
        functools.partial(first_kernel, chunk_count),
        [shaped((piece, depth), f32), shaped((1, depth), f32), shaped((piece, 2 * depth), bf16)],
        [me],
        [*query_grads, first, gain_two, query_full, grad_second],
    )
    messages = head_gather(message)
    outs = call(
        functools.partial(self_back_kernel, head_count),
        [shaped((piece, depth), f32)] * head_count
        + [
            shaped((rows, depth), bf16),
            shaped((rows, width), bf16),
            shaped((rows, 3 * width), bf16),
        ],
        [dec_len, me],
        [*messages, w_out, self_qkv, w_query, w_key, w_value],
        [pltpu.VMEM((rows, depth), f32)],
    )
    branch_one, grad_query_cols, grad_qkv = outs[head_count:]
    upstream = head_exchange(outs[:head_count])
    grad_in_rows, gain_self_part = call(
        functools.partial(input_kernel, head_count),
        [shaped((piece, depth), f32), shaped((1, depth), f32)],
        [me],
        [*upstream, dec_in, gain_one, grad_first],
    )
    (grad_in,) = call(
        functools.partial(place_kernel, head_count),
        [shaped((rows, depth), f32)],
        [me],
        head_gather(grad_in_rows),
    )

    layer_rows = lax.psum(ffn_partial, "head")
    (second_all,) = call(
        functools.partial(place_kernel, head_count),
        [shaped((rows, depth), f32)],
        [me],
        head_gather(second),
    )
    layer_out = (second_all + layer_rows).astype(bf16)

    grad_enc = nn(enc_key_grads, key_full) + nn(enc_value_grads, value_full)

    key_part = tn(enc_key_grads, enc_out).astype(bf16)
    value_part = tn(enc_value_grads, enc_out).astype(bf16)
    theirs = partner(jnp.where(core == 0, value_part, key_part), "dp", 1)
    own = jnp.where(core == 0, key_part, value_part).astype(f32) + theirs.astype(f32)
    own = own.astype(bf16).reshape(head_count, width, depth)
    shares = head_exchange([own[k] for k in range(head_count)])
    share = sum(part.astype(f32) for part in shares)
    for bit in range(1, dp_count.bit_length() - 1):
        share = share + partner(share.astype(bf16), "dp", 2**bit).astype(f32)
    for bit in range(blk_count.bit_length() - 1):
        share = share + partner(share.astype(bf16), "blk", 2**bit).astype(f32)
    other = partner(share, "dp", 1)
    grad_c_key = jnp.where(core == 0, share, other)
    grad_c_value = jnp.where(core == 0, other, share)

    if small:
        together = plane_gather
    else:
        together = lambda array: (array,)
    early = together(jnp.concatenate([normed_one, cotangent], axis=1))
    later = together(jnp.concatenate([normed_two, self_flat], axis=1))
    middle = together(jnp.concatenate([normed_three, hidden, grad_pre], axis=1))
    cross_side = together(jnp.concatenate([branch_two, cross_cols], axis=1))
    self_side = together(jnp.concatenate([branch_one, grad_query_cols], axis=1))
    last = together(grad_qkv)
    cols = lambda arrays, start, count: [array[:, start : start + count] for array in arrays]
    hidden_width = w_in.shape[1]
    sums = [
        weight_grad(last, cols(early, 0, depth)),
        weight_grad(cols(later, depth, width), cols(self_side, 0, depth)),
        weight_grad(cols(self_side, depth, width), cols(later, 0, depth)),
        weight_grad(cols(cross_side, depth, width), cols(cross_side, 0, depth)),
        weight_grad(cols(middle, 0, depth), cols(middle, depth + hidden_width, hidden_width)),
        weight_grad(cols(middle, depth, hidden_width), cols(early, depth, depth)),
    ]
    if not small:
        sums = lax.psum(tuple(sums), ("dp", "blk"))
    gains = lax.psum(
        jnp.concatenate([gain_self_part, gain_cross_part, gain_ffn_part], axis=0),
        ("dp", "blk", "head"),
    )
    return (
        layer_out,
        grad_in,
        grad_enc,
        gains[0],
        gains[1],
        gains[2],
        sums[0][:width],
        sums[0][width : 2 * width],
        sums[0][2 * width :],
        sums[1],
        sums[2],
        grad_c_key,
        grad_c_value,
        sums[3],
        sums[4],
        sums[5],
    )


def solution(mesh):
    rows = P(("dp", "blk"), None)
    enc = P(("dp", "blk", "head"), None)
    each = P(("dp", "blk"))
    heads = P("head", None)
    return jax.shard_map(
        body,
        mesh=mesh,
        in_specs=(
            rows,
            enc,
            each,
            each,
            each,
            P(),
            P(),
            P(),
            *[heads] * 8,
            P(None, "head"),
            heads,
            rows,
        ),
        out_specs=(rows, rows, enc, P(), P(), P(), *[heads] * 8, P(None, "head"), heads),
        check_vma=False,
    )
```

time: 1250 us -> 465 us (0.37)
  waiting for transfers between devices: 830 us -> 116 us
  local copies, waits for them, and re-layouts: 167 us -> 56.8 us
  starting transfers between devices: 19.1 us -> 119 us
  matrix products: 114 us -> 40.4 us
  Pallas kernels: 0 us -> 43.4 us
  other arithmetic: 48.9 us -> 26.1 us
  loops' own time: 19.2 us -> 0 us
  blocking collectives: 24.9 us -> 41 us
    reduce_scatter x1 -> x0, waiting for transfers between devices: 392 us -> none  [body(): lax.psum_scatter(matmul(enc_key_grads, c_key) + matmul(enc_value_grads, c...]
    psum x6 -> x1, waiting for transfers between devices: 227 us -> 0.01 us  [body(): layer_rows = lax.psum(ffn_partial, 'head')]
    all_gather x1 -> x0, waiting for transfers between devices: 204 us -> none  [body(): piece = lax.all_gather(enc_out, 'head', axis=0, tiled=True)]
    ppermute x18 -> x87, waiting for transfers between devices: 5.18 us -> 116 us  [partner(): return lax.ppermute(array, axis, [(i, i ^ by) for i in range(size)])]
    ppermute x18 -> x87, starting transfers between devices: 18.5 us -> 118 us  [partner(): return lax.ppermute(array, axis, [(i, i ^ by) for i in range(size)])]
    dot_general x50 -> x18, matrix products: 114 us -> 40.4 us  [the longest x14 24.5 us: tn(): lax.dot_general(left, right, (((0,), (0,)), ((), ())), preferred_element_...]
    pallas_call x0 -> x12, Pallas kernels: none -> 43.4 us  [the longest x1 16.6 us: cross_backward(): pl.pallas_call(functools.partial(cross_backward_kernel, blk_count, head_c...]
    dynamic_slice x16 -> x1, local copies, waits for them, and re-layouts: 43.7 us -> 0.58 us  [body(): lax.dynamic_slice_in_dim(passage_len, head_place * passages, passages)]
  transfers between devices with their start and end apart: 26 -> 88, of which waited for: 12 -> 26; matrix products, arithmetic and copies ran while one was open for 18% -> 21% of each run, Pallas kernels for 0% -> 9%
where the time goes in v1:
time: 465 us; the launch traced here: 458 us
  starting transfers between devices  119 us (26%)
  waiting for transfers between devices  116 us (25%)
  local copies, waits for them, and re-layouts  56.8 us (12%)
  Pallas kernels  43.4 us (9%)
  blocking collectives  41 us (9%)
  matrix products  40.4 us (9%)
  other arithmetic  26.1 us (6%)
  between operations  15.9 us (3%)
    ppermute x87, starting transfers between devices, partner(): return lax.ppermute(array, axis, [(i, i ^ by) for i in range(size)])  118 us
    ppermute x87, waiting for transfers between devices, partner(): return lax.ppermute(array, axis, [(i, i ^ by) for i in range(size)])  116 us
    psum x1, blocking collectives, body(): lax.psum(jnp.concatenate([gain_self_part, gain_cross_part, gain_ffn_part]...  41 us
    unnamed x182, local copies, waits for them, and re-layouts  34.3 us
    dot_general x14, matrix products, tn(): lax.dot_general(left, right, (((0,), (0,)), ((), ())), preferred_element_...  24.5 us
    pallas_call x1, Pallas kernels, cross_backward(): pl.pallas_call(functools.partial(cross_backward_kernel, blk_count, head_c...  16.6 us
    pallas_call x1, Pallas kernels, cross_forward(): pl.pallas_call(functools.partial(cross_forward_kernel, blk_count, head_co...  14.1 us
    pallas_call x10, Pallas kernels, call(): pl.pallas_call(kernel, out_shape=tuple(outs), in_specs=[smem()] * len(sca...  12.7 us
  transfers between devices with their start and end apart: 88, of which 26 were waited for; matrix products, arithmetic and copies ran while one was open for 21% of the time, Pallas kernels for 9%

profile of v1, /device:TPU:0, one launch (start us, length us, event | category | flops | bytes accessed | tf_op | source)
XLA Modules:
  0.0 458.0 jit_solution(1693081049062691493)
XLA Ops:
  26.9 15.2 %collective-permute-done.14 = bf16[192,768]{1,0:T(8,128)(2,1)} collective-permute-done((bf16[192,768]{1,0:T(8,128)(2,1)}, bf16[192,768]{1,0:T(8,128)(2,1)}, u32[]{:S(2)}, u32[]{:S(2)}) %collective-permute-start.14) | collective-permute-done | bytes 294944 | tf_op jit(solution)/shard_map/ppermute | solution.py:540
  64.6 8.4 %collective-permute-start = (bf16[128,192]{1,0:T(8,128)(2,1)S(1)}, bf16[128,192]{1,0:T(8,128)(2,1)S(1)}, u32[]{:S(2)}, u32[]{:S(2)}) collective-permute-start(bf16[128,192]{1,0:T(8,128)(2,1)S(1)} %get-tuple-element.72.refs_0_), channel_id=1, source_target_pairs={{0,1},{1,0},{2,3},{3,2},{4,5},{5,4},{6,7},{7,6},{8,9},{9,8},{10,11... | collective-permute-start | bytes 147464 | tf_op jit(solution)/shard_map/ppermute | solution.py:540
  79.3 4.5 collective-permute-done.28
  88.9 4.2 convolution_convert_fusion
  93.1 4.0 collective-permute-start.4
  103.7 4.8 %copy.40.refs_5_ = bf16[768,1920]{1,0:T(8,128)(2,1)} copy(bf16[768,1920]{0,1:T(8,128)(2,1)} %convolution_convert_fusion) | data formatting | bytes 5898240 | tf_op jit(solution)/shard_map/convert_element_type | solution.py:645
  117.3 4.1 fusion.refs_4_.refs_5_
  121.4 14.1 %shard_map.308 = (f32[32,896]{1,0:T(8,128)S(1)}, f32[32,896]{1,0:T(8,128)S(1)}, f32[32,896]{1,0:T(8,128)S(1)}, f32[32,896]{1,0:T(8,128)S(1)}, f32[32,896]{1,0:T(...) custom-call(s32[5]{0:T(128)S(1)} %dynamic-slice_xor_fusion.refs_0_, ...), custom_call_target="tpu_custom_call" | custom-call | tf_op jit(solution)/shard_map/pallas_call | solution.py:237
  145.9 5.6 %collective-permute-done.19.refs_2_ = f32[32,896]{1,0:T(8,128)S(1)} collective-permute-done((f32[32,896]{1,0:T(8,128)S(1)}, f32[32,896]{1,0:T(8,128)S(1)}, u32[]{:S(2)}, u32[]{:S(2)}) %collective-permute-start.19) | collective-permute-done | bytes 114720 | tf_op jit(solution)/shard_map/ppermute | solution.py:540
  152.2 4.7 %collective-permute-done.23.refs_6_ = f32[32,896]{1,0:T(8,128)S(1)} collective-permute-done((f32[32,896]{1,0:T(8,128)S(1)}, f32[32,896]{1,0:T(8,128)S(1)}, u32[]{:S(2)}, u32[]{:S(2)}) %collective-permute-start.23) | collective-permute-done | bytes 114720 | tf_op jit(solution)/shard_map/ppermute | solution.py:540
  187.1 8.8 %collective-permute-done.37.refs_2_ = f32[32,768]{1,0:T(8,128)S(1)} collective-permute-done((f32[32,768]{1,0:T(8,128)}, f32[32,768]{1,0:T(8,128)S(1)}, u32[]{:S(2)}, u32[]{:S(2)}) %collective-permute-start.37) | collective-permute-done | bytes 98336 | tf_op jit(solution)/shard_map/ppermute | solution.py:540
  222.7 16.6 %shard_map.313 = (f32[32,768]{1,0:T(8,128)}, f32[32,768]{1,0:T(8,128)}, f32[32,768]{1,0:T(8,128)}, f32[32,768]{1,0:T(8,128)}, f32[32,768]{1,0:T(8,128)}, /*index...) custom-call(s32[5]{0:T(128)} %copy-done.42, ...), custom_call_target="tpu_custom_call" | custom-call | tf_op jit(solution)/shard_map/pallas_call | solution.py:448
  239.3 3.8 collective-permute-start.46
  248.0 4.6 %convolution_convert_fusion.3 = bf16[768,768]{1,0:T(8,128)(2,1)S(1)} fusion(bf16[1920,768]{1,0:T(8,128)(2,1)} %get-tuple-element.113, bf16[1920,768]{1,0:T(8,128)(2,1)S(1)} %copy-done), kind=kOutput, calls=%fused_computation.10 | convolution fusion | flops 2265513984 | bytes 7077888 | tf_op jit(solution)/shard_map/dot_general | solution.py:31
  255.2 5.1 %convolution_add_fusion = f32[1920,768]{1,0:T(8,128)} fusion(f32[1920,768]{1,0:T(8,128)S(1)} %fusion.23, bf16[1920,768]{1,0:T(8,128)(2,1)S(1)} %copy-done.75, bf16[768,768]{1,0:T(8,128)(2,1)S(1)} %copy-done.63, bf16[768,768]{1,0:T(8,128)(2,1)S(1)} %copy-done.78, pred[]{:T(512)S(6)} %eq.4), kind=kOutput, calls=%fused_computation | convolution fusion | flops 2266988544 | bytes 17104896 | tf_op jit(solution)/shard_map/dot_general | solution.py:23
  260.3 4.1 broadcast_select_fusion
  280.9 4.3 collective-permute-done.54.refs_2_
  300.5 41.0 %psum.15 = f32[3,768]{1,0:T(4,128)S(1)} all-reduce(f32[3,768]{1,0:T(4,128)S(1)} %pad_maximum_fusion.11), channel_id=1, replica_groups=mesh['dp'=4,'blk'=2,'head'=4] {'dp','blk','head'}, use_global_device_ids=true, to_apply=%region_1.2 | all-reduce | flops 2304 | bytes 18432 | tf_op jit(solution)/shard_map/psum | solution.py:786
  364.1 14.2 %collective-permute-done.63 = bf16[256,576]{1,0:T(8,128)(2,1)S(1)} collective-permute-done((bf16[256,576]{1,0:T(8,128)(2,1)S(1)}, bf16[256,576]{1,0:T(8,128)(2,1)S(1)}, u32[]{:S(2)}, u32[]{:S(2)}) %collective-permute-start.63) | collective-permute-done | bytes 294944 | tf_op jit(solution)/shard_map/ppermute | solution.py:540
  384.0 5.6 %collective-permute-done.71 = bf16[256,960]{1,0:T(8,128)(2,1)} collective-permute-done((bf16[256,960]{1,0:T(8,128)(2,1)}, bf16[256,960]{1,0:T(8,128)(2,1)}, u32[]{:S(2)}, u32[]{:S(2)}) %collective-permute-start.71) | collective-permute-done | bytes 491552 | tf_op jit(solution)/shard_map/ppermute | solution.py:540
  402.6 3.5 collective-permute-done.77
  406.0 14.6 %collective-permute-done.76 = bf16[192,768]{1,0:T(8,128)(2,1)S(1)} collective-permute-done((bf16[192,768]{1,0:T(8,128)(2,1)S(1)}, bf16[192,768]{1,0:T(8,128)(2,1)S(1)}, u32[]{:S(2)}, u32[]{:S(2)}) %collective-permute-start.76) | collective-permute-done | bytes 294944 | tf_op jit(solution)/shard_map/ppermute | solution.py:540
  426.6 3.9 collective-permute-done.78
  434.1 5.5 %collective-permute-done.79 = bf16[192,768]{1,0:T(8,128)(2,1)S(1)} collective-permute-done((bf16[192,768]{1,0:T(8,128)(2,1)S(1)}, bf16[192,768]{1,0:T(8,128)(2,1)S(1)}, u32[]{:S(2)}, u32[]{:S(2)}) %collective-permute-start.79) | collective-permute-done | bytes 294944 | tf_op jit(solution)/shard_map/ppermute | solution.py:540
  (416 shorter events, 237.0 us)
Async XLA Ops:
  7.2 283.9 %all-reduce.2.cloned.1.call-start = ((), (), s32[]{:S(2)}) async-start(), calls=%async_computation | async-start | bytes 786432 | tf_op jit(solution)/shard_map/psum | solution.py:738
  9.3 38.0 %collective-permute-start.8 = (bf16[192,768]{1,0:T(8,128)(2,1)}, bf16[192,768]{1,0:T(8,128)(2,1)}, u32[]{:S(2)}, u32[]{:S(2)}) collective-permute-start(bf16[192,768]{1,0:T(8,128)(2,1)} %get-tuple-element.134), channel_id=1, source_target_pairs={{0,1},{1,0},{2,3},{3,2},{4,5},{5,4},{6,7},{7,6},{8,9},{9,8},{10,11... | collective-permute-start | bytes 884744 | tf_op jit(solution)/shard_map/ppermute | solution.py:540
  12.4 38.9 %collective-permute-start.9 = (bf16[192,768]{1,0:T(8,128)(2,1)}, bf16[192,768]{1,0:T(8,128)(2,1)}, u32[]{:S(2)}, u32[]{:S(2)}) collective-permute-start(bf16[192,768]{1,0:T(8,128)(2,1)} %get-tuple-element.134), channel_id=1, source_target_pairs={{0,3},{1,2},{2,1},{3,0},{4,7},{5,6},{6,5},{7,4},{8,11},{9,10},{10,... | collective-permute-start | bytes 884744 | tf_op jit(solution)/shard_map/ppermute | solution.py:540
  16.7 27.8 %collective-permute-start.13 = (bf16[192,768]{1,0:T(8,128)(2,1)}, bf16[192,768]{1,0:T(8,128)(2,1)}, u32[]{:S(2)}, u32[]{:S(2)}) collective-permute-start(bf16[192,768]{1,0:T(8,128)(2,1)} %get-tuple-element.132), channel_id=1, source_target_pairs={{0,1},{1,0},{2,3},{3,2},{4,5},{5,4},{6,7},{7,6},{8,9},{9,8},{10,11... | collective-permute-start | bytes 884744 | tf_op jit(solution)/shard_map/ppermute | solution.py:540
  18.3 42.0 %collective-permute-start.25 = (bf16[192,768]{1,0:T(8,128)(2,1)}, bf16[192,768]{1,0:T(8,128)(2,1)}, u32[]{:S(2)}, u32[]{:S(2)}) collective-permute-start(bf16[192,768]{1,0:T(8,128)(2,1)} %param.34), channel_id=1, source_target_pairs={{0,1},{1,0},{2,3},{3,2},{4,5},{5,4},{6,7},{7,6},{8,9},{9,8},{10,11... | collective-permute-start | bytes 884744 | tf_op jit(solution)/shard_map/ppermute | solution.py:540
  60.3 28.6 %collective-permute-start.17 = (bf16[768,768]{1,0:T(8,128)(2,1)}, bf16[768,768]{1,0:T(8,128)(2,1)S(1)}, u32[]{:S(2)}, u32[]{:S(2)}) collective-permute-start(bf16[768,768]{1,0:T(8,128)(2,1)} %constant_dynamic-update-slice_fusion.5), channel_id=1, source_target_pairs={{0,8},{8,0},{16,24},{24,16},{1,9},{9,1},{17,25},{25,17},{2,10},{10... | collective-permute-start | bytes 3538952 | tf_op jit(solution)/shard_map/ppermute | solution.py:540
  60.3 25.7 %collective-permute-start.65 = (bf16[256,1536]{1,0:T(8,128)(2,1)S(1)}, bf16[256,1536]{1,0:T(8,128)(2,1)S(1)}, u32[]{:S(2)}, u32[]{:S(2)}) collective-permute-start(bf16[256,1536]{1,0:T(8,128)(2,1)S(1)} %pad_maximum_fusion.6), channel_id=1, source_target_pairs={{0,16},{8,24},{16,0},{24,8},{1,17},{9,25},{17,1},{25,9},{2,18},{10... | collective-permute-start | bytes 2359304 | tf_op jit(solution)/shard_map/ppermute | solution.py:540
  88.9 52.2 %collective-permute-start.29 = (bf16[768,768]{1,0:T(8,128)(2,1)}, bf16[768,768]{1,0:T(8,128)(2,1)}, u32[]{:S(2)}, u32[]{:S(2)}) collective-permute-start(bf16[768,768]{1,0:T(8,128)(2,1)} %constant_dynamic-update-slice_fusion.10), channel_id=1, source_target_pairs={{0,8},{8,0},{16,24},{24,16},{1,9},{9,1},{17,25},{25,17},{2,10},{10... | collective-permute-start | bytes 3538952 | tf_op jit(solution)/shard_map/ppermute | solution.py:540
  166.5 45.9 %collective-permute-start.68 = (bf16[128,960]{1,0:T(8,128)(2,1)}, bf16[128,960]{1,0:T(8,128)(2,1)}, u32[]{:S(2)}, u32[]{:S(2)}) collective-permute-start(bf16[128,960]{1,0:T(8,128)(2,1)} %constant_dynamic-update-slice_fusion.20), channel_id=1, source_target_pairs={{0,4},{4,0},{1,5},{5,1},{2,6},{6,2},{3,7},{7,3},{8,12},{12,8},{9,1... | collective-permute-start | bytes 737288 | tf_op jit(solution)/shard_map/ppermute | solution.py:540
  166.5 39.6 %collective-permute-start.30 = (f32[32,768]{1,0:T(8,128)S(1)}, f32[32,768]{1,0:T(8,128)}, u32[]{:S(2)}, u32[]{:S(2)}) collective-permute-start(f32[32,768]{1,0:T(8,128)S(1)} %get-tuple-element.83.refs_0_.refs_4_), channel_id=1, source_target_pairs={{0,1},{1,0},{2,3},{3,2},{4,5},{5,4},{6,7},{7,6},{8,9},{9,8},{10,11... | collective-permute-start | bytes 294920 | tf_op jit(solution)/shard_map/ppermute | solution.py:540
  239.3 25.2 %collective-permute-start.46 = (f32[32,768]{1,0:T(8,128)}, f32[32,768]{1,0:T(8,128)S(1)}, u32[]{:S(2)}, u32[]{:S(2)}) collective-permute-start(f32[32,768]{1,0:T(8,128)} %get-tuple-element.97), channel_id=1, source_target_pairs={{0,1},{1,0},{2,3},{3,2},{4,5},{5,4},{6,7},{7,6},{8,9},{9,8},{10,11... | collective-permute-start | bytes 294920 | tf_op jit(solution)/shard_map/ppermute | solution.py:540
  243.8 25.8 %collective-permute-start.48 = (f32[32,768]{1,0:T(8,128)}, f32[32,768]{1,0:T(8,128)S(1)}, u32[]{:S(2)}, u32[]{:S(2)}) collective-permute-start(f32[32,768]{1,0:T(8,128)} %get-tuple-element.99), channel_id=1, source_target_pairs={{0,3},{1,2},{2,1},{3,0},{4,7},{5,6},{6,5},{7,4},{8,11},{9,10},{10,... | collective-permute-start | bytes 294920 | tf_op jit(solution)/shard_map/ppermute | solution.py:540
  245.5 25.4 %collective-permute-start.49 = (f32[32,768]{1,0:T(8,128)}, f32[32,768]{1,0:T(8,128)S(1)}, u32[]{:S(2)}, u32[]{:S(2)}) collective-permute-start(f32[32,768]{1,0:T(8,128)} %get-tuple-element.100), channel_id=1, source_target_pairs={{0,4},{1,5},{2,6},{3,7},{4,0},{5,1},{6,2},{7,3},{8,12},{9,13},{10,... | collective-permute-start | bytes 294920 | tf_op jit(solution)/shard_map/ppermute | solution.py:540
  269.5 90.3 %collective-permute-start.84 = (bf16[128,2304]{1,0:T(8,128)(2,1)}, bf16[128,2304]{1,0:T(8,128)(2,1)}, u32[]{:S(2)}, u32[]{:S(2)}) collective-permute-start(bf16[128,2304]{1,0:T(8,128)(2,1)} %constant_dynamic-update-slice_fusion.26), channel_id=1, source_target_pairs={{0,4},{4,0},{1,5},{5,1},{2,6},{6,2},{3,7},{7,3},{8,12},{12,8},{9,1... | collective-permute-start | bytes 1769480 | tf_op jit(solution)/shard_map/ppermute | solution.py:540
  270.9 71.8 %collective-permute-start.69 = (bf16[256,960]{1,0:T(8,128)(2,1)}, bf16[256,960]{1,0:T(8,128)(2,1)}, u32[]{:S(2)}, u32[]{:S(2)}) collective-permute-start(bf16[256,960]{1,0:T(8,128)(2,1)} %pad_maximum_fusion.7), channel_id=1, source_target_pairs={{0,16},{8,24},{16,0},{24,8},{1,17},{9,25},{17,1},{25,9},{2,18},{10... | collective-permute-start | bytes 1474568 | tf_op jit(solution)/shard_map/ppermute | solution.py:540
  296.2 95.8 %collective-permute-start.74 = (bf16[768,768]{1,0:T(8,128)(2,1)}, bf16[768,768]{1,0:T(8,128)(2,1)}, u32[]{:S(2)}, u32[]{:S(2)}) collective-permute-start(bf16[768,768]{1,0:T(8,128)(2,1)} %get-tuple-element.145), channel_id=1, source_target_pairs={{0,8},{8,0},{16,24},{24,16},{1,9},{9,1},{17,25},{25,17},{2,10},{10... | collective-permute-start | bytes 3538952 | tf_op jit(solution)/shard_map/ppermute | solution.py:540
  296.3 45.8 %collective-permute-start.62 = (bf16[128,576]{1,0:T(8,128)(2,1)S(1)}, bf16[128,576]{1,0:T(8,128)(2,1)S(1)}, u32[]{:S(2)}, u32[]{:S(2)}) collective-permute-start(bf16[128,576]{1,0:T(8,128)(2,1)S(1)} %get-tuple-element.118), channel_id=1, source_target_pairs={{0,4},{4,0},{1,5},{5,1},{2,6},{6,2},{3,7},{7,3},{8,12},{12,8},{9,1... | collective-permute-start | bytes 442376 | tf_op jit(solution)/shard_map/ppermute | solution.py:540
  299.4 59.5 %collective-permute-start.70 = (bf16[128,960]{1,0:T(8,128)(2,1)S(1)}, bf16[128,960]{1,0:T(8,128)(2,1)S(1)}, u32[]{:S(2)}, u32[]{:S(2)}) collective-permute-start(bf16[128,960]{1,0:T(8,128)(2,1)S(1)} %constant_dynamic-update-slice_fusion.22), channel_id=1, source_target_pairs={{0,4},{4,0},{1,5},{5,1},{2,6},{6,2},{3,7},{7,3},{8,12},{12,8},{9,1... | collective-permute-start | bytes 737288 | tf_op jit(solution)/shard_map/ppermute | solution.py:540
  347.2 48.6 %collective-permute-start.67 = (bf16[512,1536]{1,0:T(8,128)(2,1)}, bf16[512,1536]{1,0:T(8,128)(2,1)}, u32[]{:S(2)}, u32[]{:S(2)}) collective-permute-start(bf16[512,1536]{1,0:T(8,128)(2,1)} %pad_maximum_fusion.1), channel_id=1, source_target_pairs={{0,8},{8,0},{16,24},{24,16},{1,9},{9,1},{17,25},{25,17},{2,10},{10... | collective-permute-start | bytes 4718600 | tf_op jit(solution)/shard_map/ppermute | solution.py:540
  356.2 25.1 %collective-permute-start.82 = (bf16[256,960]{1,0:T(8,128)(2,1)}, bf16[256,960]{1,0:T(8,128)(2,1)}, u32[]{:S(2)}, u32[]{:S(2)}) collective-permute-start(bf16[256,960]{1,0:T(8,128)(2,1)} %pad_maximum_fusion.9), channel_id=1, source_target_pairs={{0,16},{8,24},{16,0},{24,8},{1,17},{9,25},{17,1},{25,9},{2,18},{10... | collective-permute-start | bytes 1474568 | tf_op jit(solution)/shard_map/ppermute | solution.py:540
  359.8 29.8 %collective-permute-start.71 = (bf16[256,960]{1,0:T(8,128)(2,1)}, bf16[256,960]{1,0:T(8,128)(2,1)}, u32[]{:S(2)}, u32[]{:S(2)}) collective-permute-start(bf16[256,960]{1,0:T(8,128)(2,1)} %pad_maximum_fusion.8), channel_id=1, source_target_pairs={{0,16},{8,24},{16,0},{24,8},{1,17},{9,25},{17,1},{25,9},{2,18},{10... | collective-permute-start | bytes 1474568 | tf_op jit(solution)/shard_map/ppermute | solution.py:540
  378.2 44.6 %collective-permute-start.85 = (bf16[256,2304]{1,0:T(8,128)(2,1)}, bf16[256,2304]{1,0:T(8,128)(2,1)}, u32[]{:S(2)}, u32[]{:S(2)}) collective-permute-start(bf16[256,2304]{1,0:T(8,128)(2,1)} %pad_maximum_fusion.2), channel_id=1, source_target_pairs={{0,16},{8,24},{16,0},{24,8},{1,17},{9,25},{17,1},{25,9},{2,18},{10... | collective-permute-start | bytes 3538952 | tf_op jit(solution)/shard_map/ppermute | solution.py:540
  389.6 35.3 %collective-permute-start.83 = (bf16[512,960]{0,1:T(8,128)(2,1)}, bf16[512,960]{0,1:T(8,128)(2,1)}, u32[]{:S(2)}, u32[]{:S(2)}) collective-permute-start(bf16[512,960]{0,1:T(8,128)(2,1)} %copy.44), channel_id=1, source_target_pairs={{0,8},{8,0},{16,24},{24,16},{1,9},{9,1},{17,25},{25,17},{2,10},{10... | collective-permute-start | bytes 2949128 | tf_op jit(solution)/shard_map/ppermute | solution.py:540
  406.0 27.7 %collective-permute-start.72 = (bf16[512,960]{0,1:T(8,128)(2,1)S(1)}, bf16[512,960]{0,1:T(8,128)(2,1)S(1)}, u32[]{:S(2)}, u32[]{:S(2)}) collective-permute-start(bf16[512,960]{0,1:T(8,128)(2,1)S(1)} %copy-done.58), channel_id=1, source_target_pairs={{0,8},{8,0},{16,24},{24,16},{1,9},{9,1},{17,25},{25,17},{2,10},{10... | collective-permute-start | bytes 2949128 | tf_op jit(solution)/shard_map/ppermute | solution.py:540
  (146 other events, 1743.7 us)
Sparse Core Ops, SparseCore 0:
  178.0 46.8 all-reduce.1

commit v2 on v1

v2 whole, which is shorter than its diff:
```python
import functools

import jax
import jax.numpy as jnp
from jax import lax
from jax.experimental import pallas as pl
from jax.experimental.pallas import tpu as pltpu
from jax.sharding import PartitionSpec as P

CFG = dict(
    s_w=0, s_p=1, s_c=1, s_y=0, t_cost=0.05,
    t_late="a2a", t_rsz="perm", t_agz="perm", t_latep=0, t_sh=1, t_shq=0, t_enc=0, t_broad=0,
    cost=1.0, w_k8=1, t_cs=1, m_early=0,
)
DHEAD = 64
LP = 384
LEAST = 3 * LP // 4
norm_epsilon = 1e-06
masked_score = -1e30
bf16 = jnp.bfloat16
f32 = jnp.float32
PAIR = 2 * DHEAD
STATS = 128
SECOND_LANE = 16
SPLIT_LANE = 32
VMEM_BYTES = 60 * 1024 * 1024


def nn(left, right):
    return lax.dot_general(left, right, (((1,), (0,)), ((), ())), preferred_element_type=f32)


def nt(left, right):
    return lax.dot_general(left, right, (((1,), (1,)), ((), ())), preferred_element_type=f32)


def tn(left, right):
    return lax.dot_general(left, right, (((0,), (0,)), ((), ())), preferred_element_type=f32)


def exact_nn(left, right):
    return lax.dot_general(
        left,
        right,
        (((1,), (0,)), ((), ())),
        precision=lax.Precision.HIGHEST,
        preferred_element_type=f32,
    )


def norm_scale(values):
    return lax.rsqrt(jnp.mean(values * values, axis=-1, keepdims=True) + norm_epsilon)


def normalize(values, gain):
    return values * norm_scale(values) * gain


def norm_back(upstream, values, gain):
    scale = norm_scale(values)
    unit = values * scale
    scaled = upstream * gain
    grad = scale * (scaled - unit * jnp.mean(scaled * unit, axis=-1, keepdims=True))
    return grad, jnp.sum(upstream * unit, axis=0, keepdims=True)


def cost(micros):
    return pl.CostEstimate(flops=0, bytes_accessed=int(micros * CFG["cost"] * 3e6), transcendentals=0)


def smem():
    return pl.BlockSpec(memory_space=pltpu.SMEM)


def shaped(shape, dtype):
    return jax.ShapeDtypeStruct(shape, dtype)


def whole(shape):
    return pl.BlockSpec(shape, lambda *_: (0,) * len(shape), pipeline_mode=pl.Buffered(1))


def call(kernel, outs, scalars, arrays, scratch=(), micros=3.5):
    return pl.pallas_call(
        kernel,
        grid=(1,),
        out_shape=tuple(outs),
        in_specs=[smem()] * len(scalars) + [whole(array.shape) for array in arrays],
        out_specs=tuple(whole(out.shape) for out in outs),
        scratch_shapes=list(scratch),
        cost_estimate=cost(micros),
        compiler_params=pltpu.CompilerParams(
            vmem_limit_bytes=VMEM_BYTES, dimension_semantics=("arbitrary",)
        ),
    )(*scalars, *arrays)


def my_head():
    return lax.axis_index("head")


def my_core():
    return lax.axis_index("dp") % 2


def my_blk():
    return lax.axis_index("blk")


def my_chip():
    return lax.axis_index("dp") // 2 * 2 + lax.axis_index("blk") % 2


def pack_stats(values):
    high = values.astype(bf16).astype(f32)
    middle = (values - high).astype(bf16).astype(f32)
    lowest = values - high - middle
    return (
        high + pltpu.roll(middle, SPLIT_LANE, 1) + pltpu.roll(lowest, 2 * SPLIT_LANE, 1)
    ).astype(bf16)


def unpack_stats(packed):
    packed = packed.astype(f32)
    return (
        packed
        + pltpu.roll(packed, STATS - SPLIT_LANE, 1)
        + pltpu.roll(packed, STATS - 2 * SPLIT_LANE, 1)
    )


def group_place(head_count, kb, kh):
    return (my_blk() ^ kb) * head_count + (my_head() ^ kh)


def rows_of(place, count):
    if isinstance(place, int):
        return slice(place * count, (place + 1) * count)
    return pl.ds(pl.multiple_of(place * count, count), count)


def head_blocks(width, head_count, shift):
    return [(j ^ shift) * width for j in range(head_count)]


def permuted(values, width, head_count, shift):
    if shift == 0:
        return values
    return jnp.concatenate(
        [values[:, o : o + width] for o in head_blocks(width, head_count, shift)], axis=1
    )


def self_probs(q, k, allowed):
    scores = jnp.where(allowed, nt(q, k), masked_score)
    raised = jnp.exp(scores - jnp.max(scores, axis=-1, keepdims=True))
    return raised / jnp.sum(raised, axis=-1, keepdims=True)


def causal(rows, length):
    at_q = lax.broadcasted_iota(jnp.int32, (rows, rows), 0)
    at_k = lax.broadcasted_iota(jnp.int32, (rows, rows), 1)
    return (at_k <= at_q) & (at_k.astype(f32) < length)


def self_kernel(dec_ref, len_ref, gain_ref, wq_ref, wk_ref, wv_ref, w_out_ref, *refs):
    normed_ref, qkv_ref, out_ref, *partials = refs[:-1]
    total = refs[-1]
    rows = normed_ref.shape[0]
    width = wq_ref.shape[0]
    normed = normalize(dec_ref[...].astype(f32), gain_ref[...].astype(f32)[None, :]).astype(bf16)
    normed_ref[...] = normed
    for i, weight in enumerate((wq_ref, wk_ref, wv_ref)):
        qkv_ref[:, i * width : (i + 1) * width] = nt(normed, weight[...]).astype(bf16)
    allowed = causal(rows, len_ref[0].astype(f32))
    outs = []
    for h in range(width // DHEAD):
        o = h * DHEAD
        probs = self_probs(
            qkv_ref[:, o : o + DHEAD], qkv_ref[:, width + o : width + o + DHEAD], allowed
        )
        outs.append(nn(probs.astype(bf16), qkv_ref[:, 2 * width + o : 2 * width + o + DHEAD]))
    attended = jnp.concatenate(outs, axis=1).astype(bf16)
    out_ref[...] = attended
    total[...] = nn(attended, w_out_ref[...])
    piece = rows // len(partials)
    for k, partial in enumerate(partials):
        partial[...] = total[rows_of(my_head() ^ k, piece), :]


def call_self(dec_in, dec_len, gain, w_query, w_key, w_value, w_out, head_count):
    rows, depth = dec_in.shape
    width = w_query.shape[0]
    arrays = (dec_in, dec_len, gain, w_query, w_key, w_value, w_out)
    outs = [
        shaped((rows, depth), bf16),
        shaped((rows, 3 * width), bf16),
        shaped((rows, width), bf16),
    ] + [shaped((rows // head_count, depth), f32)] * head_count
    return pl.pallas_call(
        self_kernel,
        grid=(1,),
        out_shape=tuple(outs),
        in_specs=[smem() if array is dec_len else whole(array.shape) for array in arrays],
        out_specs=tuple(whole(out.shape) for out in outs),
        scratch_shapes=[pltpu.VMEM((rows, depth), f32)],
        cost_estimate=cost(4),
        compiler_params=pltpu.CompilerParams(
            vmem_limit_bytes=VMEM_BYTES, dimension_semantics=("arbitrary",)
        ),
    )(*arrays)


def normed_kernel(count, *refs):
    chunks = refs[:count]
    dec_ref, gain_ref, first_ref, message_ref = refs[count:]
    piece = first_ref.shape[0]
    first = dec_ref[rows_of(my_head(), piece), :].astype(f32) + sum(chunk[...] for chunk in chunks)
    first_ref[...] = first
    normed = normalize(first, gain_ref[...].astype(f32)[None, :]).astype(bf16)
    for i in range(message_ref.shape[0]):
        message_ref[i] = normed


def fill_weights(target, owns, pieces):
    count = owns[0].shape[0]
    size = count // 4
    for i, own in enumerate(owns):
        target[i, :count, :] = own[...]
    others = len(pieces) // 4
    for place, piece in enumerate(pieces):
        kind = place // others
        quarter = (my_core() ^ kind // 2) * 2 + (my_blk() % 2 ^ kind % 2)
        start = (place % others + 1) * count + quarter * size
        for i in range(len(owns)):
            target[i, pl.ds(pl.multiple_of(start, size), size), :] = piece[
                i * size : (i + 1) * size, :
            ]


def piece_spec(pieces, part, of, whole_parts):
    rows, depth = pieces[0].shape
    block = (rows // whole_parts * of, depth)
    spec = pl.BlockSpec(block, lambda *_: (part, 0), pipeline_mode=pl.Buffered(1))
    return [spec] * len(pieces)


def query_kernel(blk_count, head_count, chunks_ref, c_query_ref, one_ref, self_ref, *refs):
    pieces, (early_ref, q_ref, full_ref, weights, normed) = refs[:-5], refs[-5:]
    rows, depth = one_ref.shape
    width = self_ref.shape[1]
    piece = rows // head_count
    fill_weights(weights, (c_query_ref,), pieces)
    full_ref[...] = weights[0]
    for kb in range(blk_count):
        for i in range(head_count):
            place = (my_blk() ^ kb) * head_count + i
            normed[i * piece : (i + 1) * piece, :] = chunks_ref[place]
        if kb == 0:
            early_ref[:, :depth] = one_ref[...]
            early_ref[:, depth : 2 * depth] = normed[...]
            early_ref[:, 2 * depth : 2 * depth + width] = self_ref[...]
            early_ref[:, 2 * depth + width :] = jnp.zeros(
                (rows, early_ref.shape[1] - 2 * depth - width), bf16
            )
        q_ref[kb] = nt(normed[...], weights[0]).astype(bf16)


def make_queries(chunks, c_query, normed_one, self_flat, pieces, blk_count, head_count):
    rows, depth = normed_one.shape
    width = self_flat.shape[1]
    outs = (
        shaped((rows, -(-(2 * depth + width) // 256) * 256), bf16),
        shaped((blk_count, rows, depth), bf16),
        shaped((depth, depth), bf16),
    )
    arrays = (chunks, c_query, normed_one, self_flat)
    return pl.pallas_call(
        functools.partial(query_kernel, blk_count, head_count),
        grid=(1,),
        out_shape=outs,
        in_specs=[whole(array.shape) for array in arrays] + piece_spec(pieces, 2, 1, 3),
        out_specs=tuple(whole(out.shape) for out in outs),
        scratch_shapes=[pltpu.VMEM((1, depth, depth), bf16), pltpu.VMEM((rows, depth), bf16)],
        cost_estimate=cost(4),
        compiler_params=pltpu.CompilerParams(
            vmem_limit_bytes=VMEM_BYTES, dimension_semantics=("arbitrary",)
        ),
    )(*arrays, *pieces)


def project_kernel(enc_ref, *refs):
    owns, pieces = refs[:2], refs[2:-5]
    key_ref, value_ref, key_full_ref, value_full_ref, weights = refs[-5:]

    @pl.when(pl.program_id(0) == 0)
    def _():
        fill_weights(weights, owns, pieces)
        key_full_ref[...] = weights[0]
        value_full_ref[...] = weights[1]

    key_ref[...] = nt(enc_ref[...], weights[0]).astype(bf16)
    value_ref[...] = nt(enc_ref[...], weights[1]).astype(bf16)


def project(enc, owns, pieces):
    slots, depth = enc.shape
    block = pl.BlockSpec((LP, depth), lambda p: (p, 0))
    full = shaped((depth, depth), bf16)
    return pl.pallas_call(
        project_kernel,
        grid=(slots // LP,),
        in_specs=[block] + [whole(w.shape) for w in owns] + piece_spec(pieces, 0, 2, 3),
        out_specs=(block, block, whole(full.shape), whole(full.shape)),
        out_shape=(shaped(enc.shape, bf16), shaped(enc.shape, bf16), full, full),
        scratch_shapes=[pltpu.VMEM((2, depth, depth), bf16)],
        cost_estimate=cost(9),
        compiler_params=pltpu.CompilerParams(
            vmem_limit_bytes=VMEM_BYTES, dimension_semantics=("arbitrary",)
        ),
    )(enc, *owns, *pieces)


def assemble_kernel(own_ref, *refs):
    out_ref = refs[-1]
    others = (len(refs) - 1) // 2
    count = own_ref.shape[0]
    half = count // 2
    out_ref[:count, :] = own_ref[...]
    for k in range(others):
        start = (k + 1) * count
        out_ref[rows_of(start // half + my_core(), half), :] = refs[k][...]
        out_ref[rows_of(start // half + 1 - my_core(), half), :] = refs[others + k][...]


def spread_pairs(values, target, kb):
    rows = values.shape[0]
    for j in range(values.shape[1] // PAIR):
        pair = values[:, j * PAIR : (j + 1) * PAIR]
        lane = lax.broadcasted_iota(jnp.int32, pair.shape, 1)
        zero = jnp.zeros_like(pair)
        target[kb, j, 0:rows, :] = jnp.where(lane < DHEAD, pair, zero)
        target[kb, j, rows : 2 * rows, :] = jnp.where(lane < DHEAD, zero, pair)


def within(values, length, fill):
    place = LEAST + lax.broadcasted_iota(jnp.int32, (LP - LEAST, values.shape[1]), 0)
    last = jnp.where(place < length, values[LEAST:], fill)
    return jnp.concatenate([values[:LEAST], last], axis=0)


def pair_columns(j):
    return slice(j * PAIR, (j + 1) * PAIR)


def add_pair(target, slot, j, update, factor=None):
    rows = target.shape[2]
    for i in range(2):
        span = slice(j * PAIR + i * DHEAD, j * PAIR + (i + 1) * DHEAD)
        own = update[i * DHEAD : (i + 1) * DHEAD, i * rows : (i + 1) * rows]
        old = target[slot, span, :]
        if factor is not None:
            old = old * factor[:, i * rows : (i + 1) * rows]
        target[slot, span, :] = old + own


def cross_forward_kernel(blk_count, head_count, width, *refs):
    slot_ref, len_ref, q_ref, k_ref, v_ref = refs[:5]
    out_ref, q2, acc, highest, totals, stat, flat, flat_stat, held, probs, factors = refs[5:]
    rows, depth = q_ref.shape[1], q_ref.shape[2]
    pairs = depth // PAIR
    step = pl.program_id(0)

    @pl.when(step == 0)
    def _():
        for kb in range(blk_count):
            spread_pairs(q_ref[kb], q2, kb)
        highest[...] = jnp.full(highest.shape, masked_score, f32)
        totals[...] = jnp.zeros(totals.shape, f32)
        acc[...] = jnp.zeros(acc.shape, f32)

    slot = slot_ref[step]
    for j in range(pairs):
        scores = within(nt(k_ref[:, pair_columns(j)], q2[slot, j]), len_ref[step], masked_score)
        held[j] = scores
        before = highest[slot, j : j + 1, :]
        newest = jnp.maximum(before, jnp.max(scores, axis=0, keepdims=True))
        factors[j : j + 1, :] = jnp.exp(before - newest)
        highest[slot, j : j + 1, :] = newest
    for j in range(pairs):
        raised = jnp.exp(held[j] - highest[slot, j : j + 1, :])
        probs[j] = raised.astype(bf16)
        totals[slot, j : j + 1, :] = totals[slot, j : j + 1, :] * factors[
            j : j + 1, :
        ] + jnp.sum(raised, axis=0, keepdims=True)
    for j in range(pairs):
        update = tn(v_ref[:, pair_columns(j)], probs[j])
        add_pair(acc, slot, j, update, factors[j : j + 1, :])

    @pl.when(step == pl.num_programs(0) - 1)
    def _():
        stat[...] = jnp.zeros(stat.shape, f32)
        piece = rows // head_count
        per = width // DHEAD
        for kb in range(blk_count):
            flat[...] = acc[kb].T
            for kh in range(head_count):
                for head in range(depth // DHEAD):
                    at = ((head // per) ^ kh) * per + head % per
                    lanes = slice((head % 2) * rows, (head % 2 + 1) * rows)
                    stat[at : at + 1, :] = highest[kb, head // 2 : head // 2 + 1, lanes]
                    stat[SECOND_LANE + at : SECOND_LANE + at + 1, :] = totals[
                        kb, head // 2 : head // 2 + 1, lanes
                    ]
                flat_stat[...] = stat[...].T
                mine = rows_of(my_head() ^ kh, piece)
                place = group_place(head_count, kb, kh)
                out_ref[place, :, :depth] = permuted(
                    flat[mine, :].astype(bf16), width, head_count, kh
                )
                out_ref[place, :, depth:] = pack_stats(flat_stat[mine, :])


def cross_forward(slots, lengths, queries, keys, values, head_count, width):
    blk_count, rows, depth = queries.shape
    passages = slots.shape[0]
    piece = rows // head_count
    chunk_count = blk_count * head_count
    pairs = depth // PAIR
    grid = pltpu.PrefetchScalarGridSpec(
        num_scalar_prefetch=2,
        grid=(passages,),
        in_specs=[
            whole((blk_count, rows, depth)),
            pl.BlockSpec((LP, depth), lambda p, *_: (p, 0)),
            pl.BlockSpec((LP, depth), lambda p, *_: (p, 0)),
        ],
        out_specs=whole((chunk_count, piece, depth + STATS)),
        scratch_shapes=[
            pltpu.VMEM((blk_count, pairs, 2 * rows, PAIR), bf16),
            pltpu.VMEM((blk_count, depth, rows), f32),
            pltpu.VMEM((blk_count, 8, 2 * rows), f32),
            pltpu.VMEM((blk_count, 8, 2 * rows), f32),
            pltpu.VMEM((STATS, rows), f32),
            pltpu.VMEM((rows, depth), f32),
            pltpu.VMEM((rows, STATS), f32),
            pltpu.VMEM((pairs, LP, 2 * rows), f32),
            pltpu.VMEM((pairs, LP, 2 * rows), bf16),
            pltpu.VMEM((8, 2 * rows), f32),
        ],
    )
    return pl.pallas_call(
        functools.partial(cross_forward_kernel, blk_count, head_count, width),
        out_shape=shaped((chunk_count, piece, depth + STATS), bf16),
        cost_estimate=cost(15),
        grid_spec=grid,
        compiler_params=pltpu.CompilerParams(
            vmem_limit_bytes=VMEM_BYTES, dimension_semantics=("arbitrary",)
        ),
    )(slots, lengths, queries, keys, values)


def head_matrix(depth):
    head = lax.broadcasted_iota(jnp.int32, (STATS, depth), 0)
    column = lax.broadcasted_iota(jnp.int32, (STATS, depth), 1)
    return (head == column // DHEAD).astype(f32)


def combine_kernel(width, *refs):
    chunks, first_ref, c_out_ref, gain_ref, cross_ref, second_ref, logsum_ref = refs[:7]
    messages = refs[7:]
    piece, depth = cross_ref.shape
    stats = [unpack_stats(chunks[i, :, depth:]) for i in range(chunks.shape[0])]
    highest = stats[0]
    for other in stats[1:]:
        highest = jnp.maximum(highest, other)
    lane = lax.broadcasted_iota(jnp.int32, (piece, STATS), 1)
    real = lane < depth // DHEAD
    weights = [jnp.where(real, jnp.exp(one - highest), 0.0) for one in stats]
    total = sum(w * pltpu.roll(one, STATS - SECOND_LANE, 1) for w, one in zip(weights, stats))
    total = jnp.where(real, total, 1.0)
    logsum_ref[...] = jnp.where(real, highest + jnp.log(total), 0.0)
    spread = head_matrix(depth)
    weighted = exact_nn(jnp.concatenate(weights, axis=0), spread)
    cross = sum(
        chunks[i, :, :depth].astype(f32) * weighted[i * piece : (i + 1) * piece]
        for i in range(chunks.shape[0])
    )
    cross = cross / exact_nn(total, spread)
    cross_ref[...] = cross
    rounded = cross.astype(bf16)
    second = first_ref[...] + nn(rounded, c_out_ref[...])
    second_ref[...] = second
    normed = normalize(second, gain_ref[...].astype(f32)[None, :]).astype(bf16)
    for k, message in enumerate(messages):
        message[:, :depth] = normed
        message[:, depth:] = rounded[:, k * width : (k + 1) * width]


def ffn_kernel(count, *refs):
    chunks = refs[:count]
    cot_ref, w_in_ref, w_back_ref = refs[count : count + 3]
    grads = refs[count + 3 : 2 * count + 3]
    layer_ref, wide_ref, cols_ref, total = refs[2 * count + 3 :]
    piece, depth = grads[0].shape
    for k, chunk in enumerate(chunks):
        mine = rows_of(my_head() ^ k, piece)
        wide_ref[mine, :depth] = chunk[:, :depth]
        cols_ref[mine, :] = chunk[:, depth:]
    units = w_in_ref.shape[1]
    before = nn(wide_ref[:, :depth], w_in_ref[...])
    root = 0.7978845608028654
    cube = 0.044715
    square = before * before
    bend = jnp.tanh(root * (before + cube * before * square))
    hidden = (0.5 * before * (1.0 + bend)).astype(bf16)
    slope = 0.5 * (1.0 + bend) + 0.5 * before * (1.0 - bend * bend) * root * (
        1.0 + 3.0 * cube * square
    )
    pre_grad = (nt(cot_ref[...], w_back_ref[...]) * slope).astype(bf16)
    total[...] = nt(pre_grad, w_in_ref[...])
    wide_ref[:, depth : depth + units] = hidden
    wide_ref[:, depth + units : depth + 2 * units] = pre_grad
    wide_ref[:, depth + 2 * units :] = cot_ref[...]
    for k, grad in enumerate(grads):
        grad[...] = total[rows_of(my_head() ^ k, piece), :]
    total[...] = nn(hidden, w_back_ref[...])
    for i in range(count):
        layer_ref[i] = total[i * piece : (i + 1) * piece, :]


def branch_kernel(head_count, width, *refs):
    chunks = refs[:head_count]
    second_ref, gain_ref, cot_ref, c_out_ref, cross_ref, logsum_ref = refs[
        head_count : head_count + 6
    ]
    grad_ref, gain_grad_ref, message_ref = refs[head_count + 6 :]
    piece, depth = second_ref.shape
    upstream = sum(chunk[...] for chunk in chunks)
    grad, gain_grad_ref[...] = norm_back(upstream, second_ref[...], gain_ref[...].astype(f32)[None, :])
    grad = cot_ref[rows_of(my_head(), piece), :].astype(f32) + grad
    grad_ref[...] = grad
    branch = grad.astype(bf16)
    grad_cross = nt(branch, c_out_ref[...]).astype(bf16).astype(f32)
    spread = head_matrix(depth)
    deltas = lax.dot_general(
        grad_cross * cross_ref[...],
        spread,
        (((1,), (1,)), ((), ())),
        precision=lax.Precision.HIGHEST,
        preferred_element_type=f32,
    )
    stats = logsum_ref[...] + pltpu.roll(deltas, SECOND_LANE, 1)
    per = width // DHEAD
    heads = depth // DHEAD
    source = lax.broadcasted_iota(jnp.int32, (STATS, STATS), 0)
    target = lax.broadcasted_iota(jnp.int32, (STATS, STATS), 1)
    place = source % SECOND_LANE
    for k in range(head_count):
        moved = (source - place) + ((place // per) ^ k) * per + place % per
        shuffle = ((target == moved) & (place < heads) & (source < 2 * SECOND_LANE)).astype(f32)
        aligned = exact_nn(stats, shuffle)
        packed = pack_stats(aligned)
        for kb in range(message_ref.shape[0] // head_count):
            entry = group_place(head_count, kb, k)
            message_ref[entry, :, :depth] = branch
            message_ref[entry, :, depth:] = packed


def cross_backward_kernel(blk_count, head_count, width, *refs):
    slot_ref, len_ref, q_ref, c_out_ref, k_ref, v_ref = refs[:6]
    chunks, out_ref, branch_ref, grad_k_ref, grad_v_ref = refs[6:11]
    q2, g2, stats, branch, flat_stat, grad_q, flat = refs[11:18]
    held, grad_probs, probs, grad_scores = refs[18:]
    rows, depth = q_ref.shape[1], q_ref.shape[2]
    pairs = depth // PAIR
    piece = rows // head_count
    step = pl.program_id(0)

    @pl.when(step == 0)
    def _():
        for kb in range(blk_count):
            for i in range(head_count):
                place = (my_blk() ^ kb) * head_count + i
                span = slice(i * piece, (i + 1) * piece)
                branch[span, :] = chunks[place, :, :depth]
                flat_stat[span, :] = unpack_stats(chunks[place, :, depth:])
            if kb == 0:
                branch_ref[...] = branch[...]
            stats[kb] = flat_stat[...].T
            spread_pairs(q_ref[kb], q2, kb)
            spread_pairs(nt(branch[...], c_out_ref[...]).astype(bf16), g2, kb)
        grad_q[...] = jnp.zeros(grad_q.shape, f32)

    slot = slot_ref[step]

    def both_heads(first):
        return jnp.concatenate(
            [stats[slot, first : first + 1, :], stats[slot, first + 1 : first + 2, :]], axis=1
        )

    for j in range(pairs):
        held[j] = nt(k_ref[:, pair_columns(j)], q2[slot, j])
        grad_probs[j] = nt(v_ref[:, pair_columns(j)], g2[slot, j])
    for j in range(pairs):
        raised = within(jnp.exp(held[j] - both_heads(2 * j)), len_ref[step], 0.0)
        probs[j] = raised.astype(bf16)
        grad_scores[j] = (raised * (grad_probs[j] - both_heads(SECOND_LANE + 2 * j))).astype(bf16)
    for j in range(pairs):
        grad_v_ref[:, pair_columns(j)] = nn(probs[j], g2[slot, j]).astype(bf16)
        grad_k_ref[:, pair_columns(j)] = nn(grad_scores[j], q2[slot, j]).astype(bf16)
        add_pair(grad_q, slot, j, tn(k_ref[:, pair_columns(j)], grad_scores[j]))

    @pl.when(step == pl.num_programs(0) - 1)
    def _():
        for kb in range(blk_count):
            flat[...] = grad_q[kb].T
            for kh in range(head_count):
                mine = rows_of(my_head() ^ kh, piece)
                out_ref[group_place(head_count, kb, kh)] = permuted(
                    flat[mine, :].astype(bf16), width, head_count, kh
                )


def cross_backward(slots, lengths, queries, c_out, keys, values, chunks, head_count, width):
    blk_count, rows, depth = queries.shape
    passages = slots.shape[0]
    piece = rows // head_count
    chunk_count = blk_count * head_count
    pairs = depth // PAIR
    passage = pl.BlockSpec((LP, depth), lambda p, *_: (p, 0))
    grid = pltpu.PrefetchScalarGridSpec(
        num_scalar_prefetch=2,
        grid=(passages,),
        in_specs=[
            whole((blk_count, rows, depth)),
            whole((depth, depth)),
            passage,
            passage,
            whole(chunks.shape),
        ],
        out_specs=(
            whole((chunk_count, piece, depth)),
            whole((rows, depth)),
            passage,
            passage,
        ),
        scratch_shapes=[
            pltpu.VMEM((blk_count, pairs, 2 * rows, PAIR), bf16),
            pltpu.VMEM((blk_count, pairs, 2 * rows, PAIR), bf16),
            pltpu.VMEM((blk_count, STATS, rows), f32),
            pltpu.VMEM((rows, depth), bf16),
            pltpu.VMEM((rows, STATS), f32),
            pltpu.VMEM((blk_count, depth, rows), f32),
            pltpu.VMEM((rows, depth), f32),
            pltpu.VMEM((pairs, LP, 2 * rows), f32),
            pltpu.VMEM((pairs, LP, 2 * rows), f32),
            pltpu.VMEM((pairs, LP, 2 * rows), bf16),
            pltpu.VMEM((pairs, LP, 2 * rows), bf16),
        ],
    )
    return pl.pallas_call(
        functools.partial(cross_backward_kernel, blk_count, head_count, width),
        out_shape=(
            shaped((chunk_count, piece, depth), bf16),
            shaped((rows, depth), bf16),
            shaped(keys.shape, bf16),
            shaped(keys.shape, bf16),
        ),
        cost_estimate=cost(16),
        grid_spec=grid,
        compiler_params=pltpu.CompilerParams(
            vmem_limit_bytes=VMEM_BYTES, dimension_semantics=("arbitrary",)
        ),
    )(slots, lengths, queries, c_out, keys, values, chunks)


def first_kernel(count, *refs):
    chunks, first_ref, gain_ref, c_query_ref, second_grad_ref, second_ref = refs[:6]
    layer_ref, grad_ref, gain_grad_ref = refs[6:9]
    messages = refs[9:]
    piece, depth = grad_ref.shape
    width = messages[0].shape[1] - 2 * depth
    layer = (second_ref[...] + sum(layer_ref[i] for i in range(count))).astype(bf16)
    grad_q = sum(chunks[i].astype(f32) for i in range(chunks.shape[0])).astype(bf16)
    upstream = nn(grad_q, c_query_ref[...])
    grad, gain_grad_ref[...] = norm_back(upstream, first_ref[...], gain_ref[...].astype(f32)[None, :])
    grad = second_grad_ref[...] + grad
    grad_ref[...] = grad
    branch = grad.astype(bf16)
    for k, message in enumerate(messages):
        message[:, :depth] = branch
        message[:, depth : depth + width] = grad_q[:, k * width : (k + 1) * width]
        message[:, depth + width :] = layer


def self_back_kernel(count, len_ref, *refs):
    chunks = refs[:count]
    w_out_ref, qkv_ref, wq_ref, wk_ref, wv_ref = refs[count : count + 5]
    grads, (sides_ref, layer_ref, total, side_ref) = refs[count + 5 : -4], refs[-4:]
    width, depth = wq_ref.shape
    rows = side_ref.shape[0]
    piece = rows // count
    start = depth + width
    for k, chunk in enumerate(chunks):
        mine = rows_of(my_head() ^ k, piece)
        side_ref[mine, :start] = chunk[:, :start]
        layer_ref[mine, :] = chunk[:, start:]
    grad_self = nt(side_ref[:, :depth], w_out_ref[...]).astype(bf16)
    allowed = causal(rows, len_ref[0].astype(f32))
    grad_q, grad_k, grad_v = [], [], []
    for h in range(width // DHEAD):
        o = h * DHEAD
        q = qkv_ref[:, o : o + DHEAD]
        k = qkv_ref[:, width + o : width + o + DHEAD]
        v = qkv_ref[:, 2 * width + o : 2 * width + o + DHEAD]
        g = grad_self[:, o : o + DHEAD]
        probs = self_probs(q, k, allowed)
        grad_probs = nt(g, v)
        delta = jnp.sum(probs * grad_probs, axis=-1, keepdims=True)
        grad_scores = (probs * (grad_probs - delta)).astype(bf16)
        grad_q.append(nn(grad_scores, k))
        grad_k.append(tn(grad_scores, q))
        grad_v.append(tn(probs.astype(bf16), g))
    flat = [jnp.concatenate(parts, axis=1).astype(bf16) for parts in (grad_q, grad_k, grad_v)]
    for i, part in enumerate(flat):
        side_ref[:, start + i * width : start + (i + 1) * width] = part
    total[...] = nn(flat[0], wq_ref[...]) + nn(flat[1], wk_ref[...]) + nn(flat[2], wv_ref[...])
    if len(grads) == 1:
        for i in range(count):
            grads[0][i] = total[i * piece : (i + 1) * piece, :]
    else:
        for k, grad in enumerate(grads):
            grad[...] = total[rows_of(my_head() ^ k, piece), :]
    for i in range(sides_ref.shape[0]):
        sides_ref[i] = side_ref[...]


def input_kernel(count, *refs):
    chunks = refs[:count]
    dec_ref, gain_ref, first_grad_ref, cross_gain_ref, ffn_gain_ref, message_ref = refs[count:]
    if count == 1:
        chunks = [chunks[0].at[i] for i in range(chunks[0].shape[0])]
    piece, depth = chunks[0].shape
    upstream = sum(chunk[...] for chunk in chunks)
    values = dec_ref[rows_of(my_head(), piece), :].astype(f32)
    grad, self_gain = norm_back(upstream, values, gain_ref[...].astype(f32)[None, :])
    grad = first_grad_ref[...] + grad
    for i in range(message_ref.shape[0]):
        message_ref[i, :piece, :] = grad
        message_ref[i, piece:, :] = jnp.zeros((message_ref.shape[1] - piece, depth), f32)
        message_ref[i, piece : piece + 1, :] = self_gain
        message_ref[i, piece + 1 : piece + 2, :] = cross_gain_ref[...]
        message_ref[i, piece + 2 : piece + 3, :] = ffn_gain_ref[...]


def place_kernel(count, *refs):
    chunks, (out_ref, gain_ref) = refs[:-2], refs[-2:]
    piece = out_ref.shape[0] // count
    if len(chunks) == 1:
        chunks = [chunks[0].at[i] for i in range(count)]
        places = range(count)
    else:
        places = [my_head() ^ k for k in range(count)]
    for place, chunk in zip(places, chunks):
        out_ref[rows_of(place, piece), :] = chunk[:piece, :]
    gain_ref[...] = sum(chunk[piece:, :] for chunk in chunks)


def weight_kernel(early_count, late_count, width, *refs):
    early, late = refs[:early_count], refs[early_count : early_count + late_count]
    wq_ref, wk_ref, wv_ref, out_ref, query_ref, normed, side = refs[early_count + late_count :]
    depth = wq_ref.shape[1]
    stack_up(early, normed)
    stack_up(late, side)
    start = depth + width
    qkv = tn(side[:, start:], normed[:, :depth])
    for i, target in enumerate((wq_ref, wk_ref, wv_ref)):
        target[...] = qkv[i * width : (i + 1) * width]
    query_ref[...] = tn(side[:, depth:start], normed[:, depth : 2 * depth])
    out_ref[...] = tn(normed[:, 2 * depth : 2 * depth + width], side[:, :depth])


def stack_up(parts, target):
    start = 0
    if len(parts) == 1 and len(parts[0].shape) == 3:
        place = lax.axis_index("dp")
        entries = [(place ^ k) * 2 + (my_blk() ^ b) for k in (0, 2, 1, 3) for b in (0, 1)]
        rows = parts[0].shape[1]
        for i, entry in enumerate(entries):
            target[i * rows : (i + 1) * rows, :] = parts[0][entry]
        return
    for part in parts:
        target[start : start + part.shape[0], :] = part[...]
        start += part.shape[0]


def wide_kernel(count, *refs):
    in_ref, back_ref, stack = refs[count:]
    depth, units = in_ref.shape
    stack_up(refs[:count], stack)
    in_ref[...] = tn(stack[:, :depth], stack[:, depth + units : depth + 2 * units])
    back_ref[...] = tn(stack[:, depth : depth + units], stack[:, depth + 2 * units :])


def projection_grad_kernel(head_count, plane, *refs):
    keys_ref, values_ref, enc_ref, cols_ref, branch_ref, out_ref, total = refs
    step = pl.program_id(0)
    count, depth = total.shape
    width = cols_ref.shape[1]
    blocks = count // width

    @pl.when(step == 0)
    def _():
        cross = tn(cols_ref[...], branch_ref[...]).astype(bf16)
        if len(out_ref.shape) == 2:
            out_ref[2 * depth :, :] = cross
        else:
            size = width // plane
            for device in range(plane):
                start = depth // 4
                out_ref[device, start : start + size, :] = cross[device * size : (device + 1) * size]

    for weight, grad_ref in enumerate((keys_ref, values_ref)):
        total[...] = tn(grad_ref[...], enc_ref[...])
        if len(out_ref.shape) == 2:
            start = pl.multiple_of(weight * depth + step * count, 16)
            out_ref[pl.ds(start, count), :] = total[...].astype(bf16)
            continue
        size = width // 4
        for block in range(blocks):
            place = pl.multiple_of((step * blocks + block) * size, 16)
            for part in range(4):
                start = block * width + part * size
                device = (part // 2 * 2 + weight) * 2 + part % 2
                out_ref[device, pl.ds(place, size), :] = total[start : start + size, :].astype(bf16)


def projection_grads(key_grads, value_grads, enc, cross_cols, branch, plane, head_count):
    slots, depth = enc.shape
    width = cross_cols.shape[1]
    steps = 2
    block = pl.BlockSpec((slots, depth // steps), lambda j: (0, j))
    if plane == 8:
        out = shaped((plane, -(-(depth // 4 + width // plane) // 16) * 16, depth), bf16)
    else:
        out = shaped((2 * depth + width, depth), bf16)
    return pl.pallas_call(
        functools.partial(projection_grad_kernel, head_count, plane),
        grid=(steps,),
        in_specs=[block, block, whole(enc.shape), whole(cross_cols.shape), whole(branch.shape)],
        out_specs=whole(out.shape),
        out_shape=out,
        scratch_shapes=[pltpu.VMEM((depth // steps, depth), f32)],
        cost_estimate=cost(4),
        compiler_params=pltpu.CompilerParams(
            vmem_limit_bytes=VMEM_BYTES, dimension_semantics=("arbitrary",)
        ),
    )(key_grads, value_grads, enc, cross_cols, branch)


def encoder_grad_kernel(keys_ref, values_ref, key_ref, value_ref, out_ref):
    out_ref[...] = nn(keys_ref[...], key_ref[...]) + nn(values_ref[...], value_ref[...])


def encoder_grads(key_grads, value_grads, key_full, value_full):
    slots, depth = key_grads.shape
    block = pl.BlockSpec((LP, depth), lambda p: (p, 0))
    return pl.pallas_call(
        encoder_grad_kernel,
        grid=(slots // LP,),
        in_specs=[block, block, whole(key_full.shape), whole(value_full.shape)],
        out_specs=block,
        out_shape=shaped((slots, depth), f32),
        cost_estimate=cost(7 * CFG["t_cost"]),
        compiler_params=pltpu.CompilerParams(
            vmem_limit_bytes=VMEM_BYTES, dimension_semantics=("arbitrary",)
        ),
    )(key_grads, value_grads, key_full, value_full)


def share_kernel(shares_ref, blocks_ref, cross_ref):
    count, size = blocks_ref.shape[:2]
    total = sum(shares_ref[i].astype(f32) for i in range(shares_ref.shape[0]))
    for k in range(count):
        blocks_ref[my_head() ^ k] = total[k * size : (k + 1) * size].astype(bf16)
    cross_ref[...] = total[count * size : count * size + cross_ref.shape[0]].astype(bf16)


def spread_kernel(blocks_ref, cross_ref, gains_ref, out_ref):
    size, more = blocks_ref.shape[1], cross_ref.shape[0]
    block = sum(blocks_ref[i].astype(f32) for i in range(blocks_ref.shape[0])).astype(bf16)
    pieces = []
    for i in range(3):
        rest = gains_ref[i : i + 1, :]
        for step in range(3):
            pieces.append(rest.astype(bf16).astype(f32))
            rest = rest - pieces[-1]
    fill = out_ref.shape[1] - size - more - len(pieces)
    pieces.append(jnp.zeros((fill, out_ref.shape[2]), f32))
    tail = jnp.concatenate([cross_ref[...].astype(f32), *pieces], axis=0).astype(bf16)
    for device in range(out_ref.shape[0]):
        out_ref[device, :size, :] = block
        out_ref[device, size:, :] = tail


def collect_kernel(shares_ref, key_ref, value_ref, cross_ref, gains_ref):
    plane = shares_ref.shape[0]
    size = key_ref.shape[0] // 4
    more = cross_ref.shape[0] // plane
    total = 0.0
    for device in range(plane):
        place, blk = device // 2, device % 2
        target = value_ref if place % 2 else key_ref
        part = place // 2 * 2 + blk
        share = shares_ref[device].astype(f32)
        target[part * size : (part + 1) * size, :] = share[:size]
        cross_ref[device * more : (device + 1) * more, :] = share[size : size + more]
        total = total + share[size + more :]
    for i in range(3):
        gains_ref[i : i + 1, :] = jnp.sum(total[3 * i : 3 * i + 3, :], axis=0, keepdims=True)
    gains_ref[3:, :] = jnp.zeros((gains_ref.shape[0] - 3, gains_ref.shape[1]), f32)


def after(array, *others):
    return lax.optimization_barrier((array, *others))[0]


def hold(arrays, *others):
    arrays = tuple(arrays)
    return list(lax.optimization_barrier((*arrays, *others))[: len(arrays)])


def partner(array, axis, by):
    size = lax.axis_size(axis)
    return lax.ppermute(array, axis, [(i, i ^ by) for i in range(size)])


def hold_lists(one, two):
    together = hold([*one, *two])
    return together[: len(one)], together[len(one) :]


def exchange(array, *axes):
    return lax.all_to_all(array, axes, 0, 0)


def swap_parts(parts):
    return [parts[0]] + [partner(parts[k], "head", k) for k in range(1, len(parts))]


def share_heads(array):
    return [array] + [partner(array, "head", k) for k in range(1, lax.axis_size("head"))]


def across_core(parts):
    return [partner(part, "dp", 1) for part in parts]


def to_chip(array, k):
    axis, by = [("blk", 1), ("dp", 2), (("dp", "blk"), 5)][k - 1]
    return partner(array, axis, by)


def plane_gather(array):
    chips = [array] + [to_chip(array, k) for k in (1, 2, 3)]
    return chips + across_core(chips)


def plane_gather_wide(array, beside, small):
    if not small:
        return [array]
    both = jnp.concatenate([array, beside], axis=0)
    far = partner(both, "dp", 2)
    return [both, far]


def body(
    dec_in,
    enc_out,
    passage_len,
    dec_len,
    passage_owner,
    gain_self,
    gain_cross,
    gain_ffn,
    w_query,
    w_key,
    w_value,
    w_out,
    c_query,
    c_key,
    c_value,
    c_out,
    w_in,
    w_back,
    cotangent,
):
    blk_count = lax.axis_size("blk")
    dp_count = lax.axis_size("dp")
    head_count = lax.axis_size("head")
    small = blk_count == 2 and dp_count == 4
    chunk_count = blk_count * head_count
    plane = dp_count * blk_count
    width, depth = w_query.shape
    units = w_in.shape[1]
    rows = dec_in.shape[0]
    piece = rows // head_count
    passages = enc_out.shape[0] // LP
    head_place = lax.axis_index("head")
    blk_place = lax.axis_index("blk")
    core = lax.axis_index("dp") % 2
    gain_one, gain_two, gain_three = gain_self, gain_cross, gain_ffn

    half = width // 2
    slots = lax.dynamic_slice_in_dim(passage_owner, head_place * passages, passages) ^ blk_place
    lengths = lax.dynamic_slice_in_dim(passage_len, head_place * passages, passages)

    normed_one, self_qkv, self_flat, *partials = call_self(
        dec_in, dec_len, gain_one, w_query, w_key, w_value, w_out, head_count
    )
    quarter = (core * 2 + blk_place % 2) * (width // 4)
    if CFG["s_w"] == 1:
        quarter = after(quarter, self_flat)
    pieces = jnp.concatenate(
        [
            lax.dynamic_slice_in_dim(weight, quarter, width // 4, 0)
            for weight in (c_key, c_value, c_query)
        ],
        axis=0,
    )
    pieces = [partner(pieces, "head", k) for k in range(1, head_count)]
    if CFG["s_y"] == 1:
        pieces = hold(pieces, self_flat)
    near = pieces
    beside = [partner(piece_, "blk", 1) for piece_ in pieces]
    pieces = pieces + beside + across_core(pieces) + across_core(beside)
    partials = swap_parts(partials)
    if CFG["s_p"] == 2:
        partials = hold(partials, *near)
    elif CFG["s_p"] == 3:
        partials = hold(partials, near[0])
    first, message = call(
        functools.partial(normed_kernel, head_count),
        [shaped((piece, depth), f32), shaped((chunk_count, piece, depth), bf16)],
        [],
        [*partials, dec_in, gain_two],
    )
    if CFG["s_p"] == 1:
        (message,) = hold([message], *near)
    elif CFG["s_p"] == 4:
        (message,) = hold([message], near[0])
    chunks = exchange(message, "blk", "head")
    enc_keys, enc_values, key_full, value_full = project(enc_out, (c_key, c_value), pieces)
    early, queries, query_full = make_queries(
        chunks, c_query, normed_one, self_flat, pieces, blk_count, head_count
    )
    c_gate = {0: [queries], 1: [queries, enc_keys]}[CFG["s_c"]]
    mine = lax.dynamic_slice_in_dim(c_out, after(core, *c_gate) * half, half, 0)
    cross_out = [partner(mine, "head", k) for k in range(1, head_count)]
    early_beside = partner(after(early, *c_gate), "blk", 1)

    partials = cross_forward(
        slots, lengths, queries, enc_keys, enc_values, head_count, width
    )
    partials, early_beside, *cross_out = hold([partials, early_beside, *cross_out])
    (cross_out_full,) = call(
        assemble_kernel,
        [shaped((depth, depth), bf16)],
        [],
        [c_out, *cross_out, *across_core(cross_out)],
    )
    cross, second, logsum, *messages = call(
        functools.partial(combine_kernel, width),
        [
            shaped((piece, depth), f32),
            shaped((piece, depth), f32),
            shaped((piece, STATS), f32),
        ]
        + [shaped((piece, depth + width), bf16)] * head_count,
        [],
        [exchange(partials, "blk", "head"), first, cross_out_full, gain_three],
    )
    chunks = swap_parts(messages)
    outs = call(
        functools.partial(ffn_kernel, head_count),
        [shaped((piece, depth), f32)] * head_count
        + [
            shaped((head_count, piece, depth), f32),
            shaped((rows, 2 * depth + 2 * units), bf16),
            shaped((rows, width), bf16),
        ],
        [],
        [*chunks, cotangent, w_in, w_back],
        [pltpu.VMEM((rows, depth), f32)],
    )
    layer, wide, cross_cols = outs[head_count:]
    wide_beside = partner(wide, "blk", 1)
    if CFG["m_early"] == 0:
        early = plane_gather_wide(after(early, wide), early_beside, small)
    upstream = swap_parts(outs[:head_count])
    grad_second, gain_ffn_part, message = call(
        functools.partial(branch_kernel, head_count, width),
        [
            shaped((piece, depth), f32),
            shaped((1, depth), f32),
            shaped((chunk_count, piece, depth + STATS), bf16),
        ],
        [],
        [*upstream, second, gain_three, cotangent, cross_out_full, cross, logsum],
    )
    message, wide, wide_beside = hold([message, wide, wide_beside])
    branches = exchange(message, "blk", "head")
    branches, layer = hold([branches, layer])
    wide = plane_gather_wide(wide, wide_beside, small)
    if CFG["m_early"] == 1:
        early = plane_gather_wide(after(early, message), early_beside, small)
    layer = exchange(layer, "head")
    query_grads, branch_two, enc_key_grads, enc_value_grads = cross_backward(
        slots,
        lengths,
        queries,
        cross_out_full,
        enc_keys,
        enc_values,
        branches,
        head_count,
        width,
    )
    if CFG["m_early"] == 2:
        query_grads, layer = hold([query_grads, layer])
        early = plane_gather_wide(after(early, query_grads), early_beside, small)
    else:
        query_grads, layer, *early = hold([query_grads, layer, *early])
    query_grads = exchange(query_grads, "blk", "head")

    shares = projection_grads(
        enc_key_grads, enc_value_grads, enc_out, cross_cols, branch_two, plane, head_count
    )
    if CFG["t_cs"] == 1:
        query_grads, shares = hold([query_grads, shares])
    if CFG["w_k8"] == 1:
        (query_grads,) = hold([query_grads], *wide[1:])
    grad_first, gain_cross_part, *messages = call(
        functools.partial(first_kernel, head_count),
        [shaped((piece, depth), f32), shaped((1, depth), f32)]
        + [shaped((piece, 2 * depth + width), bf16)] * head_count,
        [],
        [query_grads, first, gain_two, query_full, grad_second, second, layer],
    )
    chunks = swap_parts(messages)
    if small:
        if CFG["t_shq"] == 1:
            shares = after(shares, messages[0])
        shares = exchange(shares, "dp", "blk")
        wide = wide + across_core(wide)
        early = early + across_core(early)
    else:
        early = early[:1]
    outs = call(
        functools.partial(self_back_kernel, head_count),
        (
            [shaped((piece, depth), f32)] * head_count
            if CFG["t_rsz"] == "perm"
            else [shaped((head_count, piece, depth), f32)]
        )
        + [
            shaped((plane if small else 1, rows, depth + 4 * width), bf16),
            shaped((rows, depth), bf16),
        ],
        [dec_len],
        [*chunks, w_out, self_qkv, w_query, w_key, w_value],
        [pltpu.VMEM((rows, depth), f32), pltpu.VMEM((rows, depth + 4 * width), bf16)],
    )
    late, layer_out = outs[-2:]
    shares_gate = {5: [chunks[len(chunks) > 1]], 0: [], 1: [late], 2: []}[CFG["t_sh"]]
    shares, *wide = hold([shares, *wide], *shares_gate)
    if not small:
        late = [late.reshape(late.shape[1:])]
    elif CFG["t_late"] == "a2a":
        late = [exchange(late, "dp", "blk")]
    else:
        late = plane_gather(late.reshape(late.shape[1:]))
    if CFG["t_rsz"] == "perm":
        upstream = swap_parts(outs[:head_count])
    else:
        upstream = [exchange(outs[0], "head")]
    if CFG["t_enc"] == 0:
        enc_grad_pair = hold([enc_key_grads, enc_value_grads], upstream[-1])
        grad_enc = encoder_grads(*enc_grad_pair, key_full, value_full)
    (message,) = call(
        functools.partial(input_kernel, len(upstream)),
        [shaped((head_count if CFG["t_agz"] == "a2a" else 1, piece + 8, depth), f32)],
        [],
        [*upstream, dec_in, gain_one, grad_first, gain_cross_part, gain_ffn_part],
        micros=3 * CFG["t_cost"],
    )
    if CFG["t_latep"] == 1:
        message = after(message, *late[: len(late) // 2 + 1])
    if CFG["t_sh"] == 2:
        shares = after(shares, message)
    if CFG["t_agz"] == "perm":
        chunks = share_heads(message.reshape(message.shape[1:]))
    else:
        chunks = [exchange(message, "head")]
    if CFG["t_latep"] == 2:
        chunks = hold(chunks, *late[: len(late) // 2 + 1])
    if CFG["t_enc"] == 1:
        enc_grad_pair = hold([enc_key_grads, enc_value_grads], message)
        grad_enc = encoder_grads(*enc_grad_pair, key_full, value_full)
    elif CFG["t_enc"] == 2:
        grad_enc = encoder_grads(enc_key_grads, enc_value_grads, key_full, value_full)
    elif CFG["t_enc"] == 3:
        enc_grad_pair = hold([enc_key_grads, enc_value_grads], chunks[-1])
        grad_enc = encoder_grads(*enc_grad_pair, key_full, value_full)
    grad_in, gains = call(
        functools.partial(place_kernel, head_count),
        [shaped((rows, depth), f32), shaped((8, depth), f32)],
        [],
        chunks,
        micros=3 * CFG["t_cost"],
    )
    if small:
        blocks, cross_share = call(
            share_kernel,
            [
                shaped((head_count, width // 4, depth), bf16),
                shaped((width // plane, depth), bf16),
            ],
            [],
            [shares],
            micros=3 * CFG["t_cost"],
        )
        blocks = exchange(blocks, "head")
        (shares,) = call(
            spread_kernel,
            [shaped((plane, width // 4 + width // plane + 24, depth), bf16)],
            [],
            [blocks, cross_share, gains],
            micros=3 * CFG["t_cost"],
        )
        grad_c_key, grad_c_value, grad_c_out, gains = call(
            collect_kernel,
            [shaped((width, depth), f32)] * 3 + [shaped((8, depth), f32)],
            [],
            [exchange(shares, "dp", "blk")],
            micros=3 * CFG["t_cost"],
        )
    else:
        gains, shares = lax.psum((gains, shares.astype(f32)), ("dp", "blk"))
        blocks = shares[: 2 * depth].reshape(2, head_count, width, depth)
        blocks = jnp.swapaxes(blocks, 0, 1)
        blocks = sum(swap_parts([blocks[k] for k in range(head_count)]))
        grad_c_key, grad_c_value = blocks[0], blocks[1]
        grad_c_out = shares[2 * depth :]


    if CFG["t_broad"] == 1:
        wide = hold(wide, message)
    elif CFG["t_broad"] == 2:
        wide = hold(wide, grad_in)
    broad = call(
        functools.partial(wide_kernel, len(wide)),
        [shaped((depth, units), f32), shaped((units, depth), f32)],
        [],
        wide,
        [pltpu.VMEM((sum(part.shape[0] for part in wide), wide[0].shape[1]), bf16)],
        8 * CFG["t_cost"],
    )
    slim = call(
        functools.partial(weight_kernel, len(early), len(late), width),
        [shaped((width, depth), f32)] * 5,
        [],
        [*early, *late],
        [
            pltpu.VMEM((sum(part.shape[0] for part in early), early[0].shape[1]), bf16),
            pltpu.VMEM((plane * rows if small else rows, late[0].shape[-1]), bf16),
        ],
        6 * CFG["t_cost"],
    )
    if not small:
        slim, broad = lax.psum((tuple(slim), tuple(broad)), ("dp", "blk"))
    return (
        layer_out,
        grad_in,
        grad_enc,
        gains[0],
        gains[1],
        gains[2],
        *slim,
        grad_c_key,
        grad_c_value,
        grad_c_out,
        *broad,
    )


def solution(mesh):
    rows = P(("dp", "blk"), None)
    enc = P(("dp", "blk", "head"), None)
    each = P(("dp", "blk"))
    heads = P("head", None)
    return jax.shard_map(
        body,
        mesh=mesh,
        in_specs=(
            rows,
            enc,
            each,
            each,
            each,
            P(),
            P(),
            P(),
            *[heads] * 8,
            P(None, "head"),
            heads,
            rows,
        ),
        out_specs=(rows, rows, enc, P(), P(), P(), *[heads] * 8, P(None, "head"), heads),
        check_vma=False,
    )
```

time: 465 us -> 332 us (0.71); the launches traced: 458 us -> 330 us
  Pallas kernels: 43.4 us -> 108 us
  matrix products: 40.4 us -> 0 us
  local copies, waits for them, and re-layouts: 56.8 us -> 18.3 us
  starting transfers between devices: 119 us -> 83.3 us
  blocking collectives: 41 us -> 14.9 us
  other arithmetic: 26.1 us -> 0.6 us
  between operations: 15.9 us -> 1.78 us
  waiting for transfers between devices: 116 us -> 103 us
    pallas_call x10 -> x19, Pallas kernels: 12.7 us -> 84.9 us  [the longest x14 48.2 us: call(): pl.pallas_call(kernel, grid=(1,), out_shape=tuple(outs), in_specs=[smem()...]
    ppermute x87 -> x44, starting transfers between devices: 118 us -> 48.2 us  [partner(): return lax.ppermute(array, axis, [(i, i ^ by) for i in range(size)])]
    ppermute x87 -> x44, waiting for transfers between devices: 116 us -> 71.5 us  [partner(): return lax.ppermute(array, axis, [(i, i ^ by) for i in range(size)])]
    psum x1 -> x0, blocking collectives: 41 us -> none  [body(): lax.psum(jnp.concatenate([gain_self_part, gain_cross_part, gain_ffn_part]...]
    dot_general x18 -> x0, matrix products: 40.4 us -> none  [the longest x14 24.5 us: tn(): lax.dot_general(left, right, (((0,), (0,)), ((), ())), preferred_element_...]
    all_to_all x0 -> x8, starting transfers between devices: none -> 35.1 us  [exchange(): return lax.all_to_all(array, axes, 0, 0)]
    all_to_all x0 -> x8, waiting for transfers between devices: none -> 31.6 us  [exchange(): return lax.all_to_all(array, axes, 0, 0)]
    unnamed x182 -> x106, local copies, waits for them, and re-layouts: 34.3 us -> 12.3 us
  transfers between devices with their start and end apart: 88 -> 52, of which waited for: 26 -> 25; matrix products, arithmetic and copies ran while one was open for 21% -> 2% of each run, Pallas kernels for 9% -> 28%
where the time goes in v2:
time: 332 us; the launch traced here: 330 us
  Pallas kernels  108 us (33%)
  waiting for transfers between devices  103 us (31%)
  starting transfers between devices  83.3 us (25%)
  local copies, waits for them, and re-layouts  18.3 us (6%)
  blocking collectives  14.9 us (4%)
    ppermute x44, waiting for transfers between devices, partner(): return lax.ppermute(array, axis, [(i, i ^ by) for i in range(size)])  71.5 us
    pallas_call x14, Pallas kernels, call(): pl.pallas_call(kernel, grid=(1,), out_shape=tuple(outs), in_specs=[smem()...  48.2 us
    ppermute x44, starting transfers between devices, partner(): return lax.ppermute(array, axis, [(i, i ^ by) for i in range(size)])  48.2 us
    all_to_all x8, starting transfers between devices, exchange(): return lax.all_to_all(array, axes, 0, 0)  35.1 us
    all_to_all x8, waiting for transfers between devices, exchange(): return lax.all_to_all(array, axes, 0, 0)  31.6 us
    all_to_all x1, blocking collectives, exchange(): return lax.all_to_all(array, axes, 0, 0)  14.9 us
    pallas_call x1, Pallas kernels, cross_backward(): pl.pallas_call(functools.partial(cross_backward_kernel, blk_count, head_c...  13.3 us
    unnamed x106, local copies, waits for them, and re-layouts  12.3 us
  transfers between devices with their start and end apart: 52, of which 25 were waited for; matrix products, arithmetic and copies ran while one was open for 2% of the time, Pallas kernels for 28%

profile of v2, /device:TPU:0, one launch (start us, length us, event | category | flops | bytes accessed | tf_op | source)
XLA Modules:
  0.0 329.7 jit_solution(12293447767737455023)
XLA Ops:
  2.5 5.1 %collective-permute-start.5 = (bf16[144,768]{1,0:T(8,128)(2,1)S(1)}, bf16[144,768]{1,0:T(8,128)(2,1)S(1)}, u32[]{:S(2)}, u32[]{:S(2)}) collective-permute-start(bf16[144,768]{1,0:T(8,128)(2,1)S(1)} %pad_maximum_fusion), channel_id=1, source_target_pairs={{0,3},{1,2},{2,1},{3,0},{4,7},{5,6},{6,5},{7,4},{8,11},{9,10},{10,... | collective-permute-start | bytes 663560 | tf_op jit(solution)/shard_map/ppermute | solution.py:936
  17.2 8.1 %collective-permute-done.refs_1_ = f32[32,768]{1,0:T(8,128)S(1)} collective-permute-done((f32[32,768]{1,0:T(8,128)}, f32[32,768]{1,0:T(8,128)S(1)}, u32[]{:S(2)}, u32[]{:S(2)}) %collective-permute-start) | collective-permute-done | bytes 98336 | tf_op jit(solution)/shard_map/ppermute | solution.py:936
  25.2 8.5 %collective-permute-done.1.refs_2_ = f32[32,768]{1,0:T(8,128)S(1)} collective-permute-done((f32[32,768]{1,0:T(8,128)}, f32[32,768]{1,0:T(8,128)S(1)}, u32[]{:S(2)}, u32[]{:S(2)}) %collective-permute-start.1) | collective-permute-done | bytes 98336 | tf_op jit(solution)/shard_map/ppermute | solution.py:936
  36.4 4.9 %all-to-all-start = ((bf16[8,32,768]{2,1,0:T(8,128)(2,1)}), bf16[8,32,768]{2,1,0:T(8,128)(2,1)S(1)}, u32[]{:S(2)}, u32[]{:S(2)}) async-start(bf16[8,32,768]{2,1,0:T(8,128)(2,1)} %get-tuple-element.113), calls=%async_computation | async-start | bytes 786432 | tf_op jit(solution)/shard_map/all_to_all | solution.py:945
  45.9 7.5 %collective-permute-done.8.refs_5_.refs_7_ = bf16[144,768]{1,0:T(8,128)(2,1)S(1)} collective-permute-done((bf16[144,768]{1,0:T(8,128)(2,1)S(1)}, bf16[144,768]{1,0:T(8,128)(2,1)S(1)}, u32[]{:S(2)}, u32[]{:S(2)}) %collective-permute-start.8) | collective-permute-done | bytes 221216 | tf_op jit(solution)/shard_map/ppermute | solution.py:936
  53.5 4.7 %collective-permute-done.7.refs_4_.refs_6_ = bf16[144,768]{1,0:T(8,128)(2,1)S(1)} collective-permute-done((bf16[144,768]{1,0:T(8,128)(2,1)S(1)}, bf16[144,768]{1,0:T(8,128)(2,1)S(1)}, u32[]{:S(2)}, u32[]{:S(2)}) %collective-permute-start.7) | collective-permute-done | bytes 221216 | tf_op jit(solution)/shard_map/ppermute | solution.py:936
  64.4 9.5 %shard_map.309 = (bf16[1920,768]{1,0:T(8,128)(2,1)}, bf16[1920,768]{1,0:T(8,128)(2,1)}, bf16[768,768]{1,0:T(8,128)(2,1)}, bf16[768,768]{1,0:T(8,128)(2,1)}) custom-call(bf16[1920,768]{1,0:T(8,128)(2,1)} %refs_2_.2, bf16[192,768]{1,0:T(8,128)(2,1)} %refs_0_.1, bf16[192,768]{1,0:T(8,128)(2,1)} %refs_1_.1, bf16[144,768]{1,0:T(8,128)(2,1)} %copy-done.11, ...), custom_call_target="tpu_custom_call" | custom-call | bytes 27000000 | tf_op jit(solution)/shard_map/pallas_call | solution.py:310
  85.2 9.6 %shard_map.310 = bf16[8,32,896]{2,1,0:T(8,128)(2,1)} custom-call(s32[5]{0:T(128)} %dynamic-slice_xor_fusion.refs_0_, s32[5]{0:T(128)} %dynamic_slice.19.refs_1_, bf16[2,128,768]{2,1,0:T(8,128)(2,1)} %get-tuple-element.116.refs_2_, bf16[1920,768]{1,0:T(8,128)(2,1)} %get-tuple-element.117.refs_3_.refs_4_, bf16[1920,768]{1,0:T(8,128)(2,1)} %get-tuple-element.118.refs_4_.refs_5_), custom_call_target="tpu_custom_call" | custom-call | bytes 45000000 | tf_op jit(solution)/shard_map/pallas_call | solution.py:452
  104.6 7.8 %all-to-all-done.1.refs_0_ = bf16[8,32,896]{2,1,0:T(8,128)(2,1)S(1)} async-done(((bf16[8,32,896]{2,1,0:T(8,128)(2,1)}), bf16[8,32,896]{2,1,0:T(8,128)(2,1)S(1)}, u32[]{:S(2)}, u32[]{:S(2)}) %all-to-all-start.1) | async-done | bytes 458784 | tf_op jit(solution)/shard_map/all_to_all | solution.py:945
  134.8 5.6 %collective-permute-done.26.refs_2_ = f32[32,768]{1,0:T(8,128)S(1)} collective-permute-done((f32[32,768]{1,0:T(8,128)}, f32[32,768]{1,0:T(8,128)S(1)}, u32[]{:S(2)}, u32[]{:S(2)}) %collective-permute-start.26) | collective-permute-done | bytes 98336 | tf_op jit(solution)/shard_map/ppermute | solution.py:936
  145.6 5.5 %all-to-all-start.2 = ((bf16[8,32,896]{2,1,0:T(8,128)(2,1)}), bf16[8,32,896]{2,1,0:T(8,128)(2,1)S(1)}, u32[]{:S(2)}, u32[]{:S(2)}) async-start(bf16[8,32,896]{2,1,0:T(8,128)(2,1)} %get-tuple-element.140), calls=%async_computation.2 | async-start | bytes 917504 | tf_op jit(solution)/shard_map/all_to_all | solution.py:945
  152.8 10.4 %all-to-all-done.2.refs_6_ = bf16[8,32,896]{2,1,0:T(8,128)(2,1)S(1)} async-done(((bf16[8,32,896]{2,1,0:T(8,128)(2,1)}), bf16[8,32,896]{2,1,0:T(8,128)(2,1)S(1)}, u32[]{:S(2)}, u32[]{:S(2)}) %all-to-all-start.2) | async-done | bytes 458784 | tf_op jit(solution)/shard_map/all_to_all | solution.py:945
  172.5 13.3 %shard_map.315 = (bf16[8,32,768]{2,1,0:T(8,128)(2,1)}, bf16[128,768]{1,0:T(8,128)(2,1)}, bf16[1920,768]{1,0:T(8,128)(2,1)}, bf16[1920,768]{1,0:T(8,128)(2,1)}) custom-call(s32[5]{0:T(128)} %dynamic-slice_xor_fusion.refs_0_, s32[5]{0:T(128)} %dynamic_slice.19.refs_1_, bf16[2,128,768]{2,1,0:T(8,128)(2,1)} %get-tuple-element.116.refs_2_, ...), custom_call_target="tpu_custom_call" | custom-call | bytes 48000000 | tf_op jit(solution)/shard_map/pallas_call | solution.py:662
  185.9 4.9 %all-to-all-start.4 = ((bf16[8,32,768]{2,1,0:T(8,128)(2,1)}), bf16[8,32,768]{2,1,0:T(8,128)(2,1)S(1)}, u32[]{:S(2)}, u32[]{:S(2)}) async-start(bf16[8,32,768]{2,1,0:T(8,128)(2,1)} %get-tuple-element.147), calls=%async_computation.4 | async-start | bytes 786432 | tf_op jit(solution)/shard_map/all_to_all | solution.py:945
  190.8 10.0 %shard_map.316 = bf16[8,224,768]{2,1,0:T(8,128)(2,1)} custom-call(bf16[1920,768]{1,0:T(8,128)(2,1)} %get-tuple-element.173.refs_0_.keys_ref, bf16[1920,768]{1,0:T(8,128)(2,1)} %get-tuple-element.174.refs_1_.values_ref, bf16[1920,768]{1,0:T(8,128)(2,1)} %refs_2_.2, bf16[128,192]{1,0:T(8,128)(2,1)} %get-tuple-element.150.refs_3_, ...), custom_call_target="tpu_custom_call" | custom-call | bytes 12000000 | tf_op jit(solution)/shard_map/pallas_call | solution.py:848
  214.4 8.2 %collective-permute-done.32.refs_2_ = bf16[32,1728]{1,0:T(8,128)(2,1)S(1)} collective-permute-done((bf16[32,1728]{1,0:T(8,128)(2,1)}, bf16[32,1728]{1,0:T(8,128)(2,1)S(1)}, u32[]{:S(2)}, u32[]{:S(2)}) %collective-permute-start.32) | collective-permute-done | bytes 110624 | tf_op jit(solution)/shard_map/ppermute | solution.py:936
  223.3 5.3 %shard_map.318 = (f32[32,768]{1,0:T(8,128)}, f32[32,768]{1,0:T(8,128)}, f32[32,768]{1,0:T(8,128)}, f32[32,768]{1,0:T(8,128)}, bf16[8,128,1536]{2,1,0:T(8,128)(2,1)}, /*index=5*/bf16[128,768]{1,0:T(8,128)(2,1)}) custom-call(s32[1]{0:T(128)S(6)} %copy.37.len_ref, bf16[32,1728]{1,0:T(8,128)(2,1)} %get-tuple-element.159.refs_0_, bf16[32,1728]{1,0:T(8,128)(2,1)} %copy-done.32, ...), custom_call_target="tpu_custom_call" | custom-call | bytes 10500000 | tf_op jit(solution)/shard_map/pallas_call | solution.py:84
  228.6 9.2 %all-to-all-done.5.shares_ref = bf16[8,224,768]{2,1,0:T(8,128)(2,1)S(1)} async-done(((bf16[8,224,768]{2,1,0:T(8,128)(2,1)}), bf16[8,224,768]{2,1,0:T(8,128)(2,1)S(1)}, u32[]{:S(2)}, u32[]{:S(2)}) %all-to-all-start.5) | async-done | bytes 2752544 | tf_op jit(solution)/shard_map/all_to_all | solution.py:945
  242.2 14.9 %all_to_all.45.blocks_ref = bf16[4,48,768]{2,1,0:T(8,128)(2,1)} all-to-all(bf16[4,48,768]{2,1,0:T(8,128)(2,1)} %get-tuple-element.180), channel_id=1, replica_groups=mesh['dp'=4,'blk'=2,'head'=4] {'head'}, dimensions={0} | all-to-all | bytes 589824 | tf_op jit(solution)/shard_map/all_to_all | solution.py:945
  267.1 5.2 %collective-permute-done.35.refs_2_ = f32[32,768]{1,0:T(8,128)S(1)} collective-permute-done((f32[32,768]{1,0:T(8,128)S(1)}, f32[32,768]{1,0:T(8,128)S(1)}, u32[]{:S(2)}, u32[]{:S(2)}) %collective-permute-start.35) | collective-permute-done | bytes 98336 | tf_op jit(solution)/shard_map/ppermute | solution.py:936
  283.2 5.2 %collective-permute-done.38.refs_2_ = f32[40,768]{1,0:T(8,128)S(1)} collective-permute-done((f32[40,768]{1,0:T(8,128)}, f32[40,768]{1,0:T(8,128)S(1)}, u32[]{:S(2)}, u32[]{:S(2)}) %collective-permute-start.38) | collective-permute-done | bytes 122912 | tf_op jit(solution)/shard_map/ppermute | solution.py:936
  302.9 9.6 %shard_map.321 = f32[1920,768]{1,0:T(8,128)} custom-call(bf16[1920,768]{1,0:T(8,128)(2,1)} %get-tuple-element.173.refs_0_.keys_ref, bf16[1920,768]{1,0:T(8,128)(2,1)} %get-tuple-element.174.refs_1_.values_ref, bf16[768,768]{1,0:T(8,128)(2,1)} %get-tuple-element.175.key_ref, bf16[768,768]{1,0:T(8,128)(2,1)} %get-tuple-element.176.value_ref), custom_call_target="tpu_custom_call" | custom-call | bytes 1050000 | tf_op jit(solution)/shard_map/pallas_call | solution.py:869
  312.5 6.9 %shard_map.326 = (f32[768,768]{1,0:T(8,128)}, f32[768,768]{1,0:T(8,128)}) custom-call(bf16[256,3072]{1,0:T(8,128)(2,1)} %constant_dynamic-update-slice_fusion.2.refs_0_, bf16[256,3072]{1,0:T(8,128)(2,1)} %collective-permute-done.30.refs_1_, bf16[256,3072]{1,0:T(8,128)(2,1)} %collective-permute-done.40.refs_2_, bf16[256,3072]{1,0:T(8,128)(2,1)} %collective-permute-done.41.refs_3_), custom_call_target="tpu_custom_call" | custom-call | bytes 1200000 | tf_op jit(solution)/shard_map/pallas_call | solution.py:84
  319.4 6.3 %shard_map.325 = (f32[192,768]{1,0:T(8,128)}, f32[192,768]{1,0:T(8,128)}, f32[192,768]{1,0:T(8,128)}, f32[192,768]{1,0:T(8,128)}, f32[192,768]{1,0:T(8,128)}) custom-call(bf16[256,1792]{1,0:T(8,128)(2,1)} %copy-done.2, bf16[256,1792]{1,0:T(8,128)(2,1)} %copy-done.8, bf16[256,1792]{1,0:T(8,128)(2,1)} %collective-permute-done.42.refs_2_, ...), custom_call_target="tpu_custom_call" | custom-call | bytes 900000 | tf_op jit(solution)/shard_map/pallas_call | solution.py:84
  (217 shorter events, 141.6 us)
Async XLA Ops:
  2.5 33.9 %collective-permute-start.5 = (bf16[144,768]{1,0:T(8,128)(2,1)S(1)}, bf16[144,768]{1,0:T(8,128)(2,1)S(1)}, u32[]{:S(2)}, u32[]{:S(2)}) collective-permute-start(bf16[144,768]{1,0:T(8,128)(2,1)S(1)} %pad_maximum_fusion), channel_id=1, source_target_pairs={{0,3},{1,2},{2,1},{3,0},{4,7},{5,6},{6,5},{7,4},{8,11},{9,10},{10,... | collective-permute-start | bytes 663560 | tf_op jit(solution)/shard_map/ppermute | solution.py:936
  7.6 28.8 %collective-permute-start.4 = (bf16[144,768]{1,0:T(8,128)(2,1)S(1)}, bf16[144,768]{1,0:T(8,128)(2,1)S(1)}, u32[]{:S(2)}, u32[]{:S(2)}) collective-permute-start(bf16[144,768]{1,0:T(8,128)(2,1)S(1)} %pad_maximum_fusion), channel_id=1, source_target_pairs={{0,2},{1,3},{2,0},{3,1},{4,6},{5,7},{6,4},{7,5},{8,10},{9,11},{10,... | collective-permute-start | bytes 663560 | tf_op jit(solution)/shard_map/ppermute | solution.py:936
  7.6 28.8 %collective-permute-start.3 = (bf16[144,768]{1,0:T(8,128)(2,1)S(1)}, bf16[144,768]{1,0:T(8,128)(2,1)S(1)}, u32[]{:S(2)}, u32[]{:S(2)}) collective-permute-start(bf16[144,768]{1,0:T(8,128)(2,1)S(1)} %pad_maximum_fusion), channel_id=1, source_target_pairs={{0,1},{1,0},{2,3},{3,2},{4,5},{5,4},{6,7},{7,6},{8,9},{9,8},{10,11... | collective-permute-start | bytes 663560 | tf_op jit(solution)/shard_map/ppermute | solution.py:936
  14.2 19.5 %collective-permute-start.1 = (f32[32,768]{1,0:T(8,128)}, f32[32,768]{1,0:T(8,128)S(1)}, u32[]{:S(2)}, u32[]{:S(2)}) collective-permute-start(f32[32,768]{1,0:T(8,128)} %get-tuple-element.110), channel_id=1, source_target_pairs={{0,2},{1,3},{2,0},{3,1},{4,6},{5,7},{6,4},{7,5},{8,10},{9,11},{10,... | collective-permute-start | bytes 294920 | tf_op jit(solution)/shard_map/ppermute | solution.py:936
  36.4 37.5 %all-to-all-start = ((bf16[8,32,768]{2,1,0:T(8,128)(2,1)}), bf16[8,32,768]{2,1,0:T(8,128)(2,1)S(1)}, u32[]{:S(2)}, u32[]{:S(2)}) async-start(bf16[8,32,768]{2,1,0:T(8,128)(2,1)} %get-tuple-element.113), calls=%async_computation | async-start | bytes 786432 | tf_op jit(solution)/shard_map/all_to_all | solution.py:945
  43.5 18.7 %collective-permute-start.6 = (bf16[144,768]{1,0:T(8,128)(2,1)S(1)}, bf16[144,768]{1,0:T(8,128)(2,1)S(1)}, u32[]{:S(2)}, u32[]{:S(2)}) collective-permute-start(bf16[144,768]{1,0:T(8,128)(2,1)S(1)} %collective-permute-done.3.refs_0_.refs_2_), channel_id=1, source_target_pairs={{0,4},{4,0},{1,5},{5,1},{2,6},{6,2},{3,7},{7,3},{8,12},{12,8},{9,1... | collective-permute-start | bytes 663560 | tf_op jit(solution)/shard_map/ppermute | solution.py:936
  45.4 16.7 %collective-permute-start.10 = (bf16[144,768]{1,0:T(8,128)(2,1)S(1)}, bf16[144,768]{1,0:T(8,128)(2,1)S(1)}, u32[]{:S(2)}, u32[]{:S(2)}) collective-permute-start(bf16[144,768]{1,0:T(8,128)(2,1)S(1)} %collective-permute-done.4.refs_1_.refs_3_), channel_id=1, source_target_pairs={{0,8},{8,0},{16,24},{24,16},{1,9},{9,1},{17,25},{25,17},{2,10},{10... | collective-permute-start | bytes 663560 | tf_op jit(solution)/shard_map/ppermute | solution.py:936
  45.4 16.7 %collective-permute-start.9 = (bf16[144,768]{1,0:T(8,128)(2,1)S(1)}, bf16[144,768]{1,0:T(8,128)(2,1)S(1)}, u32[]{:S(2)}, u32[]{:S(2)}) collective-permute-start(bf16[144,768]{1,0:T(8,128)(2,1)S(1)} %collective-permute-done.3.refs_0_.refs_2_), channel_id=1, source_target_pairs={{0,8},{8,0},{16,24},{24,16},{1,9},{9,1},{17,25},{25,17},{2,10},{10... | collective-permute-start | bytes 663560 | tf_op jit(solution)/shard_map/ppermute | solution.py:936
  78.4 16.8 %collective-permute-start.15 = (bf16[128,1792]{1,0:T(8,128)(2,1)}, bf16[128,1792]{1,0:T(8,128)(2,1)S(1)}, u32[]{:S(2)}, u32[]{:S(2)}) collective-permute-start(bf16[128,1792]{1,0:T(8,128)(2,1)} %get-tuple-element.145), channel_id=1, source_target_pairs={{0,4},{4,0},{1,5},{5,1},{2,6},{6,2},{3,7},{7,3},{8,12},{12,8},{9,1... | collective-permute-start | bytes 1376264 | tf_op jit(solution)/shard_map/ppermute | solution.py:936
  79.6 15.2 %collective-permute-start.18 = (bf16[96,768]{1,0:T(8,128)(2,1)S(1)}, bf16[96,768]{1,0:T(8,128)(2,1)S(1)}, u32[]{:S(2)}, u32[]{:S(2)}) collective-permute-start(bf16[96,768]{1,0:T(8,128)(2,1)S(1)} %constant_dynamic-slice_fusion), channel_id=1, source_target_pairs={{0,3},{1,2},{2,1},{3,0},{4,7},{5,6},{6,5},{7,4},{8,11},{9,10},{10,... | collective-permute-start | bytes 442376 | tf_op jit(solution)/shard_map/ppermute | solution.py:936
  95.1 17.3 %all-to-all-start.1 = ((bf16[8,32,896]{2,1,0:T(8,128)(2,1)}), bf16[8,32,896]{2,1,0:T(8,128)(2,1)S(1)}, u32[]{:S(2)}, u32[]{:S(2)}) async-start(bf16[8,32,896]{2,1,0:T(8,128)(2,1)} %shard_map.310), calls=%async_computation.1 | async-start | bytes 917504 | tf_op jit(solution)/shard_map/all_to_all | solution.py:945
  128.9 16.7 %collective-permute-start.28 = (bf16[128,3072]{1,0:T(8,128)(2,1)}, bf16[128,3072]{1,0:T(8,128)(2,1)}, u32[]{:S(2)}, u32[]{:S(2)}) collective-permute-start(bf16[128,3072]{1,0:T(8,128)(2,1)} %get-tuple-element.153), channel_id=1, source_target_pairs={{0,4},{4,0},{1,5},{5,1},{2,6},{6,2},{3,7},{7,3},{8,12},{12,8},{9,1... | collective-permute-start | bytes 2359304 | tf_op jit(solution)/shard_map/ppermute | solution.py:936
  145.6 17.6 %all-to-all-start.2 = ((bf16[8,32,896]{2,1,0:T(8,128)(2,1)}), bf16[8,32,896]{2,1,0:T(8,128)(2,1)S(1)}, u32[]{:S(2)}, u32[]{:S(2)}) async-start(bf16[8,32,896]{2,1,0:T(8,128)(2,1)} %get-tuple-element.140), calls=%async_computation.2 | async-start | bytes 917504 | tf_op jit(solution)/shard_map/all_to_all | solution.py:945
  151.2 34.6 %collective-permute-start.29 = (bf16[256,1792]{1,0:T(8,128)(2,1)S(1)}, bf16[256,1792]{1,0:T(8,128)(2,1)S(1)}, u32[]{:S(2)}, u32[]{:S(2)}) collective-permute-start(bf16[256,1792]{1,0:T(8,128)(2,1)S(1)} %constant_dynamic-update-slice_fusion.refs_0_), channel_id=1, source_target_pairs={{0,16},{8,24},{16,0},{24,8},{1,17},{9,25},{17,1},{25,9},{2,18},{10... | collective-permute-start | bytes 2752520 | tf_op jit(solution)/shard_map/ppermute | solution.py:936
  163.2 22.7 %all-to-all-start.3 = ((f32[4,32,768]{2,1,0:T(8,128)}), f32[4,32,768]{2,1,0:T(8,128)S(1)}, u32[]{:S(2)}, u32[]{:S(2)}) async-start(f32[4,32,768]{2,1,0:T(8,128)} %get-tuple-element.144), calls=%async_computation.3 | async-start | bytes 786432 | tf_op jit(solution)/shard_map/all_to_all | solution.py:945
  171.0 34.5 %collective-permute-start.30 = (bf16[256,3072]{1,0:T(8,128)(2,1)}, bf16[256,3072]{1,0:T(8,128)(2,1)}, u32[]{:S(2)}, u32[]{:S(2)}) collective-permute-start(bf16[256,3072]{1,0:T(8,128)(2,1)} %constant_dynamic-update-slice_fusion.2.refs_0_), channel_id=1, source_target_pairs={{0,16},{8,24},{16,0},{24,8},{1,17},{9,25},{17,1},{25,9},{2,18},{10... | collective-permute-start | bytes 4718600 | tf_op jit(solution)/shard_map/ppermute | solution.py:936
  185.9 14.9 %all-to-all-start.4 = ((bf16[8,32,768]{2,1,0:T(8,128)(2,1)}), bf16[8,32,768]{2,1,0:T(8,128)(2,1)S(1)}, u32[]{:S(2)}, u32[]{:S(2)}) async-start(bf16[8,32,768]{2,1,0:T(8,128)(2,1)} %get-tuple-element.147), calls=%async_computation.4 | async-start | bytes 786432 | tf_op jit(solution)/shard_map/all_to_all | solution.py:945
  201.5 36.4 %all-to-all-start.5 = ((bf16[8,224,768]{2,1,0:T(8,128)(2,1)}), bf16[8,224,768]{2,1,0:T(8,128)(2,1)S(1)}, u32[]{:S(2)}, u32[]{:S(2)}) async-start(bf16[8,224,768]{2,1,0:T(8,128)(2,1)} %shard_map.316), calls=%async_computation.5 | async-start | bytes 5505024 | tf_op jit(solution)/shard_map/all_to_all | solution.py:945
  205.1 23.5 %collective-permute-start.40 = (bf16[256,3072]{1,0:T(8,128)(2,1)}, bf16[256,3072]{1,0:T(8,128)(2,1)}, u32[]{:S(2)}, u32[]{:S(2)}) collective-permute-start(bf16[256,3072]{1,0:T(8,128)(2,1)} %constant_dynamic-update-slice_fusion.2.refs_0_), channel_id=1, source_target_pairs={{0,8},{8,0},{16,24},{24,16},{1,9},{9,1},{17,25},{25,17},{2,10},{10... | collective-permute-start | bytes 4718600 | tf_op jit(solution)/shard_map/ppermute | solution.py:936
  205.5 23.1 %collective-permute-start.41 = (bf16[256,3072]{1,0:T(8,128)(2,1)}, bf16[256,3072]{1,0:T(8,128)(2,1)}, u32[]{:S(2)}, u32[]{:S(2)}) collective-permute-start(bf16[256,3072]{1,0:T(8,128)(2,1)} %collective-permute-done.30.refs_1_), channel_id=1, source_target_pairs={{0,8},{8,0},{16,24},{24,16},{1,9},{9,1},{17,25},{25,17},{2,10},{10... | collective-permute-start | bytes 4718600 | tf_op jit(solution)/shard_map/ppermute | solution.py:936
  257.1 40.7 %all-to-all-start.8 = ((bf16[8,128,1536]{2,1,0:T(8,128)(2,1)}), bf16[8,128,1536]{2,1,0:T(8,128)(2,1)S(1)}, u32[]{:S(2)}, u32[]{:S(2)}) async-start(bf16[8,128,1536]{2,1,0:T(8,128)(2,1)} %get-tuple-element.178), calls=%async_computation.8 | async-start | bytes 6291456 | tf_op jit(solution)/shard_map/all_to_all | solution.py:945
  297.8 27.9 %all-to-all-start.7 = ((bf16[8,96,768]{2,1,0:T(8,128)(2,1)}), bf16[8,96,768]{2,1,0:T(8,128)(2,1)}, u32[]{:S(2)}, u32[]{:S(2)}) async-start(bf16[8,96,768]{2,1,0:T(8,128)(2,1)} %shard_map.323), calls=%async_computation.7 | async-start | bytes 2359296 | tf_op jit(solution)/shard_map/all_to_all | solution.py:945
  302.3 17.1 %collective-permute-start.42 = (bf16[256,1792]{1,0:T(8,128)(2,1)}, bf16[256,1792]{1,0:T(8,128)(2,1)}, u32[]{:S(2)}, u32[]{:S(2)}) collective-permute-start(bf16[256,1792]{1,0:T(8,128)(2,1)} %copy-done.2), channel_id=1, source_target_pairs={{0,8},{8,0},{16,24},{24,16},{1,9},{9,1},{17,25},{25,17},{2,10},{10... | collective-permute-start | bytes 2752520 | tf_op jit(solution)/shard_map/ppermute | solution.py:936
  302.5 16.9 %collective-permute-start.43 = (bf16[256,1792]{1,0:T(8,128)(2,1)}, bf16[256,1792]{1,0:T(8,128)(2,1)}, u32[]{:S(2)}, u32[]{:S(2)}) collective-permute-start(bf16[256,1792]{1,0:T(8,128)(2,1)} %copy-done.8), channel_id=1, source_target_pairs={{0,8},{8,0},{16,24},{24,16},{1,9},{9,1},{17,25},{25,17},{2,10},{10... | collective-permute-start | bytes 2752520 | tf_op jit(solution)/shard_map/ppermute | solution.py:936
  (80 other events, 545.8 us)

commit v3 on v2

--- a/solution.py
+++ b/solution.py
@@ -8,9 +8,9 @@
 from jax.sharding import PartitionSpec as P
 
 CFG = dict(
-    s_w=0, s_p=1, s_c=1, s_y=0, t_cost=0.05,
-    t_late="a2a", t_rsz="perm", t_agz="perm", t_latep=0, t_sh=1, t_shq=0, t_enc=0, t_broad=0,
-    cost=1.0, w_k8=1, t_cs=1, m_early=0,
+    s_o=1, s_a=1, s_xy=1, l_d=1, t_a=1, t_cost=0.05, k1=0.1, vmem=64, s_rs="bf16", m_e=1, t_shg=3, e_c=0, w_c=0,
+    t_late="perm", t_rsz="perm", t_agz="perm", t_shq=1, sh_q=0, cost=1.0, t_cs=1,
+    t_p=4, w_x=1, w_xy=1, l_p=0, l_xy=0, e_p=4, b_p=3, e_y=1,
 )
 DHEAD = 64
 LP = 384
@@ -23,7 +23,7 @@
 STATS = 128
 SECOND_LANE = 16
 SPLIT_LANE = 32
-VMEM_BYTES = 60 * 1024 * 1024
+VMEM_BYTES = CFG["vmem"] * 1024 * 1024
 
 
 def nn(left, right):
@@ -80,19 +80,37 @@
     return pl.BlockSpec(shape, lambda *_: (0,) * len(shape), pipeline_mode=pl.Buffered(1))
 
 
+class Weight:
+    def __init__(self, array, index):
+        self.array, self.index = array, index
+        self.shape = array.shape[1:]
+
+
+def spec_of(array):
+    if isinstance(array, Weight):
+        block = (None, *array.shape)
+        index = array.index
+        return pl.BlockSpec(block, lambda *_: (index, 0, 0), pipeline_mode=pl.Buffered(1))
+    return whole(array.shape)
+
+
+def value_of(array):
+    return array.array if isinstance(array, Weight) else array
+
+
 def call(kernel, outs, scalars, arrays, scratch=(), micros=3.5):
     return pl.pallas_call(
         kernel,
         grid=(1,),
         out_shape=tuple(outs),
-        in_specs=[smem()] * len(scalars) + [whole(array.shape) for array in arrays],
+        in_specs=[smem()] * len(scalars) + [spec_of(array) for array in arrays],
         out_specs=tuple(whole(out.shape) for out in outs),
         scratch_shapes=list(scratch),
         cost_estimate=cost(micros),
         compiler_params=pltpu.CompilerParams(
             vmem_limit_bytes=VMEM_BYTES, dimension_semantics=("arbitrary",)
         ),
-    )(*scalars, *arrays)
+    )(*scalars, *[value_of(array) for array in arrays])
 
 
 def my_head():
@@ -185,7 +203,7 @@
     total[...] = nn(attended, w_out_ref[...])
     piece = rows // len(partials)
     for k, partial in enumerate(partials):
-        partial[...] = total[rows_of(my_head() ^ k, piece), :]
+        partial[...] = total[rows_of(my_head() ^ k, piece), :].astype(partial.dtype)
 
 
 def call_self(dec_in, dec_len, gain, w_query, w_key, w_value, w_out, head_count):
@@ -196,7 +214,7 @@
         shaped((rows, depth), bf16),
         shaped((rows, 3 * width), bf16),
         shaped((rows, width), bf16),
-    ] + [shaped((rows // head_count, depth), f32)] * head_count
+    ] + [shaped((rows // head_count, depth), f32 if CFG["s_rs"] == "f32" else bf16)] * head_count
     return pl.pallas_call(
         self_kernel,
         grid=(1,),
@@ -204,7 +222,7 @@
         in_specs=[smem() if array is dec_len else whole(array.shape) for array in arrays],
         out_specs=tuple(whole(out.shape) for out in outs),
         scratch_shapes=[pltpu.VMEM((rows, depth), f32)],
-        cost_estimate=cost(4),
+        cost_estimate=cost(CFG["k1"]),
         compiler_params=pltpu.CompilerParams(
             vmem_limit_bytes=VMEM_BYTES, dimension_semantics=("arbitrary",)
         ),
@@ -215,43 +233,41 @@
     chunks = refs[:count]
     dec_ref, gain_ref, first_ref, message_ref = refs[count:]
     piece = first_ref.shape[0]
-    first = dec_ref[rows_of(my_head(), piece), :].astype(f32) + sum(chunk[...] for chunk in chunks)
+    first = dec_ref[rows_of(my_head(), piece), :].astype(f32) + sum(
+        chunk[...].astype(f32) for chunk in chunks
+    )
     first_ref[...] = first
     normed = normalize(first, gain_ref[...].astype(f32)[None, :]).astype(bf16)
     for i in range(message_ref.shape[0]):
         message_ref[i] = normed
 
 
-def fill_weights(target, owns, pieces):
-    count = owns[0].shape[0]
-    size = count // 4
-    for i, own in enumerate(owns):
-        target[i, :count, :] = own[...]
-    others = len(pieces) // 4
-    for place, piece in enumerate(pieces):
-        kind = place // others
-        quarter = (my_core() ^ kind // 2) * 2 + (my_blk() % 2 ^ kind % 2)
-        start = (place % others + 1) * count + quarter * size
-        for i in range(len(owns)):
-            target[i, pl.ds(pl.multiple_of(start, size), size), :] = piece[
-                i * size : (i + 1) * size, :
-            ]
-
-
-def piece_spec(pieces, part, of, whole_parts):
-    rows, depth = pieces[0].shape
-    block = (rows // whole_parts * of, depth)
-    spec = pl.BlockSpec(block, lambda *_: (part, 0), pipeline_mode=pl.Buffered(1))
-    return [spec] * len(pieces)
+def join_kernel(*refs):
+    start = 0
+    for part in refs[:-1]:
+        refs[-1][start : start + part.shape[0], :] = part[...]
+        start += part.shape[0]
+
+
+def put_weights(count, owns, arrays, out_ref):
+    rows = owns[0].shape[0]
+    half = rows // 2
+    for weight, own in enumerate(owns):
+        out_ref[weight, :rows, :] = own[...]
+    pair = lax.axis_index("dp") // 2 % 2
+    for place, array in enumerate(arrays):
+        weight = (my_core() ^ place // 4) * 2 + (pair ^ place // 2 % 2)
+        side = my_blk() % 2 ^ place % 2
+        for k in range(count):
+            start = pl.multiple_of((k + 1) * rows + side * half, half)
+            out_ref[weight, pl.ds(start, half), :] = array[k * half : (k + 1) * half, :]
 
 
 def query_kernel(blk_count, head_count, chunks_ref, c_query_ref, one_ref, self_ref, *refs):
-    pieces, (early_ref, q_ref, full_ref, weights, normed) = refs[:-5], refs[-5:]
+    early_ref, q_ref, normed = refs
     rows, depth = one_ref.shape
     width = self_ref.shape[1]
     piece = rows // head_count
-    fill_weights(weights, (c_query_ref,), pieces)
-    full_ref[...] = weights[0]
     for kb in range(blk_count):
         for i in range(head_count):
             place = (my_blk() ^ kb) * head_count + i
@@ -263,74 +279,35 @@
             early_ref[:, 2 * depth + width :] = jnp.zeros(
                 (rows, early_ref.shape[1] - 2 * depth - width), bf16
             )
-        q_ref[kb] = nt(normed[...], weights[0]).astype(bf16)
-
-
-def make_queries(chunks, c_query, normed_one, self_flat, pieces, blk_count, head_count):
-    rows, depth = normed_one.shape
-    width = self_flat.shape[1]
-    outs = (
-        shaped((rows, -(-(2 * depth + width) // 256) * 256), bf16),
-        shaped((blk_count, rows, depth), bf16),
-        shaped((depth, depth), bf16),
-    )
-    arrays = (chunks, c_query, normed_one, self_flat)
-    return pl.pallas_call(
-        functools.partial(query_kernel, blk_count, head_count),
-        grid=(1,),
-        out_shape=outs,
-        in_specs=[whole(array.shape) for array in arrays] + piece_spec(pieces, 2, 1, 3),
-        out_specs=tuple(whole(out.shape) for out in outs),
-        scratch_shapes=[pltpu.VMEM((1, depth, depth), bf16), pltpu.VMEM((rows, depth), bf16)],
-        cost_estimate=cost(4),
-        compiler_params=pltpu.CompilerParams(
-            vmem_limit_bytes=VMEM_BYTES, dimension_semantics=("arbitrary",)
-        ),
-    )(*arrays, *pieces)
-
-
-def project_kernel(enc_ref, *refs):
-    owns, pieces = refs[:2], refs[2:-5]
-    key_ref, value_ref, key_full_ref, value_full_ref, weights = refs[-5:]
+        q_ref[kb] = nt(normed[...], c_query_ref[...]).astype(bf16)
+
+
+def project_kernel(count, enc_ref, *refs):
+    owns, arrays, (key_ref, value_ref, weights_ref) = refs[:4], refs[4:-3], refs[-3:]
 
     @pl.when(pl.program_id(0) == 0)
     def _():
-        fill_weights(weights, owns, pieces)
-        key_full_ref[...] = weights[0]
-        value_full_ref[...] = weights[1]
-
-    key_ref[...] = nt(enc_ref[...], weights[0]).astype(bf16)
-    value_ref[...] = nt(enc_ref[...], weights[1]).astype(bf16)
-
-
-def project(enc, owns, pieces):
+        put_weights(count, owns, arrays, weights_ref)
+
+    key_ref[...] = nt(enc_ref[...], weights_ref[0]).astype(bf16)
+    value_ref[...] = nt(enc_ref[...], weights_ref[1]).astype(bf16)
+
+
+def project(enc, owns, arrays, count):
     slots, depth = enc.shape
     block = pl.BlockSpec((LP, depth), lambda p: (p, 0))
-    full = shaped((depth, depth), bf16)
+    weights = shaped((4, depth, depth), bf16)
     return pl.pallas_call(
-        project_kernel,
+        functools.partial(project_kernel, count),
         grid=(slots // LP,),
-        in_specs=[block] + [whole(w.shape) for w in owns] + piece_spec(pieces, 0, 2, 3),
-        out_specs=(block, block, whole(full.shape), whole(full.shape)),
-        out_shape=(shaped(enc.shape, bf16), shaped(enc.shape, bf16), full, full),
-        scratch_shapes=[pltpu.VMEM((2, depth, depth), bf16)],
+        in_specs=[block] + [whole(array.shape) for array in (*owns, *arrays)],
+        out_specs=(block, block, whole(weights.shape)),
+        out_shape=(shaped(enc.shape, bf16), shaped(enc.shape, bf16), weights),
         cost_estimate=cost(9),
         compiler_params=pltpu.CompilerParams(
             vmem_limit_bytes=VMEM_BYTES, dimension_semantics=("arbitrary",)
         ),
-    )(enc, *owns, *pieces)
-
-
-def assemble_kernel(own_ref, *refs):
-    out_ref = refs[-1]
-    others = (len(refs) - 1) // 2
-    count = own_ref.shape[0]
-    half = count // 2
-    out_ref[:count, :] = own_ref[...]
-    for k in range(others):
-        start = (k + 1) * count
-        out_ref[rows_of(start // half + my_core(), half), :] = refs[k][...]
-        out_ref[rows_of(start // half + 1 - my_core(), half), :] = refs[others + k][...]
+    )(enc, *owns, *arrays)
 
 
 def spread_pairs(values, target, kb):
@@ -501,8 +478,8 @@
     chunks = refs[:count]
     cot_ref, w_in_ref, w_back_ref = refs[count : count + 3]
     grads = refs[count + 3 : 2 * count + 3]
-    layer_ref, wide_ref, cols_ref, total = refs[2 * count + 3 :]
-    piece, depth = grads[0].shape
+    wide_ref, cols_ref, total = refs[2 * count + 3 :]
+    piece, depth = grads[0].shape[0], grads[0].shape[1] // 2
     for k, chunk in enumerate(chunks):
         mine = rows_of(my_head() ^ k, piece)
         wide_ref[mine, :depth] = chunk[:, :depth]
@@ -523,10 +500,10 @@
     wide_ref[:, depth + units : depth + 2 * units] = pre_grad
     wide_ref[:, depth + 2 * units :] = cot_ref[...]
     for k, grad in enumerate(grads):
-        grad[...] = total[rows_of(my_head() ^ k, piece), :]
+        grad[:, :depth] = total[rows_of(my_head() ^ k, piece), :].astype(bf16)
     total[...] = nn(hidden, w_back_ref[...])
-    for i in range(count):
-        layer_ref[i] = total[i * piece : (i + 1) * piece, :]
+    for k, grad in enumerate(grads):
+        grad[:, depth:] = total[rows_of(my_head() ^ k, piece), :].astype(bf16)
 
 
 def branch_kernel(head_count, width, *refs):
@@ -534,9 +511,11 @@
     second_ref, gain_ref, cot_ref, c_out_ref, cross_ref, logsum_ref = refs[
         head_count : head_count + 6
     ]
-    grad_ref, gain_grad_ref, message_ref = refs[head_count + 6 :]
+    grad_ref, gain_grad_ref, layer_ref, message_ref = refs[head_count + 6 :]
     piece, depth = second_ref.shape
-    upstream = sum(chunk[...] for chunk in chunks)
+    received = sum(chunk[...].astype(f32) for chunk in chunks)
+    upstream = received[:, :depth]
+    layer_ref[...] = (second_ref[...] + received[:, depth:]).astype(bf16)
     grad, gain_grad_ref[...] = norm_back(upstream, second_ref[...], gain_ref[...].astype(f32)[None, :])
     grad = cot_ref[rows_of(my_head(), piece), :].astype(f32) + grad
     grad_ref[...] = grad
@@ -634,7 +613,7 @@
         grid=(passages,),
         in_specs=[
             whole((blk_count, rows, depth)),
-            whole((depth, depth)),
+            spec_of(c_out),
             passage,
             passage,
             whole(chunks.shape),
@@ -672,16 +651,15 @@
         compiler_params=pltpu.CompilerParams(
             vmem_limit_bytes=VMEM_BYTES, dimension_semantics=("arbitrary",)
         ),
-    )(slots, lengths, queries, c_out, keys, values, chunks)
-
-
-def first_kernel(count, *refs):
-    chunks, first_ref, gain_ref, c_query_ref, second_grad_ref, second_ref = refs[:6]
-    layer_ref, grad_ref, gain_grad_ref = refs[6:9]
-    messages = refs[9:]
+    )(slots, lengths, queries, value_of(c_out), keys, values, chunks)
+
+
+def first_kernel(*refs):
+    chunks, first_ref, gain_ref, c_query_ref, second_grad_ref = refs[:5]
+    grad_ref, gain_grad_ref = refs[5:7]
+    messages = refs[7:]
     piece, depth = grad_ref.shape
-    width = messages[0].shape[1] - 2 * depth
-    layer = (second_ref[...] + sum(layer_ref[i] for i in range(count))).astype(bf16)
+    width = messages[0].shape[1] - depth
     grad_q = sum(chunks[i].astype(f32) for i in range(chunks.shape[0])).astype(bf16)
     upstream = nn(grad_q, c_query_ref[...])
     grad, gain_grad_ref[...] = norm_back(upstream, first_ref[...], gain_ref[...].astype(f32)[None, :])
@@ -690,22 +668,20 @@
     branch = grad.astype(bf16)
     for k, message in enumerate(messages):
         message[:, :depth] = branch
-        message[:, depth : depth + width] = grad_q[:, k * width : (k + 1) * width]
-        message[:, depth + width :] = layer
+        message[:, depth:] = grad_q[:, k * width : (k + 1) * width]
 
 
 def self_back_kernel(count, len_ref, *refs):
     chunks = refs[:count]
     w_out_ref, qkv_ref, wq_ref, wk_ref, wv_ref = refs[count : count + 5]
-    grads, (sides_ref, layer_ref, total, side_ref) = refs[count + 5 : -4], refs[-4:]
+    grads, (sides_ref, total, side_ref) = refs[count + 5 : -3], refs[-3:]
     width, depth = wq_ref.shape
     rows = side_ref.shape[0]
     piece = rows // count
     start = depth + width
     for k, chunk in enumerate(chunks):
         mine = rows_of(my_head() ^ k, piece)
-        side_ref[mine, :start] = chunk[:, :start]
-        layer_ref[mine, :] = chunk[:, start:]
+        side_ref[mine, :start] = chunk[...]
     grad_self = nt(side_ref[:, :depth], w_out_ref[...]).astype(bf16)
     allowed = causal(rows, len_ref[0].astype(f32))
     grad_q, grad_k, grad_v = [], [], []
@@ -728,34 +704,49 @@
     total[...] = nn(flat[0], wq_ref[...]) + nn(flat[1], wk_ref[...]) + nn(flat[2], wv_ref[...])
     if len(grads) == 1:
         for i in range(count):
-            grads[0][i] = total[i * piece : (i + 1) * piece, :]
+            grads[0][i] = total[i * piece : (i + 1) * piece, :].astype(bf16)
     else:
         for k, grad in enumerate(grads):
-            grad[...] = total[rows_of(my_head() ^ k, piece), :]
+            grad[...] = total[rows_of(my_head() ^ k, piece), :].astype(bf16)
     for i in range(sides_ref.shape[0]):
         sides_ref[i] = side_ref[...]
 
 
 def input_kernel(count, *refs):
     chunks = refs[:count]
-    dec_ref, gain_ref, first_grad_ref, cross_gain_ref, ffn_gain_ref, message_ref = refs[count:]
+    dec_ref, gain_ref, first_grad_ref, cross_gain_ref, ffn_gain_ref, layer_ref = refs[count:-1]
+    message_ref = refs[-1]
     if count == 1:
         chunks = [chunks[0].at[i] for i in range(chunks[0].shape[0])]
     piece, depth = chunks[0].shape
-    upstream = sum(chunk[...] for chunk in chunks)
+    upstream = sum(chunk[...].astype(f32) for chunk in chunks)
     values = dec_ref[rows_of(my_head(), piece), :].astype(f32)
     grad, self_gain = norm_back(upstream, values, gain_ref[...].astype(f32)[None, :])
-    grad = first_grad_ref[...] + grad
+    grad = (first_grad_ref[...] + grad).astype(bf16)
+    gains = gain_rows([self_gain, cross_gain_ref[...], ffn_gain_ref[...]])
+    fill = jnp.zeros((message_ref.shape[1] - 2 * piece - len(gains), depth), f32)
+    gains = jnp.concatenate([*gains, fill], axis=0).astype(bf16)
     for i in range(message_ref.shape[0]):
         message_ref[i, :piece, :] = grad
-        message_ref[i, piece:, :] = jnp.zeros((message_ref.shape[1] - piece, depth), f32)
-        message_ref[i, piece : piece + 1, :] = self_gain
-        message_ref[i, piece + 1 : piece + 2, :] = cross_gain_ref[...]
-        message_ref[i, piece + 2 : piece + 3, :] = ffn_gain_ref[...]
+        message_ref[i, piece : 2 * piece, :] = layer_ref[...]
+        message_ref[i, 2 * piece :, :] = gains
+
+
+def gain_rows(gains):
+    rows = []
+    for rest in gains:
+        for step in range(3):
+            rows.append(rest.astype(bf16).astype(f32))
+            rest = rest - rows[-1]
+    return rows
+
+
+def gain_sums(rows):
+    return [jnp.sum(rows[3 * i : 3 * i + 3, :], axis=0, keepdims=True) for i in range(3)]
 
 
 def place_kernel(count, *refs):
-    chunks, (out_ref, gain_ref) = refs[:-2], refs[-2:]
+    chunks, (out_ref, gain_ref, layer_ref) = refs[:-3], refs[-3:]
     piece = out_ref.shape[0] // count
     if len(chunks) == 1:
         chunks = [chunks[0].at[i] for i in range(count)]
@@ -763,8 +754,11 @@
     else:
         places = [my_head() ^ k for k in range(count)]
     for place, chunk in zip(places, chunks):
-        out_ref[rows_of(place, piece), :] = chunk[:piece, :]
-    gain_ref[...] = sum(chunk[piece:, :] for chunk in chunks)
+        out_ref[rows_of(place, piece), :] = chunk[:piece, :].astype(f32)
+        layer_ref[rows_of(place, piece), :] = chunk[piece : 2 * piece, :]
+    gains = gain_sums(sum(chunk[2 * piece :, :].astype(f32) for chunk in chunks))
+    fill = jnp.zeros((gain_ref.shape[0] - len(gains), gain_ref.shape[1]), f32)
+    gain_ref[...] = jnp.concatenate([*gains, fill], axis=0)
 
 
 def weight_kernel(early_count, late_count, width, *refs):
@@ -869,14 +863,14 @@
     return pl.pallas_call(
         encoder_grad_kernel,
         grid=(slots // LP,),
-        in_specs=[block, block, whole(key_full.shape), whole(value_full.shape)],
+        in_specs=[block, block, spec_of(key_full), spec_of(value_full)],
         out_specs=block,
         out_shape=shaped((slots, depth), f32),
         cost_estimate=cost(7 * CFG["t_cost"]),
         compiler_params=pltpu.CompilerParams(
             vmem_limit_bytes=VMEM_BYTES, dimension_semantics=("arbitrary",)
         ),
-    )(key_grads, value_grads, key_full, value_full)
+    )(key_grads, value_grads, value_of(key_full), value_of(value_full))
 
 
 def share_kernel(shares_ref, blocks_ref, cross_ref):
@@ -890,12 +884,7 @@
 def spread_kernel(blocks_ref, cross_ref, gains_ref, out_ref):
     size, more = blocks_ref.shape[1], cross_ref.shape[0]
     block = sum(blocks_ref[i].astype(f32) for i in range(blocks_ref.shape[0])).astype(bf16)
-    pieces = []
-    for i in range(3):
-        rest = gains_ref[i : i + 1, :]
-        for step in range(3):
-            pieces.append(rest.astype(bf16).astype(f32))
-            rest = rest - pieces[-1]
+    pieces = gain_rows([gains_ref[i : i + 1, :] for i in range(3)])
     fill = out_ref.shape[1] - size - more - len(pieces)
     pieces.append(jnp.zeros((fill, out_ref.shape[2]), f32))
     tail = jnp.concatenate([cross_ref[...].astype(f32), *pieces], axis=0).astype(bf16)
@@ -917,8 +906,8 @@
         target[part * size : (part + 1) * size, :] = share[:size]
         cross_ref[device * more : (device + 1) * more, :] = share[size : size + more]
         total = total + share[size + more :]
-    for i in range(3):
-        gains_ref[i : i + 1, :] = jnp.sum(total[3 * i : 3 * i + 3, :], axis=0, keepdims=True)
+    for i, gain in enumerate(gain_sums(total)):
+        gains_ref[i : i + 1, :] = gain
     gains_ref[3:, :] = jnp.zeros((gains_ref.shape[0] - 3, gains_ref.shape[1]), f32)
 
 
@@ -965,14 +954,6 @@
 def plane_gather(array):
     chips = [array] + [to_chip(array, k) for k in (1, 2, 3)]
     return chips + across_core(chips)
-
-
-def plane_gather_wide(array, beside, small):
-    if not small:
-        return [array]
-    both = jnp.concatenate([array, beside], axis=0)
-    far = partner(both, "dp", 2)
-    return [both, far]
 
 
 def body(
@@ -1016,60 +997,65 @@
     slots = lax.dynamic_slice_in_dim(passage_owner, head_place * passages, passages) ^ blk_place
     lengths = lax.dynamic_slice_in_dim(passage_len, head_place * passages, passages)
 
+    half = width // 2
+    sides = [
+        lax.dynamic_slice_in_dim(weight, blk_place % 2 * half, half, 0)
+        for weight in (c_key, c_value, c_query, c_out)
+    ]
+    pair = lax.axis_index("dp") // 2 % 2
+    mine = jnp.where(
+        core == 0, jnp.where(pair == 0, *sides[:2]), jnp.where(pair == 0, *sides[2:])
+    )
+    near = [partner(mine, "head", k) for k in range(1, head_count)]
     normed_one, self_qkv, self_flat, *partials = call_self(
-        dec_in, dec_len, gain_one, w_query, w_key, w_value, w_out, head_count
-    )
-    quarter = (core * 2 + blk_place % 2) * (width // 4)
-    if CFG["s_w"] == 1:
-        quarter = after(quarter, self_flat)
-    pieces = jnp.concatenate(
-        [
-            lax.dynamic_slice_in_dim(weight, quarter, width // 4, 0)
-            for weight in (c_key, c_value, c_query)
-        ],
-        axis=0,
-    )
-    pieces = [partner(pieces, "head", k) for k in range(1, head_count)]
-    if CFG["s_y"] == 1:
-        pieces = hold(pieces, self_flat)
-    near = pieces
-    beside = [partner(piece_, "blk", 1) for piece_ in pieces]
-    pieces = pieces + beside + across_core(pieces) + across_core(beside)
+        after(dec_in, mine) if CFG["s_o"] == 1 else dec_in,
+        dec_len, gain_one, w_query, w_key, w_value, w_out, head_count
+    )
     partials = swap_parts(partials)
-    if CFG["s_p"] == 2:
-        partials = hold(partials, *near)
-    elif CFG["s_p"] == 3:
-        partials = hold(partials, near[0])
+    if CFG["s_a"] == 1:
+        near = hold(near, partials[1])
+    elif CFG["s_a"] == 2:
+        *near, self_flat = hold([*near, self_flat])
+    (near,) = call(
+        join_kernel, [shaped((len(near) * half, depth), bf16)], [], near, micros=0.3
+    )
+    beside = partner(near, "blk", 1)
+    arrays = [near, beside, partner(near, "dp", 2)]
+    if CFG["s_xy"] == 1 and blk_count == 2:
+        arrays.append(partner(near, ("dp", "blk"), 5))
+    else:
+        arrays.append(partner(beside, "dp", 2))
+    arrays = arrays + across_core(arrays)
     first, message = call(
         functools.partial(normed_kernel, head_count),
         [shaped((piece, depth), f32), shaped((chunk_count, piece, depth), bf16)],
         [],
-        [*partials, dec_in, gain_two],
-    )
-    if CFG["s_p"] == 1:
-        (message,) = hold([message], *near)
-    elif CFG["s_p"] == 4:
-        (message,) = hold([message], near[0])
+        [*hold(partials, slots, lengths), dec_in, gain_two],
+    )
+    if CFG["s_a"] == 3:
+        message, near, beside = hold([message, near, beside])
     chunks = exchange(message, "blk", "head")
-    enc_keys, enc_values, key_full, value_full = project(enc_out, (c_key, c_value), pieces)
-    early, queries, query_full = make_queries(
-        chunks, c_query, normed_one, self_flat, pieces, blk_count, head_count
-    )
-    c_gate = {0: [queries], 1: [queries, enc_keys]}[CFG["s_c"]]
-    mine = lax.dynamic_slice_in_dim(c_out, after(core, *c_gate) * half, half, 0)
-    cross_out = [partner(mine, "head", k) for k in range(1, head_count)]
-    early_beside = partner(after(early, *c_gate), "blk", 1)
-
+    enc_keys, enc_values, weights = project(
+        enc_out, (c_key, c_value, c_query, c_out), arrays, head_count - 1
+    )
+    key_full, value_full, query_full, cross_out_full = [Weight(weights, i) for i in range(4)]
+    early, queries = call(
+        functools.partial(query_kernel, blk_count, head_count),
+        [
+            shaped((rows, -(-(2 * depth + width) // 256) * 256), bf16),
+            shaped((blk_count, rows, depth), bf16),
+        ],
+        [],
+        [chunks, query_full, normed_one, self_flat],
+        [pltpu.VMEM((rows, depth), bf16)],
+    )
+    if CFG["e_y"] == 0:
+        early_beside = partner(after(early, enc_keys), "blk", 1)
     partials = cross_forward(
         slots, lengths, queries, enc_keys, enc_values, head_count, width
     )
-    partials, early_beside, *cross_out = hold([partials, early_beside, *cross_out])
-    (cross_out_full,) = call(
-        assemble_kernel,
-        [shaped((depth, depth), bf16)],
-        [],
-        [c_out, *cross_out, *across_core(cross_out)],
-    )
+    if CFG["e_y"] == 0:
+        partials, early_beside = hold([partials, early_beside])
     cross, second, logsum, *messages = call(
         functools.partial(combine_kernel, width),
         [
@@ -1081,12 +1067,19 @@
         [],
         [exchange(partials, "blk", "head"), first, cross_out_full, gain_three],
     )
+    if CFG["e_y"] == 0:
+        early = [early, early_beside] if small else [early]
+        if small:
+            early += [partner(part, "dp", 2) for part in hold(early, second)]
+    else:
+        early = [after(early, second)]
+        if small:
+            early += [partner(early[0], "blk", 1), partner(early[0], "dp", 2)]
     chunks = swap_parts(messages)
     outs = call(
         functools.partial(ffn_kernel, head_count),
-        [shaped((piece, depth), f32)] * head_count
+        [shaped((piece, 2 * depth), bf16)] * head_count
         + [
-            shaped((head_count, piece, depth), f32),
             shaped((rows, 2 * depth + 2 * units), bf16),
             shaped((rows, width), bf16),
         ],
@@ -1094,28 +1087,30 @@
         [*chunks, cotangent, w_in, w_back],
         [pltpu.VMEM((rows, depth), f32)],
     )
-    layer, wide, cross_cols = outs[head_count:]
+    wide, cross_cols = outs[head_count:]
     wide_beside = partner(wide, "blk", 1)
-    if CFG["m_early"] == 0:
-        early = plane_gather_wide(after(early, wide), early_beside, small)
+    wide = [wide, wide_beside, partner(wide, "dp", 2)] if small else [wide]
+    if small and CFG["e_y"] == 1:
+        early.append(partner(after(early[1], wide[0]), "dp", 2))
     upstream = swap_parts(outs[:head_count])
-    grad_second, gain_ffn_part, message = call(
+    grad_second, gain_ffn_part, layer, message = call(
         functools.partial(branch_kernel, head_count, width),
         [
             shaped((piece, depth), f32),
             shaped((1, depth), f32),
+            shaped((piece, depth), bf16),
             shaped((chunk_count, piece, depth + STATS), bf16),
         ],
         [],
         [*upstream, second, gain_three, cotangent, cross_out_full, cross, logsum],
     )
-    message, wide, wide_beside = hold([message, wide, wide_beside])
+    if small:
+        if CFG["m_e"] == 1:
+            message, *early = hold([message, *early])
     branches = exchange(message, "blk", "head")
-    branches, layer = hold([branches, layer])
-    wide = plane_gather_wide(wide, wide_beside, small)
-    if CFG["m_early"] == 1:
-        early = plane_gather_wide(after(early, message), early_beside, small)
-    layer = exchange(layer, "head")
+    if small and CFG["e_c"] == 1:
+        early = early + across_core(early)
+        branches, *early = hold([branches, *early])
     query_grads, branch_two, enc_key_grads, enc_value_grads = cross_backward(
         slots,
         lengths,
@@ -1127,95 +1122,146 @@
         head_count,
         width,
     )
-    if CFG["m_early"] == 2:
-        query_grads, layer = hold([query_grads, layer])
-        early = plane_gather_wide(after(early, query_grads), early_beside, small)
-    else:
-        query_grads, layer, *early = hold([query_grads, layer, *early])
     query_grads = exchange(query_grads, "blk", "head")
 
+    if small and CFG["w_x"] == 1:
+        enc_key_grads, enc_value_grads = hold([enc_key_grads, enc_value_grads], *wide)
+        wide.append(partner(after(wide[1], enc_key_grads), "dp", 2))
+    elif small:
+        wide.append(partner(wide[1], "dp", 2))
     shares = projection_grads(
         enc_key_grads, enc_value_grads, enc_out, cross_cols, branch_two, plane, head_count
     )
-    if CFG["t_cs"] == 1:
+    if small and CFG["w_c"] == 1:
+        wide_there = across_core(wide[:3])
+        query_grads, shares, *wide_there = hold([query_grads, shares, *wide_there])
+    elif CFG["t_cs"] == 1:
         query_grads, shares = hold([query_grads, shares])
-    if CFG["w_k8"] == 1:
-        (query_grads,) = hold([query_grads], *wide[1:])
     grad_first, gain_cross_part, *messages = call(
-        functools.partial(first_kernel, head_count),
+        first_kernel,
         [shaped((piece, depth), f32), shaped((1, depth), f32)]
-        + [shaped((piece, 2 * depth + width), bf16)] * head_count,
+        + [shaped((piece, depth + width), bf16)] * head_count,
         [],
-        [query_grads, first, gain_two, query_full, grad_second, second, layer],
-    )
+        [query_grads, first, gain_two, query_full, grad_second],
+    )
+    if CFG["w_xy"] == 1:
+        messages = hold(messages, *wide)
     chunks = swap_parts(messages)
     if small:
-        if CFG["t_shq"] == 1:
+        if CFG["sh_q"] == 1:
+            shares = after(shares, chunks[1])
+        elif CFG["sh_q"] == 2:
+            shares = after(shares, chunks[-1])
+        elif CFG["t_shq"] == 1:
             shares = after(shares, messages[0])
         shares = exchange(shares, "dp", "blk")
-        wide = wide + across_core(wide)
-        early = early + across_core(early)
-    else:
-        early = early[:1]
+    if CFG["e_p"] == 4:
+        grad_enc = encoder_grads(
+            *hold([enc_key_grads, enc_value_grads], messages[0]), key_full, value_full
+        )
+        chunks = hold(chunks, grad_enc)
     outs = call(
         functools.partial(self_back_kernel, head_count),
         (
-            [shaped((piece, depth), f32)] * head_count
+            [shaped((piece, depth), bf16)] * head_count
             if CFG["t_rsz"] == "perm"
-            else [shaped((head_count, piece, depth), f32)]
+            else [shaped((head_count, piece, depth), bf16)]
         )
         + [
-            shaped((plane if small else 1, rows, depth + 4 * width), bf16),
-            shaped((rows, depth), bf16),
+            shaped(
+                (plane if small and CFG["t_late"] == "a2a" else 1, rows, depth + 4 * width), bf16
+            )
         ],
         [dec_len],
         [*chunks, w_out, self_qkv, w_query, w_key, w_value],
         [pltpu.VMEM((rows, depth), f32), pltpu.VMEM((rows, depth + 4 * width), bf16)],
     )
-    late, layer_out = outs[-2:]
-    shares_gate = {5: [chunks[len(chunks) > 1]], 0: [], 1: [late], 2: []}[CFG["t_sh"]]
-    shares, *wide = hold([shares, *wide], *shares_gate)
+    late = outs[-1]
+    if small:
+        if CFG["e_c"] == 0:
+            early = hold(early, late)
+            early = early + across_core(early)
+        if CFG["w_c"] == 1:
+            wide = wide + wide_there + across_core(hold(wide[3:], late))
+        else:
+            wide = hold(wide, late)
+            wide = wide + across_core(wide)
     if not small:
         late = [late.reshape(late.shape[1:])]
     elif CFG["t_late"] == "a2a":
         late = [exchange(late, "dp", "blk")]
     else:
-        late = plane_gather(late.reshape(late.shape[1:]))
+        late = late.reshape(late.shape[1:])
+        late = [late, partner(late, "blk", 1), partner(late, "dp", 2)]
+        if CFG["l_d"] == 1:
+            late.append(partner(late[0], ("dp", "blk"), 5))
     if CFG["t_rsz"] == "perm":
         upstream = swap_parts(outs[:head_count])
     else:
         upstream = [exchange(outs[0], "head")]
-    if CFG["t_enc"] == 0:
-        enc_grad_pair = hold([enc_key_grads, enc_value_grads], upstream[-1])
-        grad_enc = encoder_grads(*enc_grad_pair, key_full, value_full)
+    if small and CFG["l_p"] == 2:
+        joined = hold([*upstream, *late])
+        upstream, late = joined[: len(upstream)], joined[len(upstream) :]
+        late.append(partner(late[1], "dp", 2))
+    if CFG["t_shg"] == 1:
+        (shares,) = hold([shares], *upstream)
+    elif CFG["t_shg"] == 2:
+        (shares,) = hold([shares], upstream[1])
     (message,) = call(
         functools.partial(input_kernel, len(upstream)),
-        [shaped((head_count if CFG["t_agz"] == "a2a" else 1, piece + 8, depth), f32)],
+        [shaped((head_count if CFG["t_agz"] == "a2a" else 1, 2 * piece + 16, depth), bf16)],
         [],
-        [*upstream, dec_in, gain_one, grad_first, gain_cross_part, gain_ffn_part],
+        [*upstream, dec_in, gain_one, grad_first, gain_cross_part, gain_ffn_part, layer],
         micros=3 * CFG["t_cost"],
     )
-    if CFG["t_latep"] == 1:
-        message = after(message, *late[: len(late) // 2 + 1])
-    if CFG["t_sh"] == 2:
-        shares = after(shares, message)
+    if small and CFG["t_late"] == "perm" and CFG["l_p"] == 1:
+        message, *late = hold([message, *late])
+        late.append(partner(late[1], "dp", 2))
     if CFG["t_agz"] == "perm":
         chunks = share_heads(message.reshape(message.shape[1:]))
     else:
         chunks = [exchange(message, "head")]
-    if CFG["t_latep"] == 2:
-        chunks = hold(chunks, *late[: len(late) // 2 + 1])
-    if CFG["t_enc"] == 1:
-        enc_grad_pair = hold([enc_key_grads, enc_value_grads], message)
-        grad_enc = encoder_grads(*enc_grad_pair, key_full, value_full)
-    elif CFG["t_enc"] == 2:
-        grad_enc = encoder_grads(enc_key_grads, enc_value_grads, key_full, value_full)
-    elif CFG["t_enc"] == 3:
-        enc_grad_pair = hold([enc_key_grads, enc_value_grads], chunks[-1])
-        grad_enc = encoder_grads(*enc_grad_pair, key_full, value_full)
-    grad_in, gains = call(
+    if CFG["t_shg"] == 3:
+        shares = after(shares, chunks[1])
+    elif CFG["t_shg"] == 4:
+        shares = after(shares, message)
+    pair = [enc_key_grads, enc_value_grads]
+    if CFG["e_p"] == 1:
+        pair = hold(pair, *upstream)
+    elif CFG["e_p"] == 2:
+        pair = hold(pair, message)
+    elif CFG["e_p"] == 3:
+        pair = hold(pair, chunks[1])
+    if CFG["e_p"] != 4:
+        grad_enc = encoder_grads(*pair, key_full, value_full)
+        if CFG["e_p"] > 0:
+            chunks = hold(chunks, grad_enc)
+    if CFG["b_p"] == 3:
+        wide = hold(wide, message)
+    elif CFG["b_p"] == 4:
+        wide = hold(wide, upstream[0])
+    broad = call(
+        functools.partial(wide_kernel, len(wide)),
+        [shaped((depth, units), f32), shaped((units, depth), f32)],
+        [],
+        wide,
+        [pltpu.VMEM((sum(part.shape[0] for part in wide), wide[0].shape[1]), bf16)],
+        8 * CFG["t_cost"],
+    )
+    if CFG["b_p"] == 3 or CFG["b_p"] == 4:
+        chunks = hold(chunks, broad[0])
+    if small and CFG["l_p"] == 2 and CFG["l_xy"] == 1:
+        *chunks, late[-1] = hold([*chunks, late[-1]])
+    if small and CFG["t_late"] == "perm" and CFG["l_p"] == 0:
+        joined = hold([*chunks, *late])
+        chunks, late = joined[: len(chunks)], joined[len(chunks) :]
+        if len(late) == 3:
+            late.append(partner(late[1], "dp", 2))
+    elif CFG["l_xy"] == 1:
+        chunks = hold(chunks, late[-1])
+    grad_in, gains, layer_out = call(
         functools.partial(place_kernel, head_count),
-        [shaped((rows, depth), f32), shaped((8, depth), f32)],
+        [shaped((rows, depth), f32), shaped((8, depth), f32), shaped((rows, depth), bf16)],
         [],
         chunks,
         micros=3 * CFG["t_cost"],
@@ -1232,6 +1278,14 @@
             micros=3 * CFG["t_cost"],
         )
         blocks = exchange(blocks, "head")
+        if CFG["t_p"] == 4:
+            blocks, late[3] = hold([blocks, late[3]])
+        if CFG["t_p"] == 1:
+            (blocks,) = hold([blocks], grad_enc, broad[0], *late)
+        elif CFG["t_p"] == 2:
+            (blocks,) = hold([blocks], *late)
+        elif CFG["t_p"] == 3:
+            (blocks,) = hold([blocks], grad_enc, *late)
         (shares,) = call(
             spread_kernel,
             [shaped((plane, width // 4 + width // plane + 24, depth), bf16)],
@@ -1255,18 +1309,8 @@
         grad_c_out = shares[2 * depth :]
 
 
-    if CFG["t_broad"] == 1:
-        wide = hold(wide, message)
-    elif CFG["t_broad"] == 2:
-        wide = hold(wide, grad_in)
-    broad = call(
-        functools.partial(wide_kernel, len(wide)),
-        [shaped((depth, units), f32), shaped((units, depth), f32)],
-        [],
-        wide,
-        [pltpu.VMEM((sum(part.shape[0] for part in wide), wide[0].shape[1]), bf16)],
-        8 * CFG["t_cost"],
-    )
+    if small and CFG["t_late"] == "perm":
+        late = late + across_core(late)
     slim = call(
         functools.partial(weight_kernel, len(early), len(late), width),
         [shaped((width, depth), f32)] * 5,

time: 332 us -> 273 us (0.82)
  waiting for transfers between devices: 103 us -> 62.1 us
  local copies, waits for them, and re-layouts: 18.3 us -> 2.71 us
  starting transfers between devices: 83.3 us -> 75.2 us
  blocking collectives: 14.9 us -> 20 us
    ppermute x44 -> x49, waiting for transfers between devices: 71.5 us -> 48.1 us  [partner(): return lax.ppermute(array, axis, [(i, i ^ by) for i in range(size)])]
    all_to_all x8 -> x6, waiting for transfers between devices: 31.6 us -> 14 us  [exchange(): return lax.all_to_all(array, axes, 0, 0)]
    unnamed x106 -> x0, local copies, waits for them, and re-layouts: 12.3 us -> none
    all_to_all x8 -> x6, starting transfers between devices: 35.1 us -> 26.4 us  [exchange(): return lax.all_to_all(array, axes, 0, 0)]
    all_to_all x1, blocking collectives: 14.9 us -> 20 us  [exchange(): return lax.all_to_all(array, axes, 0, 0)]
    pallas_call x2 -> x1, Pallas kernels: 13.2 us -> 11.1 us  [project(): pl.pallas_call(functools.partial(project_kernel, count), grid=(slots // L...]
    pallas_call x14 -> x15, Pallas kernels: 48.2 us -> 49.2 us  [call(): pl.pallas_call(kernel, grid=(1,), out_shape=tuple(outs), in_specs=[smem()...]
    ppermute x44 -> x49, starting transfers between devices: 48.2 us -> 48.8 us  [partner(): return lax.ppermute(array, axis, [(i, i ^ by) for i in range(size)])]
  transfers between devices with their start and end apart: 52 -> 55, of which waited for: 25 -> 27; matrix products, arithmetic and copies ran while one was open for 2% -> 1% of each run, Pallas kernels for 28% -> 31%
where the time goes in v3:
time: 273 us; the launch traced here: 271 us
  Pallas kernels  106 us (39%)
  starting transfers between devices  75.2 us (28%)
  waiting for transfers between devices  62.1 us (23%)
  blocking collectives  20 us (7%)
  other arithmetic  3.1 us (1%)
    pallas_call x15, Pallas kernels, call(): pl.pallas_call(kernel, grid=(1,), out_shape=tuple(outs), in_specs=[smem()...  49.2 us
    ppermute x49, starting transfers between devices, partner(): return lax.ppermute(array, axis, [(i, i ^ by) for i in range(size)])  48.8 us
    ppermute x49, waiting for transfers between devices, partner(): return lax.ppermute(array, axis, [(i, i ^ by) for i in range(size)])  48.1 us
    all_to_all x6, starting transfers between devices, exchange(): return lax.all_to_all(array, axes, 0, 0)  26.4 us
    all_to_all x1, blocking collectives, exchange(): return lax.all_to_all(array, axes, 0, 0)  20 us
    all_to_all x6, waiting for transfers between devices, exchange(): return lax.all_to_all(array, axes, 0, 0)  14 us
    pallas_call x1, Pallas kernels, cross_backward(): pl.pallas_call(functools.partial(cross_backward_kernel, blk_count, head_c...  13.3 us
    pallas_call x1, Pallas kernels, project(): pl.pallas_call(functools.partial(project_kernel, count), grid=(slots // L...  11.1 us
  transfers between devices with their start and end apart: 55, of which 27 were waited for; matrix products, arithmetic and copies ran while one was open for 1% of the time, Pallas kernels for 31%

profile of v3, /device:TPU:0, one launch (start us, length us, event | category | flops | bytes accessed | tf_op | source)
XLA Modules:
  0.0 271.1 jit_solution(6849633835316608863)
XLA Ops:
  2.6 5.0 %collective-permute-start.5 = (bf16[96,768]{1,0:T(8,128)(2,1)}, bf16[96,768]{1,0:T(8,128)(2,1)}, u32[]{:S(2)}, u32[]{:S(2)}) collective-permute-start(bf16[96,768]{1,0:T(8,128)(2,1)} %select_select_fusion), channel_id=1, source_target_pairs={{0,3},{1,2},{2,1},{3,0},{4,7},{5,6},{6,5},{7,4},{8,11},{9,10},{10,... | collective-permute-start | bytes 442376 | tf_op jit(solution)/shard_map/ppermute | solution.py:925
  8.8 3.8 %shard_map.306 = (bf16[128,768]{1,0:T(8,128)(2,1)}, bf16[128,576]{1,0:T(8,128)(2,1)}, bf16[128,192]{1,0:T(8,128)(2,1)}, bf16[32,768]{1,0:T(8,128)(2,1)}, bf16[32...) custom-call(bf16[128,768]{1,0:T(8,128)(2,1)} %refs_4_.7, s32[1]{0:T(128)S(6)} %copy.35.len_ref, ...), custom_call_target="tpu_custom_call" | custom-call | bytes 300000 | tf_op jit(solution)/shard_map/pallas_call | solution.py:218
  14.1 4.4 %collective-permute-done.refs_1_ = bf16[32,768]{1,0:T(8,128)(2,1)} collective-permute-done((bf16[32,768]{1,0:T(8,128)(2,1)}, bf16[32,768]{1,0:T(8,128)(2,1)}, u32[]{:S(2)}, u32[]{:S(2)}) %collective-permute-start) | collective-permute-done | bytes 49184 | tf_op jit(solution)/shard_map/ppermute | solution.py:925
  34.0 5.0 %all-to-all-start = ((bf16[8,32,768]{2,1,0:T(8,128)(2,1)}), bf16[8,32,768]{2,1,0:T(8,128)(2,1)}, u32[]{:S(2)}, u32[]{:S(2)}) async-start(bf16[8,32,768]{2,1,0:T(8,128)(2,1)} %get-tuple-element.149), calls=%async_computation | async-start | bytes 786432 | tf_op jit(solution)/shard_map/all_to_all | solution.py:934
  39.6 4.7 %collective-permute-done.7.refs_6_ = bf16[288,768]{1,0:T(8,128)(2,1)} collective-permute-done((bf16[288,768]{1,0:T(8,128)(2,1)}, bf16[288,768]{1,0:T(8,128)(2,1)}, u32[]{:S(2)}, u32[]{:S(2)}) %collective-permute-start.7) | collective-permute-done | bytes 442400 | tf_op jit(solution)/shard_map/ppermute | solution.py:925
  48.5 11.1 %shard_map.309 = (bf16[1920,768]{1,0:T(8,128)(2,1)}, bf16[1920,768]{1,0:T(8,128)(2,1)}, bf16[4,768,768]{2,1,0:T(8,128)(2,1)}) custom-call(bf16[1920,768]{1,0:T(8,128)(2,1)} %refs_2_.4, bf16[192,768]{1,0:T(8,128)(2,1)} %refs_0_.1, bf16[192,768]{1,0:T(8,128)(2,1)} %refs_1_.1, bf16[192,768]{1,0:T(8,128)(2,1)} %refs_2_.3, bf16[192,768]{1,0:T(8,128)(2,1)} %refs_3_.2, ...), custom_call_target="tpu_custom_call" | custom-call | bytes 27000000 | tf_op jit(solution)/shard_map/pallas_call | solution.py:300
  62.7 9.6 %shard_map.311 = bf16[8,32,896]{2,1,0:T(8,128)(2,1)} custom-call(s32[5]{0:T(128)} %dynamic-slice_xor_fusion.refs_0_, s32[5]{0:T(128)} %dynamic_slice.19.refs_1_, bf16[2,128,768]{2,1,0:T(8,128)(2,1)} %get-tuple-element.156.refs_2_, bf16[1920,768]{1,0:T(8,128)(2,1)} %get-tuple-element.157.refs_3_.refs_4_, bf16[1920,768]{1,0:T(8,128)(2,1)} %get-tuple-element.158.refs_4_.refs_5_), custom_call_target="tpu_custom_call" | custom-call | bytes 45000000 | tf_op jit(solution)/shard_map/pallas_call | solution.py:429
  72.2 20.0 %all_to_all.35.refs_0_ = bf16[8,32,896]{2,1,0:T(8,128)(2,1)} all-to-all(bf16[8,32,896]{2,1,0:T(8,128)(2,1)} %shard_map.311), channel_id=1, replica_groups=mesh['dp'=4,'blk'=2,'head'=4] {'blk','head'}, dimensions={0} | all-to-all | bytes 917504 | tf_op jit(solution)/shard_map/all_to_all | solution.py:934
  104.3 4.0 %shard_map.313 = (bf16[32,1536]{1,0:T(8,128)(2,1)}, bf16[32,1536]{1,0:T(8,128)(2,1)}, bf16[32,1536]{1,0:T(8,128)(2,1)}, bf16[32,1536]{1,0:T(8,128)(2,1)}, bf16[1...) custom-call(bf16[32,960]{1,0:T(8,128)(2,1)} %get-tuple-element.160.refs_0_, ...), custom_call_target="tpu_custom_call" | custom-call | bytes 10500000 | tf_op jit(solution)/shard_map/pallas_call | solution.py:102
  123.6 4.3 %all-to-all-start.2 = ((bf16[8,32,896]{2,1,0:T(8,128)(2,1)}), bf16[8,32,896]{2,1,0:T(8,128)(2,1)}, u32[]{:S(2)}, u32[]{:S(2)}) async-start(bf16[8,32,896]{2,1,0:T(8,128)(2,1)} %get-tuple-element.176), calls=%async_computation.2 | async-start | bytes 917504 | tf_op jit(solution)/shard_map/all_to_all | solution.py:934
  130.2 10.6 %all-to-all-done.2.refs_6_ = bf16[8,32,896]{2,1,0:T(8,128)(2,1)} async-done(((bf16[8,32,896]{2,1,0:T(8,128)(2,1)}), bf16[8,32,896]{2,1,0:T(8,128)(2,1)}, u32[]{:S(2)}, u32[]{:S(2)}) %all-to-all-start.2) | async-done | bytes 458784 | tf_op jit(solution)/shard_map/all_to_all | solution.py:934
  140.7 13.3 %shard_map.315 = (bf16[8,32,768]{2,1,0:T(8,128)(2,1)}, bf16[128,768]{1,0:T(8,128)(2,1)}, bf16[1920,768]{1,0:T(8,128)(2,1)}, bf16[1920,768]{1,0:T(8,128)(2,1)}) custom-call(s32[5]{0:T(128)} %dynamic-slice_xor_fusion.refs_0_, s32[5]{0:T(128)} %dynamic_slice.19.refs_1_, bf16[2,128,768]{2,1,0:T(8,128)(2,1)} %get-tuple-element.156.refs_2_, ...), custom_call_target="tpu_custom_call" | custom-call | bytes 48000000 | tf_op jit(solution)/shard_map/pallas_call | solution.py:641
  154.7 4.1 %all-to-all-start.3 = ((bf16[8,32,768]{2,1,0:T(8,128)(2,1)}), bf16[8,32,768]{2,1,0:T(8,128)(2,1)}, u32[]{:S(2)}, u32[]{:S(2)}) async-start(bf16[8,32,768]{2,1,0:T(8,128)(2,1)} %get-tuple-element.177), calls=%async_computation.3 | async-start | bytes 786432 | tf_op jit(solution)/shard_map/all_to_all | solution.py:934
  158.8 10.0 %shard_map.316 = bf16[8,224,768]{2,1,0:T(8,128)(2,1)} custom-call(bf16[1920,768]{1,0:T(8,128)(2,1)} %get-tuple-element.195.refs_0_.keys_ref, bf16[1920,768]{1,0:T(8,128)(2,1)} %get-tuple-element.196.refs_1_.values_ref, bf16[1920,768]{1,0:T(8,128)(2,1)} %refs_2_.4, bf16[128,192]{1,0:T(8,128)(2,1)} %get-tuple-element.182.refs_3_, ...), custom_call_target="tpu_custom_call" | custom-call | bytes 12000000 | tf_op jit(solution)/shard_map/pallas_call | solution.py:842
  171.7 4.4 %all-to-all-start.4 = ((bf16[8,224,768]{2,1,0:T(8,128)(2,1)}), bf16[8,224,768]{2,1,0:T(8,128)(2,1)}, u32[]{:S(2)}, u32[]{:S(2)}) async-start(bf16[8,224,768]{2,1,0:T(8,128)(2,1)} %shard_map.316), calls=%async_computation.4 | async-start | bytes 5505024 | tf_op jit(solution)/shard_map/all_to_all | solution.py:934
  180.6 9.6 %shard_map.318 = f32[1920,768]{1,0:T(8,128)} custom-call(bf16[1920,768]{1,0:T(8,128)(2,1)} %get-tuple-element.195.refs_0_.keys_ref, bf16[1920,768]{1,0:T(8,128)(2,1)} %get-tuple-element.196.refs_1_.values_ref, bf16[4,768,768]{2,1,0:T(8,128)(2,1)} %get-tuple-element.153.c_query_ref.refs_2_.refs_7_.refs_3_.key_ref.value_ref, ...), custom_call_target="tpu_custom_call" | custom-call | bytes 1050000 | tf_op jit(solution)/shard_map/pallas_call | solution.py:863
  190.3 4.2 %shard_map.319 = (bf16[32,768]{1,0:T(8,128)(2,1)}, bf16[32,768]{1,0:T(8,128)(2,1)}, bf16[32,768]{1,0:T(8,128)(2,1)}, bf16[32,768]{1,0:T(8,128)(2,1)}, bf16[1,128,1536]{2,1,0:T(8,128)(2,1)}) custom-call(s32[1]{0:T(128)S(6)} %copy.35.len_ref, bf16[32,960]{1,0:T(8,128)(2,1)} %get-tuple-element.197.refs_0_, bf16[32,960]{1,0:T(8,128)(2,1)} %collective-permute-done.25.refs_1_, ...), custom_call_target="tpu_custom_call" | custom-call | bytes 10500000 | tf_op jit(solution)/shard_map/pallas_call | solution.py:102
  196.1 3.8 %collective-permute-done.28.refs_1_ = bf16[32,768]{1,0:T(8,128)(2,1)} collective-permute-done((bf16[32,768]{1,0:T(8,128)(2,1)}, bf16[32,768]{1,0:T(8,128)(2,1)}, u32[]{:S(2)}, u32[]{:S(2)}) %collective-permute-start.28) | collective-permute-done | bytes 49184 | tf_op jit(solution)/shard_map/ppermute | solution.py:925
  201.8 4.0 %collective-permute-done.29.refs_2_ = bf16[32,768]{1,0:T(8,128)(2,1)} collective-permute-done((bf16[32,768]{1,0:T(8,128)(2,1)}, bf16[32,768]{1,0:T(8,128)(2,1)}, u32[]{:S(2)}, u32[]{:S(2)}) %collective-permute-start.29) | collective-permute-done | bytes 49184 | tf_op jit(solution)/shard_map/ppermute | solution.py:925
  213.9 5.2 %collective-permute-done.31.refs_1_ = bf16[80,768]{1,0:T(8,128)(2,1)} collective-permute-done((bf16[80,768]{1,0:T(8,128)(2,1)}, bf16[80,768]{1,0:T(8,128)(2,1)}, u32[]{:S(2)}, u32[]{:S(2)}) %collective-permute-start.31) | collective-permute-done | bytes 122912 | tf_op jit(solution)/shard_map/ppermute | solution.py:925
  221.9 4.1 %all-to-all-start.5 = ((bf16[4,48,768]{2,1,0:T(8,128)(2,1)}), bf16[4,48,768]{2,1,0:T(8,128)(2,1)}, u32[]{:S(2)}, u32[]{:S(2)}) async-start(bf16[4,48,768]{2,1,0:T(8,128)(2,1)} %get-tuple-element.237), calls=%async_computation.5 | async-start | bytes 589824 | tf_op jit(solution)/shard_map/all_to_all | solution.py:934
  233.3 6.8 %shard_map.321 = (f32[768,768]{1,0:T(8,128)}, f32[768,768]{1,0:T(8,128)}) custom-call(bf16[128,3072]{1,0:T(8,128)(2,1)} %get-tuple-element.215.refs_0_, bf16[128,3072]{1,0:T(8,128)(2,1)} %collective-permute-done.22.refs_1_, bf16[128,3072]{1,0:T(8,128)(2,1)} %collective-permute-done.23.refs_2_, bf16[128,3072]{1,0:T(8,128)(2,1)} %collective-permute-done.24.refs_3_, ...), custom_call_target="tpu_custom_call" | custom-call | bytes 1200000 | tf_op jit(solution)/shard_map/pallas_call | solution.py:102
  246.9 4.5 %all-to-all-start.6 = ((bf16[8,96,768]{2,1,0:T(8,128)(2,1)}), bf16[8,96,768]{2,1,0:T(8,128)(2,1)}, u32[]{:S(2)}, u32[]{:S(2)}) async-start(bf16[8,96,768]{2,1,0:T(8,128)(2,1)} %shard_map.324), calls=%async_computation.6 | async-start | bytes 2359296 | tf_op jit(solution)/shard_map/all_to_all | solution.py:934
  257.8 6.3 %shard_map.326 = (f32[192,768]{1,0:T(8,128)}, f32[192,768]{1,0:T(8,128)}, f32[192,768]{1,0:T(8,128)}, f32[192,768]{1,0:T(8,128)}, f32[192,768]{1,0:T(8,128)}) custom-call(bf16[128,1792]{1,0:T(8,128)(2,1)} %get-tuple-element.247.refs_0_, bf16[128,1792]{1,0:T(8,128)(2,1)} %collective-permute-done.19.refs_1_, ...), custom_call_target="tpu_custom_call" | custom-call | bytes 900000 | tf_op jit(solution)/shard_map/pallas_call | solution.py:102
  (112 shorter events, 106.9 us)
Async XLA Ops:
  2.6 15.9 %collective-permute-start.5 = (bf16[96,768]{1,0:T(8,128)(2,1)}, bf16[96,768]{1,0:T(8,128)(2,1)}, u32[]{:S(2)}, u32[]{:S(2)}) collective-permute-start(bf16[96,768]{1,0:T(8,128)(2,1)} %select_select_fusion), channel_id=1, source_target_pairs={{0,3},{1,2},{2,1},{3,0},{4,7},{5,6},{6,5},{7,4},{8,11},{9,10},{10,... | collective-permute-start | bytes 442376 | tf_op jit(solution)/shard_map/ppermute | solution.py:925
  7.6 12.8 %collective-permute-start.3 = (bf16[96,768]{1,0:T(8,128)(2,1)}, bf16[96,768]{1,0:T(8,128)(2,1)}, u32[]{:S(2)}, u32[]{:S(2)}) collective-permute-start(bf16[96,768]{1,0:T(8,128)(2,1)} %select_select_fusion), channel_id=1, source_target_pairs={{0,1},{1,0},{2,3},{3,2},{4,5},{5,4},{6,7},{7,6},{8,9},{9,8},{10,11... | collective-permute-start | bytes 442376 | tf_op jit(solution)/shard_map/ppermute | solution.py:925
  22.3 16.8 %collective-permute-start.8 = (bf16[288,768]{1,0:T(8,128)(2,1)}, bf16[288,768]{1,0:T(8,128)(2,1)}, u32[]{:S(2)}, u32[]{:S(2)}) collective-permute-start(bf16[288,768]{1,0:T(8,128)(2,1)} %shard_map.308.refs_4_), channel_id=1, source_target_pairs={{0,20},{4,16},{8,28},{12,24},{16,4},{20,0},{24,12},{28,8},{1,21},{... | collective-permute-start | bytes 1327112 | tf_op jit(solution)/shard_map/ppermute | solution.py:925
  24.7 19.6 %collective-permute-start.7 = (bf16[288,768]{1,0:T(8,128)(2,1)}, bf16[288,768]{1,0:T(8,128)(2,1)}, u32[]{:S(2)}, u32[]{:S(2)}) collective-permute-start(bf16[288,768]{1,0:T(8,128)(2,1)} %shard_map.308.refs_4_), channel_id=1, source_target_pairs={{0,16},{8,24},{16,0},{24,8},{1,17},{9,25},{17,1},{25,9},{2,18},{10... | collective-permute-start | bytes 1327112 | tf_op jit(solution)/shard_map/ppermute | solution.py:925
  25.2 21.1 %collective-permute-start.6 = (bf16[288,768]{1,0:T(8,128)(2,1)}, bf16[288,768]{1,0:T(8,128)(2,1)}, u32[]{:S(2)}, u32[]{:S(2)}) collective-permute-start(bf16[288,768]{1,0:T(8,128)(2,1)} %shard_map.308.refs_4_), channel_id=1, source_target_pairs={{0,4},{4,0},{1,5},{5,1},{2,6},{6,2},{3,7},{7,3},{8,12},{12,8},{9,1... | collective-permute-start | bytes 1327112 | tf_op jit(solution)/shard_map/ppermute | solution.py:925
  34.0 25.5 %all-to-all-start = ((bf16[8,32,768]{2,1,0:T(8,128)(2,1)}), bf16[8,32,768]{2,1,0:T(8,128)(2,1)}, u32[]{:S(2)}, u32[]{:S(2)}) async-start(bf16[8,32,768]{2,1,0:T(8,128)(2,1)} %get-tuple-element.149), calls=%async_computation | async-start | bytes 786432 | tf_op jit(solution)/shard_map/all_to_all | solution.py:934
  100.7 22.9 %collective-permute-start.20 = (bf16[128,1792]{1,0:T(8,128)(2,1)}, bf16[128,1792]{1,0:T(8,128)(2,1)}, u32[]{:S(2)}, u32[]{:S(2)}) collective-permute-start(bf16[128,1792]{1,0:T(8,128)(2,1)} %get-tuple-element.247.refs_0_), channel_id=1, source_target_pairs={{0,16},{8,24},{16,0},{24,8},{1,17},{9,25},{17,1},{25,9},{2,18},{10... | collective-permute-start | bytes 1376264 | tf_op jit(solution)/shard_map/ppermute | solution.py:925
  108.2 15.3 %collective-permute-start.21 = (bf16[128,1792]{1,0:T(8,128)(2,1)}, bf16[128,1792]{1,0:T(8,128)(2,1)}, u32[]{:S(2)}, u32[]{:S(2)}) collective-permute-start(bf16[128,1792]{1,0:T(8,128)(2,1)} %collective-permute-done.19.refs_1_), channel_id=1, source_target_pairs={{0,16},{8,24},{16,0},{24,8},{1,17},{9,25},{17,1},{25,9},{2,18},{10... | collective-permute-start | bytes 1376264 | tf_op jit(solution)/shard_map/ppermute | solution.py:925
  123.6 17.2 %all-to-all-start.2 = ((bf16[8,32,896]{2,1,0:T(8,128)(2,1)}), bf16[8,32,896]{2,1,0:T(8,128)(2,1)}, u32[]{:S(2)}, u32[]{:S(2)}) async-start(bf16[8,32,896]{2,1,0:T(8,128)(2,1)} %get-tuple-element.176), calls=%async_computation.2 | async-start | bytes 917504 | tf_op jit(solution)/shard_map/all_to_all | solution.py:934
  127.9 26.2 %collective-permute-start.23 = (bf16[128,3072]{1,0:T(8,128)(2,1)}, bf16[128,3072]{1,0:T(8,128)(2,1)}, u32[]{:S(2)}, u32[]{:S(2)}) collective-permute-start(bf16[128,3072]{1,0:T(8,128)(2,1)} %get-tuple-element.215.refs_0_), channel_id=1, source_target_pairs={{0,16},{8,24},{16,0},{24,8},{1,17},{9,25},{17,1},{25,9},{2,18},{10... | collective-permute-start | bytes 2359304 | tf_op jit(solution)/shard_map/ppermute | solution.py:925
  128.5 25.6 %collective-permute-start.22 = (bf16[128,3072]{1,0:T(8,128)(2,1)}, bf16[128,3072]{1,0:T(8,128)(2,1)}, u32[]{:S(2)}, u32[]{:S(2)}) collective-permute-start(bf16[128,3072]{1,0:T(8,128)(2,1)} %get-tuple-element.215.refs_0_), channel_id=1, source_target_pairs={{0,4},{4,0},{1,5},{5,1},{2,6},{6,2},{3,7},{7,3},{8,12},{12,8},{9,1... | collective-permute-start | bytes 2359304 | tf_op jit(solution)/shard_map/ppermute | solution.py:925
  154.1 17.7 %collective-permute-start.24 = (bf16[128,3072]{1,0:T(8,128)(2,1)}, bf16[128,3072]{1,0:T(8,128)(2,1)}, u32[]{:S(2)}, u32[]{:S(2)}) collective-permute-start(bf16[128,3072]{1,0:T(8,128)(2,1)} %collective-permute-done.22.refs_1_), channel_id=1, source_target_pairs={{0,16},{8,24},{16,0},{24,8},{1,17},{9,25},{17,1},{25,9},{2,18},{10... | collective-permute-start | bytes 2359304 | tf_op jit(solution)/shard_map/ppermute | solution.py:925
  154.7 14.5 %all-to-all-start.3 = ((bf16[8,32,768]{2,1,0:T(8,128)(2,1)}), bf16[8,32,768]{2,1,0:T(8,128)(2,1)}, u32[]{:S(2)}, u32[]{:S(2)}) async-start(bf16[8,32,768]{2,1,0:T(8,128)(2,1)} %get-tuple-element.177), calls=%async_computation.3 | async-start | bytes 786432 | tf_op jit(solution)/shard_map/all_to_all | solution.py:934
  171.7 47.4 %all-to-all-start.4 = ((bf16[8,224,768]{2,1,0:T(8,128)(2,1)}), bf16[8,224,768]{2,1,0:T(8,128)(2,1)}, u32[]{:S(2)}, u32[]{:S(2)}) async-start(bf16[8,224,768]{2,1,0:T(8,128)(2,1)} %shard_map.316), calls=%async_computation.4 | async-start | bytes 5505024 | tf_op jit(solution)/shard_map/all_to_all | solution.py:934
  176.2 14.1 %collective-permute-start.25 = (bf16[32,960]{1,0:T(8,128)(2,1)}, bf16[32,960]{1,0:T(8,128)(2,1)}, u32[]{:S(2)}, u32[]{:S(2)}) collective-permute-start(bf16[32,960]{1,0:T(8,128)(2,1)} %get-tuple-element.192), channel_id=1, source_target_pairs={{0,1},{1,0},{2,3},{3,2},{4,5},{5,4},{6,7},{7,6},{8,9},{9,8},{10,11... | collective-permute-start | bytes 184328 | tf_op jit(solution)/shard_map/ppermute | solution.py:925
  194.5 34.4 %collective-permute-start.34 = (bf16[128,3072]{1,0:T(8,128)(2,1)}, bf16[128,3072]{1,0:T(8,128)(2,1)}, u32[]{:S(2)}, u32[]{:S(2)}) collective-permute-start(bf16[128,3072]{1,0:T(8,128)(2,1)} %get-tuple-element.215.refs_0_), channel_id=1, source_target_pairs={{0,8},{8,0},{16,24},{24,16},{1,9},{9,1},{17,25},{25,17},{2,10},{10... | collective-permute-start | bytes 2359304 | tf_op jit(solution)/shard_map/ppermute | solution.py:925
  194.5 34.9 %collective-permute-start.35 = (bf16[128,3072]{1,0:T(8,128)(2,1)}, bf16[128,3072]{1,0:T(8,128)(2,1)}, u32[]{:S(2)}, u32[]{:S(2)}) collective-permute-start(bf16[128,3072]{1,0:T(8,128)(2,1)} %collective-permute-done.22.refs_1_), channel_id=1, source_target_pairs={{0,8},{8,0},{16,24},{24,16},{1,9},{9,1},{17,25},{25,17},{2,10},{10... | collective-permute-start | bytes 2359304 | tf_op jit(solution)/shard_map/ppermute | solution.py:925
  195.0 34.6 %collective-permute-start.36 = (bf16[128,3072]{1,0:T(8,128)(2,1)}, bf16[128,3072]{1,0:T(8,128)(2,1)}, u32[]{:S(2)}, u32[]{:S(2)}) collective-permute-start(bf16[128,3072]{1,0:T(8,128)(2,1)} %collective-permute-done.23.refs_2_), channel_id=1, source_target_pairs={{0,8},{8,0},{16,24},{24,16},{1,9},{9,1},{17,25},{25,17},{2,10},{10... | collective-permute-start | bytes 2359304 | tf_op jit(solution)/shard_map/ppermute | solution.py:925
  195.1 38.2 %collective-permute-start.37 = (bf16[128,3072]{1,0:T(8,128)(2,1)}, bf16[128,3072]{1,0:T(8,128)(2,1)}, u32[]{:S(2)}, u32[]{:S(2)}) collective-permute-start(bf16[128,3072]{1,0:T(8,128)(2,1)} %collective-permute-done.24.refs_3_), channel_id=1, source_target_pairs={{0,8},{8,0},{16,24},{24,16},{1,9},{9,1},{17,25},{25,17},{2,10},{10... | collective-permute-start | bytes 2359304 | tf_op jit(solution)/shard_map/ppermute | solution.py:925
  221.9 22.9 %all-to-all-start.5 = ((bf16[4,48,768]{2,1,0:T(8,128)(2,1)}), bf16[4,48,768]{2,1,0:T(8,128)(2,1)}, u32[]{:S(2)}, u32[]{:S(2)}) async-start(bf16[4,48,768]{2,1,0:T(8,128)(2,1)} %get-tuple-element.237), calls=%async_computation.5 | async-start | bytes 589824 | tf_op jit(solution)/shard_map/all_to_all | solution.py:934
  226.0 16.5 %collective-permute-start.40 = (bf16[128,1536]{1,0:T(8,128)(2,1)}, bf16[128,1536]{1,0:T(8,128)(2,1)}, u32[]{:S(2)}, u32[]{:S(2)}) collective-permute-start(bf16[128,1536]{1,0:T(8,128)(2,1)} %bitcast.6), channel_id=1, source_target_pairs={{0,20},{4,16},{8,28},{12,24},{16,4},{20,0},{24,12},{28,8},{1,21},{... | collective-permute-start | bytes 1179656 | tf_op jit(solution)/shard_map/ppermute | solution.py:925
  228.8 14.0 %collective-permute-start.39 = (bf16[128,1536]{1,0:T(8,128)(2,1)}, bf16[128,1536]{1,0:T(8,128)(2,1)}, u32[]{:S(2)}, u32[]{:S(2)}) collective-permute-start(bf16[128,1536]{1,0:T(8,128)(2,1)} %bitcast.7), channel_id=1, source_target_pairs={{0,16},{8,24},{16,0},{24,8},{1,17},{9,25},{17,1},{25,9},{2,18},{10... | collective-permute-start | bytes 1179656 | tf_op jit(solution)/shard_map/ppermute | solution.py:925
  229.4 13.4 %collective-permute-start.38 = (bf16[128,1536]{1,0:T(8,128)(2,1)}, bf16[128,1536]{1,0:T(8,128)(2,1)}, u32[]{:S(2)}, u32[]{:S(2)}) collective-permute-start(bf16[128,1536]{1,0:T(8,128)(2,1)} %bitcast.8), channel_id=1, source_target_pairs={{0,4},{4,0},{1,5},{5,1},{2,6},{6,2},{3,7},{7,3},{8,12},{12,8},{9,1... | collective-permute-start | bytes 1179656 | tf_op jit(solution)/shard_map/ppermute | solution.py:925
  246.9 20.2 %all-to-all-start.6 = ((bf16[8,96,768]{2,1,0:T(8,128)(2,1)}), bf16[8,96,768]{2,1,0:T(8,128)(2,1)}, u32[]{:S(2)}, u32[]{:S(2)}) async-start(bf16[8,96,768]{2,1,0:T(8,128)(2,1)} %shard_map.324), calls=%async_computation.6 | async-start | bytes 2359296 | tf_op jit(solution)/shard_map/all_to_all | solution.py:934
  (31 other events, 191.4 us)

commit v4 on v3

--- a/solution.py
+++ b/solution.py
@@ -8,9 +8,9 @@
 from jax.sharding import PartitionSpec as P
 
 CFG = dict(
-    s_o=1, s_a=1, s_xy=1, l_d=1, t_a=1, t_cost=0.05, k1=0.1, vmem=64, s_rs="bf16", m_e=1, t_shg=3, e_c=0, w_c=0,
+    s_o=1, s_a=1, s_xy=1, l_d=1, l_q=1, e_w=0, x_p=1, t_cost=0.05, k1=0.1, vmem=64, s_rs="f32", m_e=1, t_shg=3, e_c=0, w_c=0,
     t_late="perm", t_rsz="perm", t_agz="perm", t_shq=1, sh_q=0, cost=1.0, t_cs=1,
-    t_p=4, w_x=1, w_xy=1, l_p=0, l_xy=0, e_p=4, b_p=3, e_y=1,
+    t_p=0, w_x=1, w_xy=1, l_p=0, l_xy=0, e_p=4, b_p=0, e_y=1,
 )
 DHEAD = 64
 LP = 384
@@ -98,13 +98,18 @@
     return array.array if isinstance(array, Weight) else array
 
 
-def call(kernel, outs, scalars, arrays, scratch=(), micros=3.5):
+def call(kernel, outs, scalars, arrays, scratch=(), micros=3.5, steps=1):
+    def out_spec(out):
+        if steps == 1:
+            return whole(out.shape)
+        return pl.BlockSpec((out.shape[0], out.shape[1] // steps), lambda n: (0, n))
+
     return pl.pallas_call(
         kernel,
-        grid=(1,),
+        grid=(steps,),
         out_shape=tuple(outs),
         in_specs=[smem()] * len(scalars) + [spec_of(array) for array in arrays],
-        out_specs=tuple(whole(out.shape) for out in outs),
+        out_specs=tuple(out_spec(out) for out in outs),
         scratch_shapes=list(scratch),
         cost_estimate=cost(micros),
         compiler_params=pltpu.CompilerParams(
@@ -893,7 +898,7 @@
         out_ref[device, size:, :] = tail
 
 
-def collect_kernel(shares_ref, key_ref, value_ref, cross_ref, gains_ref):
+def collect_kernel(shares_ref, key_ref, value_ref, cross_ref, *gain_refs):
     plane = shares_ref.shape[0]
     size = key_ref.shape[0] // 4
     more = cross_ref.shape[0] // plane
@@ -906,9 +911,8 @@
         target[part * size : (part + 1) * size, :] = share[:size]
         cross_ref[device * more : (device + 1) * more, :] = share[size : size + more]
         total = total + share[size + more :]
-    for i, gain in enumerate(gain_sums(total)):
-        gains_ref[i : i + 1, :] = gain
-    gains_ref[3:, :] = jnp.zeros((gains_ref.shape[0] - 3, gains_ref.shape[1]), f32)
+    for gain_ref, gain in zip(gain_refs, gain_sums(total)):
+        gain_ref[...] = gain[0]
 
 
 def after(array, *others):
@@ -1144,6 +1148,10 @@
         [],
         [query_grads, first, gain_two, query_full, grad_second],
     )
+    if small and CFG["e_w"] in (4, 5):
+        given = hold([*early, *wide[:3]], enc_key_grads) if CFG["e_w"] == 4 else [*early, *wide[:3]]
+        there = across_core(given)
+        messages, there = hold_lists(messages, there)
     if CFG["w_xy"] == 1:
         messages = hold(messages, *wide)
     chunks = swap_parts(messages)
@@ -1155,6 +1163,20 @@
         elif CFG["t_shq"] == 1:
             shares = after(shares, messages[0])
         shares = exchange(shares, "dp", "blk")
+    if small and CFG["e_w"] in (4, 5):
+        early, wide = early + there[:4], wide + there[4:]
+        last = across_core(hold(wide[3:4], chunks[1] if CFG["x_p"] == 1 else messages[0]))
+        chunks, last = hold_lists(chunks, last)
+        wide = wide + last
+    if small and 1 <= CFG["e_w"] <= 3:
+        both = [*early, *wide]
+        if CFG["e_w"] == 1:
+            both = hold(both, messages[0])
+        elif CFG["e_w"] == 3:
+            both = hold(both, chunks[1])
+        there = across_core(both)
+        chunks, there = hold_lists(chunks, there)
+        early, wide = both[:4] + there[:4], both[4:] + there[4:]
     if CFG["e_p"] == 4:
         grad_enc = encoder_grads(
             *hold([enc_key_grads, enc_value_grads], messages[0]), key_full, value_full
@@ -1177,7 +1199,7 @@
         [pltpu.VMEM((rows, depth), f32), pltpu.VMEM((rows, depth + 4 * width), bf16)],
     )
     late = outs[-1]
-    if small:
+    if small and CFG["e_w"] == 0:
         if CFG["e_c"] == 0:
             early = hold(early, late)
             early = early + across_core(early)
@@ -1186,15 +1208,6 @@
         else:
             wide = hold(wide, late)
             wide = wide + across_core(wide)
-    if not small:
-        late = [late.reshape(late.shape[1:])]
-    elif CFG["t_late"] == "a2a":
-        late = [exchange(late, "dp", "blk")]
-    else:
-        late = late.reshape(late.shape[1:])
-        late = [late, partner(late, "blk", 1), partner(late, "dp", 2)]
-        if CFG["l_d"] == 1:
-            late.append(partner(late[0], ("dp", "blk"), 5))
     if CFG["t_rsz"] == "perm":
         upstream = swap_parts(outs[:head_count])
     else:
@@ -1207,6 +1220,18 @@
         (shares,) = hold([shares], *upstream)
     elif CFG["t_shg"] == 2:
         (shares,) = hold([shares], upstream[1])
+    if CFG["l_q"] < 2:
+        if CFG["l_q"] == 1:
+            late = after(late, upstream[-1])
+        if not small:
+            late = [late.reshape(late.shape[1:])]
+        elif CFG["t_late"] == "a2a":
+            late = [exchange(late, "dp", "blk")]
+        else:
+            late = late.reshape(late.shape[1:])
+            late = [late, partner(late, "blk", 1), partner(late, "dp", 2)]
+            if CFG["l_d"] == 1:
+                late.append(partner(late[0], ("dp", "blk"), 5))
     (message,) = call(
         functools.partial(input_kernel, len(upstream)),
         [shaped((head_count if CFG["t_agz"] == "a2a" else 1, 2 * piece + 16, depth), bf16)],
@@ -1217,10 +1242,32 @@
     if small and CFG["t_late"] == "perm" and CFG["l_p"] == 1:
         message, *late = hold([message, *late])
         late.append(partner(late[1], "dp", 2))
+    if CFG["l_q"] == 2:
+        late = after(late, message)
+        if not small:
+            late = [late.reshape(late.shape[1:])]
+        elif CFG["t_late"] == "a2a":
+            late = [exchange(late, "dp", "blk")]
+        else:
+            late = late.reshape(late.shape[1:])
+            late = [late, partner(late, "blk", 1), partner(late, "dp", 2)]
+            if CFG["l_d"] == 1:
+                late.append(partner(late[0], ("dp", "blk"), 5))
     if CFG["t_agz"] == "perm":
         chunks = share_heads(message.reshape(message.shape[1:]))
     else:
         chunks = [exchange(message, "head")]
+    if CFG["l_q"] == 3:
+        late = after(late, chunks[1])
+        if not small:
+            late = [late.reshape(late.shape[1:])]
+        elif CFG["t_late"] == "a2a":
+            late = [exchange(late, "dp", "blk")]
+        else:
+            late = late.reshape(late.shape[1:])
+            late = [late, partner(late, "blk", 1), partner(late, "dp", 2)]
+            if CFG["l_d"] == 1:
+                late.append(partner(late[0], ("dp", "blk"), 5))
     if CFG["t_shg"] == 3:
         shares = after(shares, chunks[1])
     elif CFG["t_shg"] == 4:
@@ -1293,9 +1340,9 @@
             [blocks, cross_share, gains],
             micros=3 * CFG["t_cost"],
         )
-        grad_c_key, grad_c_value, grad_c_out, gains = call(
+        grad_c_key, grad_c_value, grad_c_out, *gains = call(
             collect_kernel,
-            [shaped((width, depth), f32)] * 3 + [shaped((8, depth), f32)],
+            [shaped((width, depth), f32)] * 3 + [shaped((depth,), f32)] * 3,
             [],
             [exchange(shares, "dp", "blk")],
             micros=3 * CFG["t_cost"],

time: 273 us -> 259 us (0.949)
  waiting for transfers between devices: 62.1 us -> 50.2 us
    ppermute x49, waiting for transfers between devices: 48.1 us -> 39.1 us  [partner(): return lax.ppermute(array, axis, [(i, i ^ by) for i in range(size)])]
    all_to_all x6, waiting for transfers between devices: 14 us -> 11.1 us  [exchange(): return lax.all_to_all(array, axes, 0, 0)]
  transfers between devices with their start and end apart: 55 -> 55, of which waited for: 27 -> 17; matrix products, arithmetic and copies ran while one was open for 1% -> 1% of each run, Pallas kernels for 31% -> 33%
where the time goes in v4:
time: 259 us; the launch traced here: 257 us
  Pallas kernels  107 us (41%)
  starting transfers between devices  73.5 us (28%)
  waiting for transfers between devices  50.2 us (19%)
  blocking collectives  21 us (8%)
  other arithmetic  3.1 us (1%)
    pallas_call x15, Pallas kernels, call(): pl.pallas_call(kernel, grid=(steps,), out_shape=tuple(outs), in_specs=[sm...  49.3 us
    ppermute x49, starting transfers between devices, partner(): return lax.ppermute(array, axis, [(i, i ^ by) for i in range(size)])  48 us
    ppermute x49, waiting for transfers between devices, partner(): return lax.ppermute(array, axis, [(i, i ^ by) for i in range(size)])  39.1 us
    all_to_all x6, starting transfers between devices, exchange(): return lax.all_to_all(array, axes, 0, 0)  25.5 us
    all_to_all x1, blocking collectives, exchange(): return lax.all_to_all(array, axes, 0, 0)  21 us
    pallas_call x1, Pallas kernels, cross_backward(): pl.pallas_call(functools.partial(cross_backward_kernel, blk_count, head_c...  13.3 us
    all_to_all x6, waiting for transfers between devices, exchange(): return lax.all_to_all(array, axes, 0, 0)  11.1 us
    pallas_call x1, Pallas kernels, project(): pl.pallas_call(functools.partial(project_kernel, count), grid=(slots // L...  11.1 us
  transfers between devices with their start and end apart: 55, of which 17 were waited for; matrix products, arithmetic and copies ran while one was open for 1% of the time, Pallas kernels for 33%

profile of v4, /device:TPU:0, one launch (start us, length us, event | category | flops | bytes accessed | tf_op | source)
XLA Modules:
  0.0 257.3 jit_solution(3250818890498010642)
XLA Ops:
  2.6 5.0 %collective-permute-start.5 = (bf16[96,768]{1,0:T(8,128)(2,1)}, bf16[96,768]{1,0:T(8,128)(2,1)}, u32[]{:S(2)}, u32[]{:S(2)}) collective-permute-start(bf16[96,768]{1,0:T(8,128)(2,1)} %select_select_fusion), channel_id=1, source_target_pairs={{0,3},{1,2},{2,1},{3,0},{4,7},{5,6},{6,5},{7,4},{8,11},{9,10},{10,... | collective-permute-start | bytes 442376 | tf_op jit(solution)/shard_map/ppermute | solution.py:929
  8.8 3.9 %shard_map.306 = (bf16[128,768]{1,0:T(8,128)(2,1)}, bf16[128,576]{1,0:T(8,128)(2,1)}, bf16[128,192]{1,0:T(8,128)(2,1)}, f32[32,768]{1,0:T(8,128)}, f32[32,768]{1...) custom-call(bf16[128,768]{1,0:T(8,128)(2,1)} %refs_4_.7, s32[1]{0:T(128)S(6)} %copy.35.len_ref, ...), custom_call_target="tpu_custom_call" | custom-call | bytes 300000 | tf_op jit(solution)/shard_map/pallas_call | solution.py:223
  14.2 6.5 %collective-permute-done.refs_1_ = f32[32,768]{1,0:T(8,128)} collective-permute-done((f32[32,768]{1,0:T(8,128)}, f32[32,768]{1,0:T(8,128)}, u32[]{:S(2)}, u32[]{:S(2)}) %collective-permute-start) | collective-permute-done | bytes 98336 | tf_op jit(solution)/shard_map/ppermute | solution.py:929
  37.3 4.1 %all-to-all-start = ((bf16[8,32,768]{2,1,0:T(8,128)(2,1)}), bf16[8,32,768]{2,1,0:T(8,128)(2,1)}, u32[]{:S(2)}, u32[]{:S(2)}) async-start(bf16[8,32,768]{2,1,0:T(8,128)(2,1)} %get-tuple-element.138), calls=%async_computation | async-start | bytes 786432 | tf_op jit(solution)/shard_map/all_to_all | solution.py:938
  47.1 11.1 %shard_map.309 = (bf16[1920,768]{1,0:T(8,128)(2,1)}, bf16[1920,768]{1,0:T(8,128)(2,1)}, bf16[4,768,768]{2,1,0:T(8,128)(2,1)}) custom-call(bf16[1920,768]{1,0:T(8,128)(2,1)} %refs_2_.4, bf16[192,768]{1,0:T(8,128)(2,1)} %refs_0_.1, bf16[192,768]{1,0:T(8,128)(2,1)} %refs_1_.1, bf16[192,768]{1,0:T(8,128)(2,1)} %refs_2_.3, bf16[192,768]{1,0:T(8,128)(2,1)} %refs_3_.2, ...), custom_call_target="tpu_custom_call" | custom-call | bytes 27000000 | tf_op jit(solution)/shard_map/pallas_call | solution.py:305
  61.2 9.6 %shard_map.311 = bf16[8,32,896]{2,1,0:T(8,128)(2,1)} custom-call(s32[5]{0:T(128)} %dynamic-slice_xor_fusion.refs_0_, s32[5]{0:T(128)} %dynamic_slice.19.refs_1_, bf16[2,128,768]{2,1,0:T(8,128)(2,1)} %get-tuple-element.145.refs_2_, bf16[1920,768]{1,0:T(8,128)(2,1)} %get-tuple-element.146.refs_3_.refs_4_, bf16[1920,768]{1,0:T(8,128)(2,1)} %get-tuple-element.147.refs_4_.refs_5_), custom_call_target="tpu_custom_call" | custom-call | bytes 45000000 | tf_op jit(solution)/shard_map/pallas_call | solution.py:434
  70.8 21.0 %all_to_all.35.refs_0_ = bf16[8,32,896]{2,1,0:T(8,128)(2,1)} all-to-all(bf16[8,32,896]{2,1,0:T(8,128)(2,1)} %shard_map.311), channel_id=1, replica_groups=mesh['dp'=4,'blk'=2,'head'=4] {'blk','head'}, dimensions={0} | all-to-all | bytes 917504 | tf_op jit(solution)/shard_map/all_to_all | solution.py:938
  91.8 3.5 %shard_map.312 = (f32[32,768]{1,0:T(8,128)}, f32[32,768]{1,0:T(8,128)}, f32[32,128]{1,0:T(8,128)}, bf16[32,960]{1,0:T(8,128)(2,1)}, bf16[32,960]{1,0:T(8,128)(2,...) custom-call(bf16[8,32,896]{2,1,0:T(8,128)(2,1)} %all_to_all.35.refs_0_, f32[32,768]{1,0:T(8,128)} %get-tuple-element.148.refs_1_, ...), custom_call_target="tpu_custom_call" | custom-call | bytes 10500000 | tf_op jit(solution)/shard_map/pallas_call | solution.py:107
  103.9 4.0 %shard_map.313 = (bf16[32,1536]{1,0:T(8,128)(2,1)}, bf16[32,1536]{1,0:T(8,128)(2,1)}, bf16[32,1536]{1,0:T(8,128)(2,1)}, bf16[32,1536]{1,0:T(8,128)(2,1)}, bf16[1...) custom-call(bf16[32,960]{1,0:T(8,128)(2,1)} %get-tuple-element.149.refs_0_, ...), custom_call_target="tpu_custom_call" | custom-call | bytes 10500000 | tf_op jit(solution)/shard_map/pallas_call | solution.py:107
  119.6 3.6 %shard_map.314 = (f32[32,768]{1,0:T(8,128)}, f32[1,768]{1,0:T(1,128)}, bf16[32,768]{1,0:T(8,128)(2,1)}, bf16[8,32,896]{2,1,0:T(8,128)(2,1)}) custom-call(bf16[32,1536]{1,0:T(8,128)(2,1)} %get-tuple-element.153.refs_0_, bf16[32,1536]{1,0:T(8,128)(2,1)} %collective-permute-done.16.refs_1_, bf16[32,1536]{1,0:T(8,128)(2,1)} %collective-permute-done.17.refs_2_, ...), custom_call_target="tpu_custom_call" | custom-call | bytes 10500000 | tf_op jit(solution)/shard_map/pallas_call | solution.py:107
  123.2 4.3 %all-to-all-start.2 = ((bf16[8,32,896]{2,1,0:T(8,128)(2,1)}), bf16[8,32,896]{2,1,0:T(8,128)(2,1)}, u32[]{:S(2)}, u32[]{:S(2)}) async-start(bf16[8,32,896]{2,1,0:T(8,128)(2,1)} %get-tuple-element.165), calls=%async_computation.2 | async-start | bytes 917504 | tf_op jit(solution)/shard_map/all_to_all | solution.py:938
  130.2 10.2 %all-to-all-done.2.refs_6_ = bf16[8,32,896]{2,1,0:T(8,128)(2,1)} async-done(((bf16[8,32,896]{2,1,0:T(8,128)(2,1)}), bf16[8,32,896]{2,1,0:T(8,128)(2,1)}, u32[]{:S(2)}, u32[]{:S(2)}) %all-to-all-start.2) | async-done | bytes 458784 | tf_op jit(solution)/shard_map/all_to_all | solution.py:938
  140.4 13.3 %shard_map.315 = (bf16[8,32,768]{2,1,0:T(8,128)(2,1)}, bf16[128,768]{1,0:T(8,128)(2,1)}, bf16[1920,768]{1,0:T(8,128)(2,1)}, bf16[1920,768]{1,0:T(8,128)(2,1)}) custom-call(s32[5]{0:T(128)} %dynamic-slice_xor_fusion.refs_0_, s32[5]{0:T(128)} %dynamic_slice.19.refs_1_, bf16[2,128,768]{2,1,0:T(8,128)(2,1)} %get-tuple-element.145.refs_2_, ...), custom_call_target="tpu_custom_call" | custom-call | bytes 48000000 | tf_op jit(solution)/shard_map/pallas_call | solution.py:646
  154.3 4.1 %all-to-all-start.3 = ((bf16[8,32,768]{2,1,0:T(8,128)(2,1)}), bf16[8,32,768]{2,1,0:T(8,128)(2,1)}, u32[]{:S(2)}, u32[]{:S(2)}) async-start(bf16[8,32,768]{2,1,0:T(8,128)(2,1)} %get-tuple-element.166), calls=%async_computation.3 | async-start | bytes 786432 | tf_op jit(solution)/shard_map/all_to_all | solution.py:938
  158.4 10.0 %shard_map.316 = bf16[8,224,768]{2,1,0:T(8,128)(2,1)} custom-call(bf16[1920,768]{1,0:T(8,128)(2,1)} %get-tuple-element.184.refs_0_.keys_ref, bf16[1920,768]{1,0:T(8,128)(2,1)} %get-tuple-element.185.refs_1_.values_ref, bf16[1920,768]{1,0:T(8,128)(2,1)} %refs_2_.4, bf16[128,192]{1,0:T(8,128)(2,1)} %get-tuple-element.171.refs_3_, ...), custom_call_target="tpu_custom_call" | custom-call | bytes 12000000 | tf_op jit(solution)/shard_map/pallas_call | solution.py:847
  171.1 4.4 %all-to-all-start.4 = ((bf16[8,224,768]{2,1,0:T(8,128)(2,1)}), bf16[8,224,768]{2,1,0:T(8,128)(2,1)}, u32[]{:S(2)}, u32[]{:S(2)}) async-start(bf16[8,224,768]{2,1,0:T(8,128)(2,1)} %shard_map.316), calls=%async_computation.4 | async-start | bytes 5505024 | tf_op jit(solution)/shard_map/all_to_all | solution.py:938
  180.0 9.6 %shard_map.318 = f32[1920,768]{1,0:T(8,128)} custom-call(bf16[1920,768]{1,0:T(8,128)(2,1)} %get-tuple-element.184.refs_0_.keys_ref, bf16[1920,768]{1,0:T(8,128)(2,1)} %get-tuple-element.185.refs_1_.values_ref, bf16[4,768,768]{2,1,0:T(8,128)(2,1)} %get-tuple-element.142.c_query_ref.refs_2_.refs_7_.refs_3_.key_ref.value_ref, ...), custom_call_target="tpu_custom_call" | custom-call | bytes 1050000 | tf_op jit(solution)/shard_map/pallas_call | solution.py:868
  189.6 4.2 %shard_map.319 = (bf16[32,768]{1,0:T(8,128)(2,1)}, bf16[32,768]{1,0:T(8,128)(2,1)}, bf16[32,768]{1,0:T(8,128)(2,1)}, bf16[32,768]{1,0:T(8,128)(2,1)}, bf16[1,128,1536]{2,1,0:T(8,128)(2,1)}) custom-call(s32[1]{0:T(128)S(6)} %copy.35.len_ref, bf16[32,960]{1,0:T(8,128)(2,1)} %get-tuple-element.186.refs_0_, bf16[32,960]{1,0:T(8,128)(2,1)} %collective-permute-done.25.refs_1_, ...), custom_call_target="tpu_custom_call" | custom-call | bytes 10500000 | tf_op jit(solution)/shard_map/pallas_call | solution.py:107
  210.1 4.2 %collective-permute-done.33.refs_3_ = bf16[80,768]{1,0:T(8,128)(2,1)} collective-permute-done((bf16[80,768]{1,0:T(8,128)(2,1)}, bf16[80,768]{1,0:T(8,128)(2,1)}, u32[]{:S(2)}, u32[]{:S(2)}) %collective-permute-start.33) | collective-permute-done | bytes 122912 | tf_op jit(solution)/shard_map/ppermute | solution.py:929
  218.9 4.1 %all-to-all-start.5 = ((bf16[4,48,768]{2,1,0:T(8,128)(2,1)}), bf16[4,48,768]{2,1,0:T(8,128)(2,1)}, u32[]{:S(2)}, u32[]{:S(2)}) async-start(bf16[4,48,768]{2,1,0:T(8,128)(2,1)} %get-tuple-element.210), calls=%async_computation.5 | async-start | bytes 589824 | tf_op jit(solution)/shard_map/all_to_all | solution.py:938
  223.6 4.7 %collective-permute-done.35.refs_10_ = bf16[128,1536]{1,0:T(8,128)(2,1)} collective-permute-done((bf16[128,1536]{1,0:T(8,128)(2,1)}, bf16[128,1536]{1,0:T(8,128)(2,1)}, u32[]{:S(2)}, u32[]{:S(2)}) %collective-permute-start.35) | collective-permute-done | bytes 393248 | tf_op jit(solution)/shard_map/ppermute | solution.py:929
  233.8 4.5 %all-to-all-start.6 = ((bf16[8,96,768]{2,1,0:T(8,128)(2,1)}), bf16[8,96,768]{2,1,0:T(8,128)(2,1)}, u32[]{:S(2)}, u32[]{:S(2)}) async-start(bf16[8,96,768]{2,1,0:T(8,128)(2,1)} %shard_map.323), calls=%async_computation.6 | async-start | bytes 2359296 | tf_op jit(solution)/shard_map/all_to_all | solution.py:938
  241.7 6.8 %shard_map.326 = (f32[768,768]{1,0:T(8,128)}, f32[768,768]{1,0:T(8,128)}) custom-call(bf16[128,3072]{1,0:T(8,128)(2,1)} %get-tuple-element.236.refs_0_, bf16[128,3072]{1,0:T(8,128)(2,1)} %collective-permute-done.22.refs_1_, bf16[128,3072]{1,0:T(8,128)(2,1)} %collective-permute-done.23.refs_2_, bf16[128,3072]{1,0:T(8,128)(2,1)} %collective-permute-done.24.refs_3_, ...), custom_call_target="tpu_custom_call" | custom-call | bytes 1200000 | tf_op jit(solution)/shard_map/pallas_call | solution.py:107
  248.5 6.3 %shard_map.325 = (f32[192,768]{1,0:T(8,128)}, f32[192,768]{1,0:T(8,128)}, f32[192,768]{1,0:T(8,128)}, f32[192,768]{1,0:T(8,128)}, f32[192,768]{1,0:T(8,128)}) custom-call(bf16[128,1792]{1,0:T(8,128)(2,1)} %get-tuple-element.220.refs_0_, bf16[128,1792]{1,0:T(8,128)(2,1)} %collective-permute-done.19.refs_1_, ...), custom_call_target="tpu_custom_call" | custom-call | bytes 900000 | tf_op jit(solution)/shard_map/pallas_call | solution.py:107
  (111 shorter events, 92.8 us)
Async XLA Ops:
  2.6 18.1 %collective-permute-start.5 = (bf16[96,768]{1,0:T(8,128)(2,1)}, bf16[96,768]{1,0:T(8,128)(2,1)}, u32[]{:S(2)}, u32[]{:S(2)}) collective-permute-start(bf16[96,768]{1,0:T(8,128)(2,1)} %select_select_fusion), channel_id=1, source_target_pairs={{0,3},{1,2},{2,1},{3,0},{4,7},{5,6},{6,5},{7,4},{8,11},{9,10},{10,... | collective-permute-start | bytes 442376 | tf_op jit(solution)/shard_map/ppermute | solution.py:929
  7.6 13.1 %collective-permute-start.4 = (bf16[96,768]{1,0:T(8,128)(2,1)}, bf16[96,768]{1,0:T(8,128)(2,1)}, u32[]{:S(2)}, u32[]{:S(2)}) collective-permute-start(bf16[96,768]{1,0:T(8,128)(2,1)} %select_select_fusion), channel_id=1, source_target_pairs={{0,2},{1,3},{2,0},{3,1},{4,6},{5,7},{6,4},{7,5},{8,10},{9,11},{10,... | collective-permute-start | bytes 442376 | tf_op jit(solution)/shard_map/ppermute | solution.py:929
  7.6 13.1 %collective-permute-start.3 = (bf16[96,768]{1,0:T(8,128)(2,1)}, bf16[96,768]{1,0:T(8,128)(2,1)}, u32[]{:S(2)}, u32[]{:S(2)}) collective-permute-start(bf16[96,768]{1,0:T(8,128)(2,1)} %select_select_fusion), channel_id=1, source_target_pairs={{0,1},{1,0},{2,3},{3,2},{4,5},{5,4},{6,7},{7,6},{8,9},{9,8},{10,11... | collective-permute-start | bytes 442376 | tf_op jit(solution)/shard_map/ppermute | solution.py:929
  22.5 18.9 %collective-permute-start.8 = (bf16[288,768]{1,0:T(8,128)(2,1)}, bf16[288,768]{1,0:T(8,128)(2,1)}, u32[]{:S(2)}, u32[]{:S(2)}) collective-permute-start(bf16[288,768]{1,0:T(8,128)(2,1)} %shard_map.308.refs_4_), channel_id=1, source_target_pairs={{0,20},{4,16},{8,28},{12,24},{16,4},{20,0},{24,12},{28,8},{1,21},{... | collective-permute-start | bytes 1327112 | tf_op jit(solution)/shard_map/ppermute | solution.py:929
  25.1 19.2 %collective-permute-start.7 = (bf16[288,768]{1,0:T(8,128)(2,1)}, bf16[288,768]{1,0:T(8,128)(2,1)}, u32[]{:S(2)}, u32[]{:S(2)}) collective-permute-start(bf16[288,768]{1,0:T(8,128)(2,1)} %shard_map.308.refs_4_), channel_id=1, source_target_pairs={{0,16},{8,24},{16,0},{24,8},{1,17},{9,25},{17,1},{25,9},{2,18},{10... | collective-permute-start | bytes 1327112 | tf_op jit(solution)/shard_map/ppermute | solution.py:929
  25.6 18.7 %collective-permute-start.6 = (bf16[288,768]{1,0:T(8,128)(2,1)}, bf16[288,768]{1,0:T(8,128)(2,1)}, u32[]{:S(2)}, u32[]{:S(2)}) collective-permute-start(bf16[288,768]{1,0:T(8,128)(2,1)} %shard_map.308.refs_4_), channel_id=1, source_target_pairs={{0,4},{4,0},{1,5},{5,1},{2,6},{6,2},{3,7},{7,3},{8,12},{12,8},{9,1... | collective-permute-start | bytes 1327112 | tf_op jit(solution)/shard_map/ppermute | solution.py:929
  37.3 20.9 %all-to-all-start = ((bf16[8,32,768]{2,1,0:T(8,128)(2,1)}), bf16[8,32,768]{2,1,0:T(8,128)(2,1)}, u32[]{:S(2)}, u32[]{:S(2)}) async-start(bf16[8,32,768]{2,1,0:T(8,128)(2,1)} %get-tuple-element.138), calls=%async_computation | async-start | bytes 786432 | tf_op jit(solution)/shard_map/all_to_all | solution.py:938
  100.3 22.9 %collective-permute-start.20 = (bf16[128,1792]{1,0:T(8,128)(2,1)}, bf16[128,1792]{1,0:T(8,128)(2,1)}, u32[]{:S(2)}, u32[]{:S(2)}) collective-permute-start(bf16[128,1792]{1,0:T(8,128)(2,1)} %get-tuple-element.220.refs_0_), channel_id=1, source_target_pairs={{0,16},{8,24},{16,0},{24,8},{1,17},{9,25},{17,1},{25,9},{2,18},{10... | collective-permute-start | bytes 1376264 | tf_op jit(solution)/shard_map/ppermute | solution.py:929
  107.9 15.3 %collective-permute-start.21 = (bf16[128,1792]{1,0:T(8,128)(2,1)}, bf16[128,1792]{1,0:T(8,128)(2,1)}, u32[]{:S(2)}, u32[]{:S(2)}) collective-permute-start(bf16[128,1792]{1,0:T(8,128)(2,1)} %collective-permute-done.19.refs_1_), channel_id=1, source_target_pairs={{0,16},{8,24},{16,0},{24,8},{1,17},{9,25},{17,1},{25,9},{2,18},{10... | collective-permute-start | bytes 1376264 | tf_op jit(solution)/shard_map/ppermute | solution.py:929
  123.2 17.2 %all-to-all-start.2 = ((bf16[8,32,896]{2,1,0:T(8,128)(2,1)}), bf16[8,32,896]{2,1,0:T(8,128)(2,1)}, u32[]{:S(2)}, u32[]{:S(2)}) async-start(bf16[8,32,896]{2,1,0:T(8,128)(2,1)} %get-tuple-element.165), calls=%async_computation.2 | async-start | bytes 917504 | tf_op jit(solution)/shard_map/all_to_all | solution.py:938
  127.5 26.1 %collective-permute-start.23 = (bf16[128,3072]{1,0:T(8,128)(2,1)}, bf16[128,3072]{1,0:T(8,128)(2,1)}, u32[]{:S(2)}, u32[]{:S(2)}) collective-permute-start(bf16[128,3072]{1,0:T(8,128)(2,1)} %get-tuple-element.236.refs_0_), channel_id=1, source_target_pairs={{0,16},{8,24},{16,0},{24,8},{1,17},{9,25},{17,1},{25,9},{2,18},{10... | collective-permute-start | bytes 2359304 | tf_op jit(solution)/shard_map/ppermute | solution.py:929
  128.5 25.2 %collective-permute-start.22 = (bf16[128,3072]{1,0:T(8,128)(2,1)}, bf16[128,3072]{1,0:T(8,128)(2,1)}, u32[]{:S(2)}, u32[]{:S(2)}) collective-permute-start(bf16[128,3072]{1,0:T(8,128)(2,1)} %get-tuple-element.236.refs_0_), channel_id=1, source_target_pairs={{0,4},{4,0},{1,5},{5,1},{2,6},{6,2},{3,7},{7,3},{8,12},{12,8},{9,1... | collective-permute-start | bytes 2359304 | tf_op jit(solution)/shard_map/ppermute | solution.py:929
  153.7 17.4 %collective-permute-start.24 = (bf16[128,3072]{1,0:T(8,128)(2,1)}, bf16[128,3072]{1,0:T(8,128)(2,1)}, u32[]{:S(2)}, u32[]{:S(2)}) collective-permute-start(bf16[128,3072]{1,0:T(8,128)(2,1)} %collective-permute-done.22.refs_1_), channel_id=1, source_target_pairs={{0,16},{8,24},{16,0},{24,8},{1,17},{9,25},{17,1},{25,9},{2,18},{10... | collective-permute-start | bytes 2359304 | tf_op jit(solution)/shard_map/ppermute | solution.py:929
  154.3 14.3 %all-to-all-start.3 = ((bf16[8,32,768]{2,1,0:T(8,128)(2,1)}), bf16[8,32,768]{2,1,0:T(8,128)(2,1)}, u32[]{:S(2)}, u32[]{:S(2)}) async-start(bf16[8,32,768]{2,1,0:T(8,128)(2,1)} %get-tuple-element.166), calls=%async_computation.3 | async-start | bytes 786432 | tf_op jit(solution)/shard_map/all_to_all | solution.py:938
  171.1 45.0 %all-to-all-start.4 = ((bf16[8,224,768]{2,1,0:T(8,128)(2,1)}), bf16[8,224,768]{2,1,0:T(8,128)(2,1)}, u32[]{:S(2)}, u32[]{:S(2)}) async-start(bf16[8,224,768]{2,1,0:T(8,128)(2,1)} %shard_map.316), calls=%async_computation.4 | async-start | bytes 5505024 | tf_op jit(solution)/shard_map/all_to_all | solution.py:938
  175.5 14.1 %collective-permute-start.25 = (bf16[32,960]{1,0:T(8,128)(2,1)}, bf16[32,960]{1,0:T(8,128)(2,1)}, u32[]{:S(2)}, u32[]{:S(2)}) collective-permute-start(bf16[32,960]{1,0:T(8,128)(2,1)} %get-tuple-element.181), channel_id=1, source_target_pairs={{0,1},{1,0},{2,3},{3,2},{4,5},{5,4},{6,7},{7,6},{8,9},{9,8},{10,11... | collective-permute-start | bytes 184328 | tf_op jit(solution)/shard_map/ppermute | solution.py:929
  206.8 22.1 %collective-permute-start.37 = (bf16[128,1792]{1,0:T(8,128)(2,1)}, bf16[128,1792]{1,0:T(8,128)(2,1)}, u32[]{:S(2)}, u32[]{:S(2)}) collective-permute-start(bf16[128,1792]{1,0:T(8,128)(2,1)} %get-tuple-element.220.refs_0_), channel_id=1, source_target_pairs={{0,8},{8,0},{16,24},{24,16},{1,9},{9,1},{17,25},{25,17},{2,10},{10... | collective-permute-start | bytes 1376264 | tf_op jit(solution)/shard_map/ppermute | solution.py:929
  206.8 16.4 %collective-permute-start.36 = (bf16[128,1536]{1,0:T(8,128)(2,1)}, bf16[128,1536]{1,0:T(8,128)(2,1)}, u32[]{:S(2)}, u32[]{:S(2)}) collective-permute-start(bf16[128,1536]{1,0:T(8,128)(2,1)} %bitcast.6), channel_id=1, source_target_pairs={{0,20},{4,16},{8,28},{12,24},{16,4},{20,0},{24,12},{28,8},{1,21},{... | collective-permute-start | bytes 1179656 | tf_op jit(solution)/shard_map/ppermute | solution.py:929
  209.5 18.8 %collective-permute-start.35 = (bf16[128,1536]{1,0:T(8,128)(2,1)}, bf16[128,1536]{1,0:T(8,128)(2,1)}, u32[]{:S(2)}, u32[]{:S(2)}) collective-permute-start(bf16[128,1536]{1,0:T(8,128)(2,1)} %bitcast.7), channel_id=1, source_target_pairs={{0,16},{8,24},{16,0},{24,8},{1,17},{9,25},{17,1},{25,9},{2,18},{10... | collective-permute-start | bytes 1179656 | tf_op jit(solution)/shard_map/ppermute | solution.py:929
  214.3 14.1 %collective-permute-start.34 = (bf16[128,1536]{1,0:T(8,128)(2,1)}, bf16[128,1536]{1,0:T(8,128)(2,1)}, u32[]{:S(2)}, u32[]{:S(2)}) collective-permute-start(bf16[128,1536]{1,0:T(8,128)(2,1)} %bitcast.8), channel_id=1, source_target_pairs={{0,4},{4,0},{1,5},{5,1},{2,6},{6,2},{3,7},{7,3},{8,12},{12,8},{9,1... | collective-permute-start | bytes 1179656 | tf_op jit(solution)/shard_map/ppermute | solution.py:929
  223.1 15.2 %collective-permute-start.38 = (bf16[128,1792]{1,0:T(8,128)(2,1)}, bf16[128,1792]{1,0:T(8,128)(2,1)}, u32[]{:S(2)}, u32[]{:S(2)}) collective-permute-start(bf16[128,1792]{1,0:T(8,128)(2,1)} %collective-permute-done.19.refs_1_), channel_id=1, source_target_pairs={{0,8},{8,0},{16,24},{24,16},{1,9},{9,1},{17,25},{25,17},{2,10},{10... | collective-permute-start | bytes 1376264 | tf_op jit(solution)/shard_map/ppermute | solution.py:929
  223.1 17.5 %collective-permute-start.45 = (bf16[128,3072]{1,0:T(8,128)(2,1)}, bf16[128,3072]{1,0:T(8,128)(2,1)}, u32[]{:S(2)}, u32[]{:S(2)}) collective-permute-start(bf16[128,3072]{1,0:T(8,128)(2,1)} %get-tuple-element.236.refs_0_), channel_id=1, source_target_pairs={{0,8},{8,0},{16,24},{24,16},{1,9},{9,1},{17,25},{25,17},{2,10},{10... | collective-permute-start | bytes 2359304 | tf_op jit(solution)/shard_map/ppermute | solution.py:929
  228.3 12.8 %collective-permute-start.47 = (bf16[128,3072]{1,0:T(8,128)(2,1)}, bf16[128,3072]{1,0:T(8,128)(2,1)}, u32[]{:S(2)}, u32[]{:S(2)}) collective-permute-start(bf16[128,3072]{1,0:T(8,128)(2,1)} %collective-permute-done.23.refs_2_), channel_id=1, source_target_pairs={{0,8},{8,0},{16,24},{24,16},{1,9},{9,1},{17,25},{25,17},{2,10},{10... | collective-permute-start | bytes 2359304 | tf_op jit(solution)/shard_map/ppermute | solution.py:929
  233.8 21.0 %all-to-all-start.6 = ((bf16[8,96,768]{2,1,0:T(8,128)(2,1)}), bf16[8,96,768]{2,1,0:T(8,128)(2,1)}, u32[]{:S(2)}, u32[]{:S(2)}) async-start(bf16[8,96,768]{2,1,0:T(8,128)(2,1)} %shard_map.323), calls=%async_computation.6 | async-start | bytes 2359296 | tf_op jit(solution)/shard_map/all_to_all | solution.py:938
  (31 other events, 232.1 us)
